TPU v7x, 32 devices: a whole 2x2x4 slice. The times are simulated.
32 devices in a mesh: grp: 4 (over x, core), blk: 4 (over z), head: 2 (over y).
Axes of the slice: x: 2, y: 2, z: 4, core: 2. Of those that a mesh axis runs over, the one named last changes fastest.
Arguments:
- prompt: bfloat16 [4096, 1024], P(('grp', 'blk', 'head')), parts along dimension 0, may hold values from -6 to 6
- continued: bfloat16 [8192, 1024], P(('grp', 'blk', 'head')), parts along dimension 0, may hold values from -6 to 6
- encoded: bfloat16 [2048, 1024], P(('grp', 'blk', 'head')), parts along dimension 0, may hold values from -6 to 6
- cont_lengths: int32 [8], P('grp'), parts along dimension 0, may hold values from 1 to 1536, 2048 in all
- self_gain: bfloat16 [1024], P(('blk', 'head')), may hold values from 0.099609375 to 1.8984375
- self_shift: bfloat16 [1024], P(('blk', 'head')), may hold values from -1.75 to 1.75
- query_weight: bfloat16 [1024, 1024], P(('blk', 'head')), may hold values from -0.1875 to 0.1875
- query_bias: bfloat16 [1024], P(('blk', 'head')), may hold values from -1.75 to 1.75
- key_weight: bfloat16 [1024, 1024], P(('blk', 'head')), may hold values from -0.1875 to 0.1875
- value_weight: bfloat16 [1024, 1024], P(('blk', 'head')), may hold values from -0.1875 to 0.1875
- value_bias: bfloat16 [1024], P(('blk', 'head')), may hold values from -1.75 to 1.75
- output_weight: bfloat16 [1024, 1024], P(('blk', 'head')), may hold values from -1.5 to 1.5
- output_bias: bfloat16 [1024], P(('blk', 'head')), may hold values from -3 to 3
- cross_gain: bfloat16 [1024], P(('blk', 'head')), may hold values from 0.099609375 to 1.8984375
- cross_shift: bfloat16 [1024], P(('blk', 'head')), may hold values from -1.75 to 1.75
- probe_weight: bfloat16 [1024, 1024], P(('blk', 'head')), may hold values from -0.1875 to 0.1875
- probe_bias: bfloat16 [1024], P(('blk', 'head')), may hold values from -1.75 to 1.75
- lookup_weight: bfloat16 [1024, 1024], P(('blk', 'head')), may hold values from -0.1875 to 0.1875
- content_weight: bfloat16 [1024, 1024], P(('blk', 'head')), may hold values from -0.1875 to 0.1875
- content_bias: bfloat16 [1024], P(('blk', 'head')), may hold values from -1.75 to 1.75
- merged_weight: bfloat16 [1024, 1024], P(('blk', 'head')), may hold values from -1.5 to 1.5
- merged_bias: bfloat16 [1024], P(('blk', 'head')), may hold values from -3 to 3
- feed_gain: bfloat16 [1024], P(('blk', 'head')), may hold values from 0.099609375 to 1.8984375
- feed_shift: bfloat16 [1024], P(('blk', 'head')), may hold values from -1.75 to 1.75
- up_weight: bfloat16 [1024, 8192], P(('blk', 'head')), may hold values from -0.1875 to 0.1875
- up_bias: bfloat16 [8192], P(('blk', 'head')), may hold values from -1.75 to 1.75
- down_weight: bfloat16 [8192, 1024], P(('blk', 'head')), may hold values from -0.0625 to 0.0625
- down_bias: bfloat16 [1024], P(('blk', 'head')), may hold values from -3 to 3
- cot_prompt: bfloat16 [4096, 1024], P(('grp', 'blk', 'head')), parts along dimension 0, may hold values from -6 to 6
- cot_cont: bfloat16 [8192, 1024], P(('grp', 'blk', 'head')), parts along dimension 0, may hold values from -6 to 6
Outputs:
- out_prompt: bfloat16 [4096, 1024], P(('grp', 'blk', 'head')), parts along dimension 0
- out_cont: bfloat16 [8192, 1024], P(('grp', 'blk', 'head')), parts along dimension 0
- prompt_gradient: float32 [4096, 1024], P(('grp', 'blk', 'head')), parts along dimension 0
- cont_gradient: float32 [8192, 1024], P(('grp', 'blk', 'head')), parts along dimension 0
- encoded_gradient: float32 [2048, 1024], P(('grp', 'blk', 'head')), parts along dimension 0
- self_gain_gradient: float32 [4096], P(('grp', 'blk', 'head')), parts along dimension 0
- self_shift_gradient: float32 [4096], P(('grp', 'blk', 'head')), parts along dimension 0
- query_weight_gradient: float32 [4096, 1024], P(('grp', 'blk', 'head')), parts along dimension 0
- query_bias_gradient: float32 [4096], P(('grp', 'blk', 'head')), parts along dimension 0
- key_weight_gradient: float32 [4096, 1024], P(('grp', 'blk', 'head')), parts along dimension 0
- value_weight_gradient: float32 [4096, 1024], P(('grp', 'blk', 'head')), parts along dimension 0
- value_bias_gradient: float32 [4096], P(('grp', 'blk', 'head')), parts along dimension 0
- output_weight_gradient: float32 [4096, 1024], P(('grp', 'blk', 'head')), parts along dimension 0
- output_bias_gradient: float32 [4096], P(('grp', 'blk', 'head')), parts along dimension 0
- cross_gain_gradient: float32 [4096], P(('grp', 'blk', 'head')), parts along dimension 0
- cross_shift_gradient: float32 [4096], P(('grp', 'blk', 'head')), parts along dimension 0
- probe_weight_gradient: float32 [4096, 1024], P(('grp', 'blk', 'head')), parts along dimension 0
- probe_bias_gradient: float32 [4096], P(('grp', 'blk', 'head')), parts along dimension 0
- lookup_weight_gradient: float32 [4096, 1024], P(('grp', 'blk', 'head')), parts along dimension 0
- content_weight_gradient: float32 [4096, 1024], P(('grp', 'blk', 'head')), parts along dimension 0
- content_bias_gradient: float32 [4096], P(('grp', 'blk', 'head')), parts along dimension 0
- merged_weight_gradient: float32 [4096, 1024], P(('grp', 'blk', 'head')), parts along dimension 0
- merged_bias_gradient: float32 [4096], P(('grp', 'blk', 'head')), parts along dimension 0
- feed_gain_gradient: float32 [4096], P(('grp', 'blk', 'head')), parts along dimension 0
- feed_shift_gradient: float32 [4096], P(('grp', 'blk', 'head')), parts along dimension 0
- up_weight_gradient: float32 [4096, 8192], P(('grp', 'blk', 'head')), parts along dimension 0
- up_bias_gradient: float32 [32768], P(('grp', 'blk', 'head')), parts along dimension 0
- down_weight_gradient: float32 [32768, 1024], P(('grp', 'blk', 'head')), parts along dimension 0
- down_bias_gradient: float32 [4096], P(('grp', 'blk', 'head')), parts along dimension 0
There are 4 independent parts, one for each index of `grp`. A program takes and returns all parts, laid end to end along the dimension named above; an argument that names none is the same for every part. Nothing has to cross between parts.
Inputs may be any that keep to these rules, and one draw needn't show every extreme that they name: `cont_lengths`: 2 continuation lengths that sum to 2048; neither is longer than 1536.
All inputs are finite; a program needn't handle non-finite values.
Results may differ from a plain program's by a relative error of at most 0.038.
Values may be sent and summed in bfloat16 or wider, within the bound.
No kernel may reach another device: no remote copies, remote signals or barrier semaphores. Data moves between devices by JAX's collectives and lax.ppermute only.
A program may use at most 448 MiB of HBM per device.

v0:
```python
import functools
import math
import types

import jax
import jax.numpy as jnp
from jax import lax
from jax.experimental import pallas as pl
from jax.experimental.pallas import tpu as pltpu
from jax.sharding import PartitionSpec as P

HEADS = 16
HD = 64


floor_value = -1e30
BLK = "blk"
HEAD = "head"
GRP = "grp"
ROW_AXES = (BLK, HEAD)
ROLE_AXES = (GRP, HEAD)
ALL_AXES = (GRP, BLK, HEAD)
PARAM_NAMES = (
    "self_gain",
    "self_shift",
    "query_weight",
    "query_bias",
    "key_weight",
    "value_weight",
    "value_bias",
    "output_weight",
    "output_bias",
    "cross_gain",
    "cross_shift",
    "probe_weight",
    "probe_bias",
    "lookup_weight",
    "content_weight",
    "content_bias",
    "merged_weight",
    "merged_bias",
    "feed_gain",
    "feed_shift",
    "up_weight",
    "up_bias",
    "down_weight",
    "down_bias",
)


def layer_norm(rows, gain, shift):
    center = jnp.mean(rows, axis=-1, keepdims=True)
    centred = rows - center
    spread = jnp.mean(centred * centred, axis=-1, keepdims=True)
    return centred * lax.rsqrt(spread + 1e-05) * gain + shift


def matmul(left, right):
    return jnp.dot(left, right, preferred_element_type=jnp.float32)


def left_product(left, right):
    return jnp.einsum("rd,re->de", left, right, preferred_element_type=jnp.float32)


def right_product(left, right):
    return jnp.einsum("re,de->rd", left, right, preferred_element_type=jnp.float32)


def column_sum(values):
    return jnp.sum(values.astype(jnp.float32), axis=0)


def exact_gelu(values):
    return jax.nn.gelu(values, approximate=False)


def row_meta(global_rows, bounds, prompt_rows, cont_rows, heads_here):
    local_rows = prompt_rows + cont_rows
    span = heads_here * local_rows
    owner = global_rows // span
    inner = global_rows % span
    device = owner * heads_here + inner // local_rows
    offset = inner % local_rows
    in_prompt = offset < prompt_rows
    places = jnp.where(
        in_prompt, device * prompt_rows + offset, device * cont_rows + offset - prompt_rows
    )
    later = jnp.sum((places[:, None] >= bounds[None, :]).astype(jnp.int32), axis=1)
    segment = jnp.where(in_prompt, 0, 1 + later)
    return (segment, places)


def allowed_pairs(query_seg, query_place, key_seg, key_place):
    from_prompt = (key_seg[None, :] == 0) & (query_seg[:, None] > 0)
    causal = (key_seg[None, :] == query_seg[:, None]) & (key_place[None, :] <= query_place[:, None])
    return from_prompt | causal


def token_body(
    prompt,
    continued,
    encoded,
    cont_lengths,
    self_gain,
    self_shift,
    query_weight,
    query_bias,
    key_weight,
    value_weight,
    value_bias,
    output_weight,
    output_bias,
    cross_gain,
    cross_shift,
    probe_weight,
    probe_bias,
    lookup_weight,
    content_weight,
    content_bias,
    merged_weight,
    merged_bias,
    feed_gain,
    feed_shift,
    up_weight,
    up_bias,
    down_weight,
    down_bias,
    cot_prompt,
    cot_cont,
):
    gathered = (
        lax.all_gather(self_gain, ROW_AXES, axis=0, tiled=True),
        lax.all_gather(self_shift, ROW_AXES, axis=0, tiled=True),
        lax.all_gather(query_weight, ROW_AXES, axis=0, tiled=True),
        lax.all_gather(query_bias, ROW_AXES, axis=0, tiled=True),
        lax.all_gather(key_weight, ROW_AXES, axis=0, tiled=True),
        lax.all_gather(value_weight, ROW_AXES, axis=0, tiled=True),
        lax.all_gather(value_bias, ROW_AXES, axis=0, tiled=True),
        lax.all_gather(output_weight, ROW_AXES, axis=0, tiled=True),
        lax.all_gather(output_bias, ROW_AXES, axis=0, tiled=True),
        lax.all_gather(cross_gain, ROW_AXES, axis=0, tiled=True),
        lax.all_gather(cross_shift, ROW_AXES, axis=0, tiled=True),
        lax.all_gather(probe_weight, ROW_AXES, axis=0, tiled=True),
        lax.all_gather(probe_bias, ROW_AXES, axis=0, tiled=True),
        lax.all_gather(lookup_weight, ROW_AXES, axis=0, tiled=True),
        lax.all_gather(content_weight, ROW_AXES, axis=0, tiled=True),
        lax.all_gather(content_bias, ROW_AXES, axis=0, tiled=True),
        lax.all_gather(merged_weight, ROW_AXES, axis=0, tiled=True),
        lax.all_gather(merged_bias, ROW_AXES, axis=0, tiled=True),
        lax.all_gather(feed_gain, ROW_AXES, axis=0, tiled=True),
        lax.all_gather(feed_shift, ROW_AXES, axis=0, tiled=True),
        lax.all_gather(up_weight, ROW_AXES, axis=0, tiled=True),
        lax.all_gather(up_bias, ROW_AXES, axis=0, tiled=True),
        lax.all_gather(down_weight, ROW_AXES, axis=0, tiled=True),
        lax.all_gather(down_bias, ROW_AXES, axis=0, tiled=True),
    )
    full = types.SimpleNamespace(**dict(zip(PARAM_NAMES, gathered)))
    heads_here = lax.axis_size(HEAD)
    prompt_rows = prompt.shape[0]
    cont_rows = continued.shape[0]
    local_rows = prompt_rows + cont_rows
    span = heads_here * local_rows
    width = prompt.shape[1]
    local_heads = HEADS // heads_here
    half = local_heads * HD
    scale = HD ** (-0.5)
    bounds = jnp.cumsum(cont_lengths)
    rows = jnp.concatenate([prompt, continued], axis=0).astype(jnp.float32)
    self_gain_full = full.self_gain.astype(jnp.float32)
    self_shift_full = full.self_shift.astype(jnp.float32)
    cross_gain_full = full.cross_gain.astype(jnp.float32)
    cross_shift_full = full.cross_shift.astype(jnp.float32)
    feed_gain_full = full.feed_gain.astype(jnp.float32)
    feed_shift_full = full.feed_shift.astype(jnp.float32)
    normed = layer_norm(rows, self_gain_full, self_shift_full).astype(jnp.bfloat16)
    queries = (matmul(normed, full.query_weight) + full.query_bias).astype(jnp.bfloat16)
    keys_rows = matmul(normed, full.key_weight).astype(jnp.bfloat16)
    values_rows = (matmul(normed, full.value_weight) + full.value_bias).astype(jnp.bfloat16)
    head_queries, head_keys, head_values = (
        lax.all_to_all(queries, HEAD, split_axis=1, concat_axis=0, tiled=True),
        lax.all_to_all(keys_rows, HEAD, split_axis=1, concat_axis=0, tiled=True),
        lax.all_to_all(values_rows, HEAD, split_axis=1, concat_axis=0, tiled=True),
    )
    query_block = math.gcd(span, 512)
    query_count = span // query_block
    own_rows = lax.axis_index(BLK) * span + jnp.arange(span, dtype=jnp.int32)
    own_seg, own_place = row_meta(own_rows, bounds, prompt_rows, cont_rows, heads_here)
    query_tiles = head_queries.reshape(query_count, query_block, local_heads, HD)
    seg_tiles = own_seg.reshape(query_count, query_block)
    place_tiles = own_place.reshape(query_count, query_block)

    def key_tiles(piece_keys, piece_values):
        count = piece_keys.shape[0]
        key_block = math.gcd(count, span)
        key_count = count // key_block
        key_rows = jnp.arange(count, dtype=jnp.int32)
        key_seg, key_place = row_meta(key_rows, bounds, prompt_rows, cont_rows, heads_here)
        return (
            piece_keys.reshape(key_count, key_block, local_heads, HD),
            piece_values.reshape(key_count, key_block, local_heads, HD),
            key_seg.reshape(key_count, key_block),
            key_place.reshape(key_count, key_block),
        )

    def scores_of(query_tile, query_seg, query_place, key_tile, key_seg, key_place):
        raw = (
            jnp.einsum("qhd,khd->qhk", query_tile, key_tile, preferred_element_type=jnp.float32)
            * scale
        )
        allowed = allowed_pairs(query_seg, query_place, key_seg, key_place)[:, None, :]
        return (jnp.where(allowed, raw, floor_value), allowed)

    start_top = jnp.full((query_count, query_block, local_heads), floor_value, jnp.float32)
    start_total = jnp.zeros((query_count, query_block, local_heads), jnp.float32)
    start_sum = jnp.zeros((query_count, query_block, local_heads, HD), jnp.float32)
    piece = (
        lax.all_gather(head_keys, BLK, axis=0, tiled=True),
        lax.all_gather(head_values, BLK, axis=0, tiled=True),
    )
    tiles = key_tiles(piece[0], piece[1])

    def fold_per_query(args):
        query_tile, query_seg, query_place, running_top, running_total, running_sum = args

        def fold_per_key(state, key_args):
            key_tile, value_tile, key_seg, key_place = key_args
            top_old, total_old, sum_old = state
            scores, allowed = scores_of(
                query_tile, query_seg, query_place, key_tile, key_seg, key_place
            )
            top_new = jnp.maximum(top_old, jnp.max(scores, axis=-1))
            weights = jnp.where(allowed, jnp.exp(scores - top_new[..., None]), 0.0)
            fade = jnp.exp(top_old - top_new)
            total_new = total_old * fade + jnp.sum(weights, axis=-1)
            sum_new = sum_old * fade[..., None] + jnp.einsum(
                "qhk,khd->qhd",
                weights.astype(jnp.bfloat16),
                value_tile,
                preferred_element_type=jnp.float32,
            )
            return ((top_new, total_new, sum_new), None)

        state, unused = lax.scan(fold_per_key, (running_top, running_total, running_sum), tiles)
        return state

    top, total, summed = lax.map(
        fold_per_query, (query_tiles, seg_tiles, place_tiles, start_top, start_total, start_sum)
    )
    attended = summed / total[..., None]
    logsum = top + jnp.log(total)
    attended_low = attended.reshape(span, half).astype(jnp.bfloat16)
    mixed = lax.all_to_all(attended_low, HEAD, split_axis=0, concat_axis=1, tiled=True)
    first = rows + matmul(mixed, full.output_weight) + full.output_bias
    normed_cross = layer_norm(first, cross_gain_full, cross_shift_full).astype(jnp.bfloat16)
    probes = (matmul(normed_cross, full.probe_weight) + full.probe_bias).astype(jnp.bfloat16)
    lookups_own = matmul(encoded, full.lookup_weight).astype(jnp.bfloat16)
    contents_own = (matmul(encoded, full.content_weight) + full.content_bias).astype(
        jnp.bfloat16
    )
    lookups, contents = (
        lax.all_gather(lookups_own, ROW_AXES, axis=0, tiled=True),
        lax.all_gather(contents_own, ROW_AXES, axis=0, tiled=True),
    )
    memory_rows = lookups.shape[0]
    memory_keys = lookups.reshape(memory_rows, HEADS, HD)
    memory_values = contents.reshape(memory_rows, HEADS, HD)
    cross_block = math.gcd(local_rows, 256)
    cross_count = local_rows // cross_block
    probe_tiles = probes.reshape(cross_count, cross_block, HEADS, HD)

    def cross_scores(probe_tile):
        return (
            jnp.einsum("qhd,khd->qhk", probe_tile, memory_keys, preferred_element_type=jnp.float32)
            * scale
        )

    def cross_forward(probe_tile):
        scores = cross_scores(probe_tile)
        peak = jnp.max(scores, axis=-1, keepdims=True)
        weights = jnp.exp(scores - peak)
        weight_sum = jnp.sum(weights, axis=-1, keepdims=True)
        probs = (weights / weight_sum).astype(jnp.bfloat16)
        recalled_tile = jnp.einsum(
            "qhk,khd->qhd", probs, memory_values, preferred_element_type=jnp.float32
        )
        return (recalled_tile, (peak + jnp.log(weight_sum))[..., 0])

    recalled, cross_logsum = lax.map(cross_forward, probe_tiles)
    recalled_low = recalled.reshape(local_rows, width).astype(jnp.bfloat16)
    second = first + matmul(recalled_low, full.merged_weight) + full.merged_bias
    normed_feed = layer_norm(second, feed_gain_full, feed_shift_full).astype(jnp.bfloat16)
    hidden = matmul(normed_feed, full.up_weight) + full.up_bias
    active = exact_gelu(hidden).astype(jnp.bfloat16)
    output = second + matmul(active, full.down_weight) + full.down_bias
    output_low = output.astype(jnp.bfloat16)
    grads = types.SimpleNamespace()
    upstream = jnp.concatenate([cot_prompt, cot_cont], axis=0)
    grads.down_weight = left_product(active, upstream)
    grads.down_bias = column_sum(upstream)
    dactive = right_product(upstream, full.down_weight)
    unused, gelu_pull = jax.vjp(exact_gelu, hidden)
    dhidden = gelu_pull(dactive)[0].astype(jnp.bfloat16)
    grads.up_weight = left_product(normed_feed, dhidden)
    grads.up_bias = column_sum(dhidden)
    dnormed_feed = right_product(dhidden, full.up_weight)
    unused, feed_pull = jax.vjp(layer_norm, second, feed_gain_full, feed_shift_full)
    dsecond_part, grads.feed_gain, grads.feed_shift = feed_pull(dnormed_feed)
    dsecond = upstream.astype(jnp.float32) + dsecond_part
    dsecond_low = dsecond.astype(jnp.bfloat16)
    grads.merged_weight = left_product(recalled_low, dsecond_low)
    grads.merged_bias = column_sum(dsecond_low)
    drecalled = right_product(dsecond_low, full.merged_weight).astype(jnp.bfloat16)
    drecalled_tiles = drecalled.reshape(cross_count, cross_block, HEADS, HD)
    cross_delta = jnp.sum(drecalled_tiles.astype(jnp.float32) * recalled, axis=-1)

    def cross_backward(state, args):
        probe_tile, drecalled_tile, logsum_tile, delta_tile = args
        dlookups_acc, dcontents_acc = state
        scores = cross_scores(probe_tile)
        probs = jnp.exp(scores - logsum_tile[..., None])
        dprobs = jnp.einsum(
            "qhd,khd->qhk", drecalled_tile, memory_values, preferred_element_type=jnp.float32
        )
        dscores = (probs * (dprobs - delta_tile[..., None])).astype(jnp.bfloat16)
        dprobe_tile = (
            jnp.einsum("qhk,khd->qhd", dscores, memory_keys, preferred_element_type=jnp.float32)
            * scale
        )
        dlookups_acc = (
            dlookups_acc
            + jnp.einsum("qhk,qhd->khd", dscores, probe_tile, preferred_element_type=jnp.float32)
            * scale
        )
        dcontents_acc = dcontents_acc + jnp.einsum(
            "qhk,qhd->khd",
            probs.astype(jnp.bfloat16),
            drecalled_tile,
            preferred_element_type=jnp.float32,
        )
        return ((dlookups_acc, dcontents_acc), dprobe_tile)

    zero_memory = jnp.zeros((memory_rows, HEADS, HD), jnp.float32)
    (dlookups, dcontents), dprobes = lax.scan(
        cross_backward,
        (zero_memory, zero_memory),
        (probe_tiles, drecalled_tiles, cross_logsum, cross_delta),
    )
    mine_lookups, mine_contents = (
        lax.psum_scatter(
            dlookups.reshape(memory_rows, width).astype(jnp.bfloat16),
            ROW_AXES,
            scatter_dimension=0,
            tiled=True,
        ).astype(jnp.float32),
        lax.psum_scatter(
            dcontents.reshape(memory_rows, width).astype(jnp.bfloat16),
            ROW_AXES,
            scatter_dimension=0,
            tiled=True,
        ).astype(jnp.float32),
    )
    mine_lookups = mine_lookups.astype(jnp.bfloat16)
    mine_contents = mine_contents.astype(jnp.bfloat16)
    grads.lookup_weight = left_product(encoded, mine_lookups)
    grads.content_weight = left_product(encoded, mine_contents)
    grads.content_bias = column_sum(mine_contents)
    encoded_gradient = right_product(mine_lookups, full.lookup_weight) + right_product(
        mine_contents, full.content_weight
    )
    dprobes_low = dprobes.reshape(local_rows, width).astype(jnp.bfloat16)
    grads.probe_weight = left_product(normed_cross, dprobes_low)
    grads.probe_bias = column_sum(dprobes_low)
    dnormed_cross = right_product(dprobes_low, full.probe_weight)
    unused, cross_pull = jax.vjp(layer_norm, first, cross_gain_full, cross_shift_full)
    dfirst_part, grads.cross_gain, grads.cross_shift = cross_pull(dnormed_cross)
    dfirst = dsecond + dfirst_part
    dfirst_low = dfirst.astype(jnp.bfloat16)
    grads.output_weight = left_product(mixed, dfirst_low)
    grads.output_bias = column_sum(dfirst_low)
    dmixed = right_product(dfirst_low, full.output_weight).astype(jnp.bfloat16)
    head_dmixed = lax.all_to_all(dmixed, HEAD, split_axis=1, concat_axis=0, tiled=True)
    dmixed_tiles = head_dmixed.reshape(query_count, query_block, local_heads, HD)
    delta_tiles = jnp.sum(dmixed_tiles.astype(jnp.float32) * attended, axis=-1)
    start_dquery = jnp.zeros((query_count, query_block, local_heads, HD), jnp.float32)
    piece = (
        lax.all_gather(head_keys, BLK, axis=0, tiled=True),
        lax.all_gather(head_values, BLK, axis=0, tiled=True),
    )
    dquery_tiles = start_dquery
    count = piece[0].shape[0]
    block_dquery_tiles = dquery_tiles
    piece_keys = piece[0]
    block_tiles = key_tiles(piece_keys, piece[1])
    count = piece_keys.shape[0]

    def block_per_query(state, args):
        dkey_part, dvalue_part = state
        query_tile, query_seg, query_place, logsum_tile, delta_tile, dmixed_tile, dquery_tile = args

        def block_per_key(dquery_acc, key_args):
            key_tile, value_tile, key_seg, key_place = key_args
            scores, allowed = scores_of(
                query_tile, query_seg, query_place, key_tile, key_seg, key_place
            )
            probs = jnp.where(allowed, jnp.exp(scores - logsum_tile[..., None]), 0.0)
            dprobs = jnp.einsum(
                "qhd,khd->qhk", dmixed_tile, value_tile, preferred_element_type=jnp.float32
            )
            dscores = (probs * (dprobs - delta_tile[..., None])).astype(jnp.bfloat16)
            dquery_acc = (
                dquery_acc
                + jnp.einsum("qhk,khd->qhd", dscores, key_tile, preferred_element_type=jnp.float32)
                * scale
            )
            dkey_tile = (
                jnp.einsum("qhk,qhd->khd", dscores, query_tile, preferred_element_type=jnp.float32)
                * scale
            )
            dvalue_tile = jnp.einsum(
                "qhk,qhd->khd",
                probs.astype(jnp.bfloat16),
                dmixed_tile,
                preferred_element_type=jnp.float32,
            )
            return (dquery_acc, (dkey_tile, dvalue_tile))

        dquery_new, key_terms = lax.scan(block_per_key, dquery_tile, block_tiles)
        return ((dkey_part + key_terms[0], dvalue_part + key_terms[1]), dquery_new)

    zero_part = jnp.zeros(block_tiles[0].shape, jnp.float32)
    parts, block_dquery_tiles = lax.scan(
        block_per_query,
        (zero_part, zero_part),
        (
            query_tiles,
            seg_tiles,
            place_tiles,
            logsum,
            delta_tiles,
            dmixed_tiles,
            block_dquery_tiles,
        ),
    )
    dquery_tiles = block_dquery_tiles
    dkey_part = parts[0].reshape(count, half)
    dvalue_part = parts[1].reshape(count, half)
    dkey_rows = dkey_part
    dvalue_rows = dvalue_part
    dquery_tiles, dkey_rows, dvalue_rows = (dquery_tiles, dkey_rows, dvalue_rows)
    own_dkeys, own_dvalues = (
        lax.psum_scatter(
            dkey_rows.astype(jnp.bfloat16), BLK, scatter_dimension=0, tiled=True
        ).astype(jnp.float32),
        lax.psum_scatter(
            dvalue_rows.astype(jnp.bfloat16), BLK, scatter_dimension=0, tiled=True
        ).astype(jnp.float32),
    )
    row_dqueries, row_dkeys, row_dvalues = (
        lax.all_to_all(
            dquery_tiles.reshape(span, half).astype(jnp.bfloat16),
            HEAD,
            split_axis=0,
            concat_axis=1,
            tiled=True,
        ),
        lax.all_to_all(
            own_dkeys.astype(jnp.bfloat16), HEAD, split_axis=0, concat_axis=1, tiled=True
        ),
        lax.all_to_all(
            own_dvalues.astype(jnp.bfloat16), HEAD, split_axis=0, concat_axis=1, tiled=True
        ),
    )
    grads.query_weight = left_product(normed, row_dqueries)
    grads.query_bias = column_sum(row_dqueries)
    grads.key_weight = left_product(normed, row_dkeys)
    grads.value_weight = left_product(normed, row_dvalues)
    grads.value_bias = column_sum(row_dvalues)
    dnormed = (
        right_product(row_dqueries, full.query_weight)
        + right_product(row_dkeys, full.key_weight)
        + right_product(row_dvalues, full.value_weight)
    )
    unused, self_pull = jax.vjp(layer_norm, rows, self_gain_full, self_shift_full)
    drows_part, grads.self_gain, grads.self_shift = self_pull(dnormed)
    row_gradient = dfirst + drows_part
    shards = tuple(
        (
            lax.psum_scatter(
                grads.self_gain.astype(jnp.bfloat16),
                ROW_AXES,
                scatter_dimension=0,
                tiled=True,
            ).astype(jnp.float32),
            lax.psum_scatter(
                grads.self_shift.astype(jnp.bfloat16),
                ROW_AXES,
                scatter_dimension=0,
                tiled=True,
            ).astype(jnp.float32),
            lax.psum_scatter(
                grads.query_weight.astype(jnp.bfloat16),
                ROW_AXES,
                scatter_dimension=0,
                tiled=True,
            ).astype(jnp.float32),
            lax.psum_scatter(
                grads.query_bias.astype(jnp.bfloat16),
                ROW_AXES,
                scatter_dimension=0,
                tiled=True,
            ).astype(jnp.float32),
            lax.psum_scatter(
                grads.key_weight.astype(jnp.bfloat16),
                ROW_AXES,
                scatter_dimension=0,
                tiled=True,
            ).astype(jnp.float32),
            lax.psum_scatter(
                grads.value_weight.astype(jnp.bfloat16),
                ROW_AXES,
                scatter_dimension=0,
                tiled=True,
            ).astype(jnp.float32),
            lax.psum_scatter(
                grads.value_bias.astype(jnp.bfloat16),
                ROW_AXES,
                scatter_dimension=0,
                tiled=True,
            ).astype(jnp.float32),
            lax.psum_scatter(
                grads.output_weight.astype(jnp.bfloat16),
                ROW_AXES,
                scatter_dimension=0,
                tiled=True,
            ).astype(jnp.float32),
            lax.psum_scatter(
                grads.output_bias.astype(jnp.bfloat16),
                ROW_AXES,
                scatter_dimension=0,
                tiled=True,
            ).astype(jnp.float32),
            lax.psum_scatter(
                grads.cross_gain.astype(jnp.bfloat16),
                ROW_AXES,
                scatter_dimension=0,
                tiled=True,
            ).astype(jnp.float32),
            lax.psum_scatter(
                grads.cross_shift.astype(jnp.bfloat16),
                ROW_AXES,
                scatter_dimension=0,
                tiled=True,
            ).astype(jnp.float32),
            lax.psum_scatter(
                grads.probe_weight.astype(jnp.bfloat16),
                ROW_AXES,
                scatter_dimension=0,
                tiled=True,
            ).astype(jnp.float32),
            lax.psum_scatter(
                grads.probe_bias.astype(jnp.bfloat16),
                ROW_AXES,
                scatter_dimension=0,
                tiled=True,
            ).astype(jnp.float32),
            lax.psum_scatter(
                grads.lookup_weight.astype(jnp.bfloat16),
                ROW_AXES,
                scatter_dimension=0,
                tiled=True,
            ).astype(jnp.float32),
            lax.psum_scatter(
                grads.content_weight.astype(jnp.bfloat16),
                ROW_AXES,
                scatter_dimension=0,
                tiled=True,
            ).astype(jnp.float32),
            lax.psum_scatter(
                grads.content_bias.astype(jnp.bfloat16),
                ROW_AXES,
                scatter_dimension=0,
                tiled=True,
            ).astype(jnp.float32),
            lax.psum_scatter(
                grads.merged_weight.astype(jnp.bfloat16),
                ROW_AXES,
                scatter_dimension=0,
                tiled=True,
            ).astype(jnp.float32),
            lax.psum_scatter(
                grads.merged_bias.astype(jnp.bfloat16),
                ROW_AXES,
                scatter_dimension=0,
                tiled=True,
            ).astype(jnp.float32),
            lax.psum_scatter(
                grads.feed_gain.astype(jnp.bfloat16),
                ROW_AXES,
                scatter_dimension=0,
                tiled=True,
            ).astype(jnp.float32),
            lax.psum_scatter(
                grads.feed_shift.astype(jnp.bfloat16),
                ROW_AXES,
                scatter_dimension=0,
                tiled=True,
            ).astype(jnp.float32),
            lax.psum_scatter(
                grads.up_weight.astype(jnp.bfloat16),
                ROW_AXES,
                scatter_dimension=0,
                tiled=True,
            ).astype(jnp.float32),
            lax.psum_scatter(
                grads.up_bias.astype(jnp.bfloat16),
                ROW_AXES,
                scatter_dimension=0,
                tiled=True,
            ).astype(jnp.float32),
            lax.psum_scatter(
                grads.down_weight.astype(jnp.bfloat16),
                ROW_AXES,
                scatter_dimension=0,
                tiled=True,
            ).astype(jnp.float32),
            lax.psum_scatter(
                grads.down_bias.astype(jnp.bfloat16),
                ROW_AXES,
                scatter_dimension=0,
                tiled=True,
            ).astype(jnp.float32),
        )
    )
    return (
        output_low[:prompt_rows],
        output_low[prompt_rows:],
        row_gradient[:prompt_rows],
        row_gradient[prompt_rows:],
        encoded_gradient,
    ) + shards


NT = (((1,), (1,)), ((), ()))
TN = (((0,), (0,)), ((), ()))
PAIR = 2 * HD
TILE = 256
VMEM_BYTES = 56 * 1024 * 1024


def dot(left, right, dims=(((1,), (0,)), ((), ()))):
    return lax.dot_general(left, right, dims, preferred_element_type=jnp.float32)


def first_lanes(shape):
    return lax.broadcasted_iota(jnp.int32, shape, len(shape) - 1) < HD


def split_heads(values, fill=0.0):
    mine = first_lanes(values.shape)
    other = jnp.full(values.shape, fill, values.dtype)
    return jnp.where(mine, values, other), jnp.where(mine, other, values)


def fold(state, query, key, value, allowed=None):
    top, acc = state
    scores = dot(query, key, NT)
    if allowed is not None:
        scores = jnp.where(allowed, scores, floor_value)
    top_new = jnp.maximum(top, jnp.max(scores, axis=1, keepdims=True))
    weights = jnp.exp(scores - top_new).astype(jnp.bfloat16)
    acc_new = acc * jnp.exp(top - top_new) + dot(weights, value)
    return top_new, acc_new


def close(state0, state1):
    top0, acc0 = state0
    top1, acc1 = state1
    mine = first_lanes(acc0.shape)
    total = jnp.where(mine, pltpu.roll(acc0, HD, 1), pltpu.roll(acc1, HD, 1))
    result = jnp.where(mine, acc0, acc1) / total
    logsum = jnp.where(mine, top0, top1) + jnp.log(total)
    turned = jnp.transpose(logsum)
    return result, turned[0:1], turned[HD : HD + 1]


def segment_start(place, bounds_ref):
    start = jnp.zeros_like(place)
    for at in range(bounds_ref.shape[0] - 1):
        start = jnp.where(place >= bounds_ref[at], bounds_ref[at], start)
    return start


SLAB_OF = (0, 2, 1, 3)
COLUMN_OF = (1, 3, 0, 2)


def shard_of(role):
    quarter, side = role >> 1, role & 1
    return (((quarter & 1) << 1) | (quarter >> 1)) * 2 + side


def natural_rows(role, total, prompt_all):
    local_rows, prompt_rows = total // 8, prompt_all // 8
    order = shard_of(role)
    pieces = []
    for low, high, base in (
        (0, prompt_rows, order * prompt_rows),
        (prompt_rows, local_rows, prompt_all + order * (local_rows - prompt_rows)),
    ):
        if not isinstance(base, int):
            base = pl.multiple_of(base, prompt_rows)
        pieces.append((low, high, pl.ds(base, high - low)))
    return pieces


def group_pieces(groups, lines_ref, total, prompt_all):
    pieces = []
    at = 0
    for group in groups:
        for place in range(group.shape[0]):
            for low, high, where in natural_rows(lines_ref[at], total, prompt_all):
                pieces.append((group, place, low, high, where))
            at += 1
    return pieces


def self_forward_kernel(
    prompt_all,
    lines_ref,
    bounds_ref,
    near_ref,
    next_ref,
    far_ref,
    att_ref,
    low_ref,
    lse_ref,
    qn,
    kn,
    v0n,
    v1n,
):
    groups = (near_ref, next_ref, far_ref)
    total = qn.shape[0]
    for group, place, low, high, where in group_pieces(groups, lines_ref, total, prompt_all):
        qn[where] = group[place, low:high, 0:PAIR] * jnp.bfloat16(HD**-0.5)
        kn[where] = group[place, low:high, PAIR : 2 * PAIR]
        v0n[where], v1n[where] = split_heads(group[place, low:high, 2 * PAIR : 3 * PAIR], 1.0)

    prompt_tiles = prompt_all // TILE
    tiles = qn.shape[0] // TILE
    start = (
        jnp.full((TILE, 1), floor_value, jnp.float32),
        jnp.zeros((TILE, PAIR), jnp.float32),
    )

    def both(state, query, base, size, allowed=None):
        key = kn[pl.ds(base, size)]
        return (
            fold(state[0], query[0], key, v0n[pl.ds(base, size)], allowed),
            fold(state[1], query[1], key, v1n[pl.ds(base, size)], allowed),
        )

    def finish(tile, state):
        result, lse0, lse1 = close(*state)
        att_ref[pl.ds(tile * TILE, TILE)] = result
        lse_ref[tile, 0:1, :] = lse0
        lse_ref[tile, 1:2, :] = lse1

    query_at = lax.broadcasted_iota(jnp.int32, (TILE, TILE), 0)
    key_at = lax.broadcasted_iota(jnp.int32, (TILE, TILE), 1)

    def prompt_tile(tile, carry):
        query = split_heads(qn[pl.ds(tile * TILE, TILE)])
        state = lax.fori_loop(
            0, tile, lambda at, now: both(now, query, at * TILE, TILE), (start, start)
        )
        state = both(state, query, tile * TILE, TILE, key_at <= query_at)
        finish(tile, state)
        return carry

    lax.fori_loop(0, prompt_tiles, prompt_tile, 0)

    def cont_tile(tile, carry):
        query = split_heads(qn[pl.ds(tile * TILE, TILE)])
        state = (start, start)
        for at in range(0, prompt_all, 2 * TILE):
            state = both(state, query, at, 2 * TILE)
        first_place = tile * TILE - prompt_all
        place = first_place + query_at
        begin = segment_start(place, bounds_ref)

        def cont_step(at, now):
            key_place = at * TILE - prompt_all + key_at
            return both(now, query, at * TILE, TILE, (key_place <= place) & (key_place >= begin))

        first_key = prompt_tiles + segment_start(first_place, bounds_ref) // TILE
        state = lax.fori_loop(first_key, tile + 1, cont_step, state)
        finish(tile, state)
        return carry

    lax.fori_loop(prompt_tiles, tiles, cont_tile, 0)
    for role in range(8):
        for low, high, where in natural_rows(role, total, prompt_all):
            low_ref[role, low:high] = att_ref[where].astype(jnp.bfloat16)


def unfold(query, key, value, grad, lse, delta, allowed=None):
    probs = jnp.exp(dot(key, query, NT) - lse)
    if allowed is not None:
        probs = jnp.where(allowed, probs, 0.0)
    dscores = (probs * (dot(value, grad, NT) - delta)).astype(jnp.bfloat16)
    return probs.astype(jnp.bfloat16), dscores


def head_inner(left, right):
    turned = jnp.transpose(left * right)
    return (
        jnp.sum(turned[:HD], axis=0, keepdims=True),
        jnp.sum(turned[HD:], axis=0, keepdims=True),
    )


def self_backward_kernel(
    prompt_all,
    lines_ref,
    bounds_ref,
    near_ref,
    next_ref,
    far_ref,
    grad_ref,
    att_ref,
    lse_ref,
    near_out,
    next_out,
    far_out,
    qn,
    kn,
    vn,
    gn,
    dqn,
    dkn,
    dvn,
):
    total = qn.shape[0]
    groups = (near_ref, next_ref, far_ref)
    for group, place, low, high, where in group_pieces(groups, lines_ref, total, prompt_all):
        qn[where] = group[place, low:high, 0:PAIR] * jnp.bfloat16(HD**-0.5)
        kn[where] = group[place, low:high, PAIR : 2 * PAIR]
        vn[where] = group[place, low:high, 2 * PAIR : 3 * PAIR]
    for role in range(8):
        for low, high, where in natural_rows(role, total, prompt_all):
            gn[where] = grad_ref[role, low:high]
    dkn[...] = jnp.zeros_like(dkn)
    dvn[...] = jnp.zeros_like(dvn)
    prompt_tiles = prompt_all // TILE
    tiles = qn.shape[0] // TILE
    key_at = lax.broadcasted_iota(jnp.int32, (TILE, TILE), 0)
    query_at = lax.broadcasted_iota(jnp.int32, (TILE, TILE), 1)

    def load(tile):
        query = split_heads(qn[pl.ds(tile * TILE, TILE)])
        whole = gn[pl.ds(tile * TILE, TILE)]
        grad = split_heads(whole)
        delta = head_inner(whole.astype(jnp.float32), att_ref[pl.ds(tile * TILE, TILE)])
        lse = (lse_ref[tile, 0:1, :], lse_ref[tile, 1:2, :])
        return query, grad, lse, delta

    def step(acc, query, grad, lse, delta, base, allowed=None):
        where = pl.ds(base, TILE)
        key, value = kn[where], vn[where]
        keys = split_heads(key)
        dkey, dvalue = dkn[where], dvn[where]
        for side in range(2):
            probs, dscores = unfold(
                query[side], key, value, grad[side], lse[side], delta[side], allowed
            )
            dvalue = dvalue + dot(probs, grad[side])
            dkey = dkey + dot(dscores, query[side])
            acc = acc + dot(dscores, keys[side], TN)
        dkn[where] = dkey
        dvn[where] = dvalue
        return acc

    def finish(tile, acc):
        dqn[pl.ds(tile * TILE, TILE)] = (acc * HD**-0.5).astype(jnp.bfloat16)

    start = jnp.zeros((TILE, PAIR), jnp.float32)

    def prompt_tile(tile, carry):
        given = load(tile)
        acc = lax.fori_loop(0, tile, lambda at, now: step(now, *given, at * TILE), start)
        acc = step(acc, *given, tile * TILE, key_at <= query_at)
        finish(tile, acc)
        return carry

    lax.fori_loop(0, prompt_tiles, prompt_tile, 0)

    def cont_tile(tile, carry):
        given = load(tile)
        acc = lax.fori_loop(0, prompt_tiles, lambda at, now: step(now, *given, at * TILE), start)
        first_place = tile * TILE - prompt_all
        place = first_place + query_at
        begin = segment_start(place, bounds_ref)

        def cont_step(at, now):
            key_place = at * TILE - prompt_all + key_at
            return step(now, *given, at * TILE, (key_place <= place) & (key_place >= begin))

        first_key = prompt_tiles + segment_start(first_place, bounds_ref) // TILE
        acc = lax.fori_loop(first_key, tile + 1, cont_step, acc)
        finish(tile, acc)
        return carry

    lax.fori_loop(prompt_tiles, tiles, cont_tile, 0)
    outs = (near_out, next_out, far_out)
    for group, place, low, high, where in group_pieces(outs, lines_ref, total, prompt_all):
        group[place, low:high, 0:PAIR] = dqn[where]
        group[place, low:high, PAIR : 2 * PAIR] = dkn[where].astype(jnp.bfloat16)
        group[place, low:high, 2 * PAIR : 3 * PAIR] = dvn[where].astype(jnp.bfloat16)


def cost(micros):
    return pl.CostEstimate(
        flops=int(micros * 9e8), bytes_accessed=int(micros * 2e6), transcendentals=0
    )


def in_vmem(count):
    return [pl.BlockSpec(memory_space=pltpu.VMEM)] * count


def in_smem(count):
    return [pl.BlockSpec(memory_space=pltpu.SMEM)] * count


def self_forward(lines, bounds, groups, prompt_all):
    local_rows = groups[0].shape[1]
    total = 8 * local_rows
    natural = pltpu.VMEM((total, PAIR), jnp.bfloat16)
    return pl.pallas_call(
        functools.partial(self_forward_kernel, prompt_all),
        out_shape=(
            jax.ShapeDtypeStruct((total, PAIR), jnp.float32),
            jax.ShapeDtypeStruct((8, local_rows, PAIR), jnp.bfloat16),
            jax.ShapeDtypeStruct((total // TILE, 2, TILE), jnp.float32),
        ),
        in_specs=in_smem(2) + in_vmem(3),
        out_specs=tuple(in_vmem(3)),
        scratch_shapes=[natural] * 4,
        compiler_params=pltpu.CompilerParams(vmem_limit_bytes=VMEM_BYTES),
        cost_estimate=cost(44),
        name="self_forward",
    )(lines, bounds, *groups)


def self_backward(lines, bounds, groups, grad, att, lse, prompt_all):
    total = 8 * groups[0].shape[1]
    natural = pltpu.VMEM((total, PAIR), jnp.bfloat16)
    wide = pltpu.VMEM((total, PAIR), jnp.float32)
    return pl.pallas_call(
        functools.partial(self_backward_kernel, prompt_all),
        out_shape=tuple(jax.ShapeDtypeStruct(group.shape, jnp.bfloat16) for group in groups),
        in_specs=in_smem(2) + in_vmem(6),
        out_specs=tuple(in_vmem(3)),
        scratch_shapes=[natural] * 5 + [wide] * 2,
        compiler_params=pltpu.CompilerParams(vmem_limit_bytes=VMEM_BYTES),
        cost_estimate=cost(60),
        name="self_backward",
    )(lines, bounds, *groups, grad, att, lse)


def pick(refs, target):
    at = pl.program_id(0)
    for place, ref in enumerate(refs):

        @pl.when(at == place)
        def unused(ref=ref):
            target[...] = ref[0 : target.shape[0]]


def project_kernel(count, *refs):
    gain_ref, shift_ref, weight_ref, bias_ref = refs[count : count + 4]
    normed_ref, rows_ref, chunk = refs[count + 4 :]
    pick(refs[:count], chunk)
    unit, unused = norm_parts(chunk[...].astype(jnp.float32))
    normed = (unit * gain_ref[...] + shift_ref[...]).astype(jnp.bfloat16)
    normed_ref[0] = normed
    rows_ref[0] = (dot(normed, weight_ref[...]) + bias_ref[...]).astype(jnp.bfloat16)


def fixed(shape):
    return pl.BlockSpec(shape, lambda at, *unused: (0,) * len(shape), pipeline_mode=pl.Buffered(1))


def stepped(shape):
    return pl.BlockSpec((1,) + shape, lambda at, *unused: (at,) + (0,) * len(shape))


def project(chunks, rows, gain, shift, weight, bias):
    count = len(chunks)
    width, columns = weight.shape
    return pl.pallas_call(
        functools.partial(project_kernel, count),
        grid=(count,),
        out_shape=(
            jax.ShapeDtypeStruct((count, rows, width), jnp.bfloat16),
            jax.ShapeDtypeStruct((count, rows, columns), jnp.bfloat16),
        ),
        in_specs=[fixed(chunk.shape) for chunk in chunks]
        + [fixed((1, width)), fixed((1, width)), fixed(weight.shape), fixed((1, columns))],
        out_specs=(stepped((rows, width)), stepped((rows, columns))),
        scratch_shapes=[pltpu.VMEM((rows, width), jnp.bfloat16)],
        compiler_params=pltpu.CompilerParams(vmem_limit_bytes=VMEM_BYTES),
        cost_estimate=cost(2.3 * count),
        name="project",
    )(*chunks, gain[None], shift[None], weight, bias[None])


def feed_kernel(count, first, last, info_ref, *refs):
    chunks, refs = refs[:count], refs[count:]
    upstreams, refs = refs[:count], refs[count:]
    weights_ref, bias_ref = refs[:2]
    refs = refs[2:]
    if not first:
        up_before, down_before, sum_before = refs[:3]
        refs = refs[3:]
    out_ref, dnormed_ref, up_after, down_after, sum_after = refs[:5]
    chunk, upstream_chunk, up_sum, down_sum, bias_sum, sems = refs[5:]
    at = pl.program_id(0)

    def carried():
        return (
            pltpu.make_async_copy(up_before, up_sum, sems.at[0]),
            pltpu.make_async_copy(down_before, down_sum, sems.at[1]),
        )

    @pl.when(at == 0)
    def begin():
        if first:
            up_sum[...] = jnp.zeros_like(up_sum)
            down_sum[...] = jnp.zeros_like(down_sum)
            bias_sum[...] = jnp.zeros_like(bias_sum)
        else:
            for copy in carried():
                copy.start()
            bias_sum[...] = sum_before[...]

    pick(chunks, chunk)
    pick(upstreams, upstream_chunk)
    feed = chunk[...]
    upstream = upstream_chunk[...]
    blocks, both, width = weights_ref.shape
    step = both // 2
    out = None
    for low in range(0, blocks * step, step):
        where = slice(low, low + step)
        up = weights_ref[:, :step, where].reshape(blocks * step, step)
        down = weights_ref[low // step, step:]
        hidden = dot(feed, up) + bias_ref[:, where]
        tail = 0.5 + 0.5 * lax.erf(hidden * math.sqrt(0.5))
        active = (hidden * tail).astype(jnp.bfloat16)
        slope = tail + hidden * jnp.exp(-0.5 * hidden * hidden) * (1.0 / math.sqrt(2.0 * math.pi))
        dhidden = (dot(upstream, down, NT) * slope).astype(jnp.bfloat16)
        if low == 0 and not first:

            @pl.when(at == 0)
            def arrive():
                for copy in carried():
                    copy.wait()

        bias_sum[0:1, where] += jnp.sum(dhidden.astype(jnp.float32), axis=0, keepdims=True)
        up_sum[:, where] += dot(feed, dhidden, TN)
        down_sum[where] += dot(active, upstream, TN)
        term, dterm = dot(active, down), dot(dhidden, up, NT)
        out, dnormed = (term, dterm) if out is None else (out + term, dnormed + dterm)
    out_ref[0] = out.astype(jnp.bfloat16)
    dnormed_ref[0] = dnormed.astype(jnp.bfloat16)

    @pl.when(at == count - 1)
    def end():
        sum_after[...] = bias_sum[...]
        if last:
            rows = up_sum.shape[0] // 8
            for role in range(8):
                line = 2 * COLUMN_OF[role // 2] + role % 2
                where = slice(line * rows, (line + 1) * rows)
                up_after[role] = up_sum[where].astype(jnp.bfloat16)
            quarter = info_ref[0]
            for block in range(4):
                where = slice(block * step, (block + 1) * step)
                slot = block ^ quarter
                down_after[slot, :step] = down_sum[where].astype(jnp.bfloat16)
                down_after[slot, step:, :step] = jnp.broadcast_to(
                    bias_sum[0:1, where], (16, step)
                ).astype(jnp.bfloat16)
        else:
            pltpu.sync_copy(up_sum, up_after)
            pltpu.sync_copy(down_sum, down_after)


def feed(chunks, upstreams, info, weights, bias, before, last):
    count = len(chunks)
    rows, width = chunks[0].shape
    columns = bias.shape[0]
    first = before is None
    anywhere = pl.BlockSpec(memory_space=pl.ANY)

    sums = jax.ShapeDtypeStruct((8, columns), jnp.float32)
    out_shape = [
        jax.ShapeDtypeStruct((count, rows, width), jnp.bfloat16),
        jax.ShapeDtypeStruct((count, rows, width), jnp.bfloat16),
    ]
    if last:
        shapes = ((8, width // 8, columns), (4, columns // 4 + 16, width))
        out_shape += [jax.ShapeDtypeStruct(shape, jnp.bfloat16) for shape in shapes]
        sum_specs = [fixed(shape) for shape in shapes]
    else:
        shapes = ((width, columns), (columns, width))
        out_shape += [jax.ShapeDtypeStruct(shape, jnp.float32) for shape in shapes]
        sum_specs = [anywhere, anywhere]
    extra = [] if first else [anywhere, anywhere, fixed((8, columns))]
    carried = () if first else before
    return pl.pallas_call(
        functools.partial(feed_kernel, count, first, last),
        grid_spec=pltpu.PrefetchScalarGridSpec(
            num_scalar_prefetch=1,
            grid=(count,),
            in_specs=[fixed((rows, width))] * (2 * count)
            + [fixed(weights.shape), fixed((1, columns))]
            + extra,
            out_specs=[stepped((rows, width)), stepped((rows, width))] + sum_specs + [fixed((8, columns))],
            scratch_shapes=[
                pltpu.VMEM((rows, width), jnp.bfloat16),
                pltpu.VMEM((rows, width), jnp.bfloat16),
                pltpu.VMEM((width, columns), jnp.float32),
                pltpu.VMEM((columns, width), jnp.float32),
                pltpu.VMEM((8, columns), jnp.float32),
                pltpu.SemaphoreType.DMA((2,)),
            ],
        ),
        out_shape=out_shape + [sums],
        compiler_params=pltpu.CompilerParams(vmem_limit_bytes=VMEM_BYTES),
        cost_estimate=cost(10.5 * count),
        name="feed",
    )(info, *chunks, *upstreams, weights, bias[None], *carried)


def cross_forward_kernel(probe_ref, lookup_ref, content_ref, out_ref, lse_ref):
    query = split_heads(probe_ref[...] * jnp.bfloat16(HD**-0.5))
    key = lookup_ref[...]
    values = split_heads(content_ref[...], 1.0)
    rows = query[0].shape[0]
    start = (jnp.full((rows, 1), floor_value, jnp.float32), jnp.zeros((rows, PAIR), jnp.float32))
    states = [fold(start, query[side], key, values[side]) for side in range(2)]
    result, lse0, lse1 = close(*states)
    out_ref[...] = result
    lse_ref[0, 0:1, :] = lse0
    lse_ref[0, 1:2, :] = lse1


def cross_backward_kernel(
    probe_ref,
    lookup_ref,
    content_ref,
    grad_ref,
    out_ref,
    lse_ref,
    lookup_weight_ref,
    content_weight_ref,
    dprobe_ref,
    dmemory_ref,
    dencoded_ref,
    dencoded,
):
    query = split_heads(probe_ref[...] * jnp.bfloat16(HD**-0.5))
    key = lookup_ref[...]
    keys = split_heads(key)
    value = content_ref[...]
    whole = grad_ref[...]
    grad = split_heads(whole)
    delta = head_inner(whole.astype(jnp.float32), out_ref[...])
    terms = []
    for side in range(2):
        probs, dscores = unfold(
            query[side], key, value, grad[side], lse_ref[0, side : side + 1, :], delta[side]
        )
        terms.append(
            (
                dot(dscores, keys[side], TN),
                dot(dscores, query[side]),
                dot(probs, grad[side]),
            )
        )
    dprobe_ref[...] = ((terms[0][0] + terms[1][0]) * HD**-0.5).astype(jnp.bfloat16)
    dlookup = (terms[0][1] + terms[1][1]).astype(jnp.bfloat16)
    dcontent = (terms[0][2] + terms[1][2]).astype(jnp.bfloat16)
    rows = dmemory_ref.shape[1] // 2
    for block in range(8):
        columns = slice(block * PAIR, (block + 1) * PAIR)
        dmemory_ref[0, :rows, columns] = dlookup[block * rows : (block + 1) * rows]
        dmemory_ref[0, rows:, columns] = dcontent[block * rows : (block + 1) * rows]
    term = dot(dlookup, lookup_weight_ref[...], NT) + dot(dcontent, content_weight_ref[...], NT)

    @pl.when(pl.program_id(0) == 0)
    def begin():
        dencoded[...] = term

    @pl.when(pl.program_id(0) > 0)
    def more():
        dencoded[...] += term

    @pl.when(pl.program_id(0) == 7)
    def end():
        dencoded_ref[...] = dencoded[...].astype(jnp.bfloat16)


def pair_block(rows):
    return pl.BlockSpec((rows, PAIR), lambda at: (0, at))


def cross_forward(probes, lookups, contents):
    rows, width = probes.shape
    memory = lookups.shape[0]
    pairs = width // PAIR
    return pl.pallas_call(
        cross_forward_kernel,
        grid=(pairs,),
        out_shape=(
            jax.ShapeDtypeStruct((rows, width), jnp.float32),
            jax.ShapeDtypeStruct((pairs, 2, rows), jnp.float32),
        ),
        in_specs=[pair_block(rows), pair_block(memory), pair_block(memory)],
        out_specs=(pair_block(rows), pl.BlockSpec((1, 2, rows), lambda at: (at, 0, 0))),
        compiler_params=pltpu.CompilerParams(vmem_limit_bytes=VMEM_BYTES),
        cost_estimate=cost(10),
        name="cross_forward",
    )(probes, lookups, contents)


def cross_backward(probes, lookups, contents, grad, recalled, lse, lookup_weight, content_weight):
    rows, width = probes.shape
    memory = lookups.shape[0]
    pairs = width // PAIR
    return pl.pallas_call(
        cross_backward_kernel,
        grid=(pairs,),
        out_shape=(
            jax.ShapeDtypeStruct((rows, width), jnp.bfloat16),
            jax.ShapeDtypeStruct((pairs, 2 * memory // 8, width), jnp.bfloat16),
            jax.ShapeDtypeStruct((memory, width), jnp.bfloat16),
        ),
        in_specs=[
            pair_block(rows),
            pair_block(memory),
            pair_block(memory),
            pair_block(rows),
            pair_block(rows),
            pl.BlockSpec((1, 2, rows), lambda at: (at, 0, 0)),
            pair_block(width),
            pair_block(width),
        ],
        out_specs=(
            pair_block(rows),
            pl.BlockSpec((1, 2 * memory // 8, width), lambda at: (at, 0, 0)),
            fixed((memory, width)),
        ),
        scratch_shapes=[pltpu.VMEM((memory, width), jnp.float32)],
        compiler_params=pltpu.CompilerParams(vmem_limit_bytes=VMEM_BYTES),
        cost_estimate=cost(20),
        name="cross_backward",
    )(probes, lookups, contents, grad, recalled, lse, lookup_weight, content_weight)


def norm_parts(values):
    center = jnp.mean(values, axis=-1, keepdims=True)
    centred = values - center
    spread = jnp.mean(centred * centred, axis=-1, keepdims=True)
    rate = lax.rsqrt(spread + 1e-05)
    return centred * rate, rate


def norm_backward(grad, unit, rate, gain):
    scaled = grad * gain
    along = jnp.mean(scaled, axis=-1, keepdims=True)
    across = jnp.mean(scaled * unit, axis=-1, keepdims=True)
    return (
        rate * (scaled - along - unit * across),
        jnp.sum(grad * unit, axis=0),
        jnp.sum(grad, axis=0),
    )


def joined(group, block, side=0, sides=1):
    return (group * 4 + block) * sides + side


class Slab:
    def __init__(self):
        group, side = lax.axis_index(GRP), lax.axis_index(HEAD)
        self.group, self.side, self.block = group, side, lax.axis_index(BLK)
        column, core = group // 2, group % 2
        chips = ((0, 0), (1, 0), (1, 1), (0, 1))
        lines = [[4 * left + 2 * own + right for left, right in chips] for own in range(2)]
        self.forward = [(line[at], line[(at + 1) % 4]) for line in lines for at in range(4)]
        self.reverse = [(right, left) for left, right in self.forward]
        self.cores = [(role, role ^ 2) for role in range(8)]
        place = jnp.where(column == 0, 3 * side, 1 + side)
        owners = []
        for step, other in ((0, 0), (0, 1), (-1, 0), (1, 0), (-1, 1), (1, 1), (2, 0), (2, 1)):
            there = (place + step) % 4
            far = ((there == 1) | (there == 2)).astype(jnp.int32)
            owners.append(4 * far + 2 * ((core + other) % 2) + (there >= 2).astype(jnp.int32))
        self.lines = jnp.stack(owners).astype(jnp.int32)

    def up(self, values):
        return lax.ppermute(values, ROLE_AXES, self.forward)

    def down(self, values):
        return lax.ppermute(values, ROLE_AXES, self.reverse)

    def swap(self, values):
        return lax.ppermute(values, ROLE_AXES, self.cores)

    def gather(self, values, gates=(None, None)):
        half = values.shape[0] // 2
        left, right, other = self.up(values), self.down(values), self.swap(values)
        if gates[0] is not None:
            left, right, other = after((left, right, other), gates[0])
        pair = (self.up(left[:half]), self.down(right[half:]))
        near, far = self.swap(left), self.swap(right)
        if gates[1] is not None:
            pair, near, far = after((pair, near, far), gates[1])
        last = jnp.concatenate(pair, axis=0)
        return ((values, other), (left, right, near, far), (last, self.swap(last)))

    def scatter(self, near, after_parts, far, gates=(None, None, None)):
        low, wide = jnp.bfloat16, jnp.float32
        swaps = [self.swap(far[1]), self.swap(after_parts[2:4]), self.swap(near[1])]
        if gates[0] is not None:
            swaps = after(swaps, gates[0])
        last = far[0].astype(wide) + swaps[0]
        half = last.shape[0] // 2
        sent = (self.up(last[:half].astype(low)), self.down(last[half:].astype(low)))
        if gates[1] is not None:
            sent = after(sent, gates[1])
        left, right = sent
        pair = after_parts[0:2].astype(wide) + swaps[1]
        behind, ahead = pair[0], pair[1]
        left = jnp.concatenate([left + ahead[:half], ahead[half:]], axis=0).astype(low)
        right = jnp.concatenate([behind[:half], right + behind[half:]], axis=0).astype(low)
        sent = (self.up(left), self.down(right))
        if gates[2] is not None:
            sent = after(sent, gates[2])
        return near[0].astype(wide) + swaps[2] + sent[0] + sent[1]

    def enter(self, values):
        moves = [
            (joined(group, block), joined(SLAB_OF[block], SLAB_OF[group]))
            for group in range(4)
            for block in range(4)
        ]
        return lax.ppermute(values, (GRP, BLK), moves)

    def leave(self, values):
        moves = [
            (joined(group, block), joined(SLAB_OF[block], SLAB_OF[group]))
            for group in range(4)
            for block in range(4)
        ]
        return lax.ppermute(values, (GRP, BLK), moves)

    def leave_columns(self, values):
        moves = [
            (joined(group, block), joined(SLAB_OF[block], COLUMN_OF[group]))
            for group in range(4)
            for block in range(4)
        ]
        return lax.ppermute(values, (GRP, BLK), moves)

    def leave_quarters(self, pieces):
        result = []
        for at, piece in enumerate(pieces):
            moves = [
                (joined(group, block), joined(SLAB_OF[block], group ^ at))
                for group in range(4)
                for block in range(4)
            ]
            result.append(lax.ppermute(piece, (GRP, BLK), moves))
        return result

    def settle(self, parts, blank):
        for at, part in enumerate(parts):
            start = (self.block ^ at,) + (0,) * part.ndim
            blank = lax.dynamic_update_slice(blank, part[None].astype(blank.dtype), start)
        return blank

    def leave_own(self, values):
        moves = [
            (joined(group, block, side, 2), joined(SLAB_OF[block], group, side, 2))
            for group in range(4)
            for block in range(4)
            for side in range(2)
        ]
        return lax.ppermute(values, ALL_AXES, moves)


def by_role(values, order=SLAB_OF):
    values = values.reshape((4, 2, -1) + values.shape[1:])
    values = jnp.stack([values[at] for at in order])
    return values.reshape((8,) + values.shape[2:])


def after(values, *others):
    return lax.optimization_barrier((values,) + others)[0]


def exchange(values, axes):
    return lax.all_to_all(values, axes, split_axis=0, concat_axis=0, tiled=True)


def columns_kernel(pieces_ref, out_ref):
    part = pieces_ref.shape[2] // 4
    for role in range(8):
        for block in range(4):
            order = (block * 2 + role % 2) * 4 + role // 2
            out_ref[:, order * part : (order + 1) * part] = pieces_ref[
                role, :, block * part : (block + 1) * part
            ].astype(jnp.float32)


def settle_columns(pieces):
    roles, rows, columns = pieces.shape
    return pl.pallas_call(
        columns_kernel,
        out_shape=jax.ShapeDtypeStruct((rows, roles * columns), jnp.float32),
        in_specs=in_vmem(1),
        out_specs=pl.BlockSpec(memory_space=pltpu.VMEM),
        compiler_params=pltpu.CompilerParams(vmem_limit_bytes=VMEM_BYTES),
        cost_estimate=cost(4),
        name="settle_columns",
    )(pieces)


def heads_kernel(pieces_ref, *outs):
    for role in range(8):
        for place, out_ref in enumerate(outs):
            out_ref[:, role * PAIR : (role + 1) * PAIR] = pieces_ref[
                role, :, place * PAIR : (place + 1) * PAIR
            ].astype(jnp.float32)


def settle_heads(pieces):
    roles, rows, columns = pieces.shape
    count = columns // PAIR
    return pl.pallas_call(
        heads_kernel,
        out_shape=(jax.ShapeDtypeStruct((rows, roles * PAIR), jnp.float32),) * count,
        in_specs=in_vmem(1),
        out_specs=tuple(in_vmem(count)),
        compiler_params=pltpu.CompilerParams(vmem_limit_bytes=VMEM_BYTES),
        cost_estimate=cost(3),
        name="settle_heads",
    )(pieces)


def head_body(
    prompt,
    continued,
    encoded,
    cont_lengths,
    self_gain,
    self_shift,
    query_weight,
    query_bias,
    key_weight,
    value_weight,
    value_bias,
    output_weight,
    output_bias,
    cross_gain,
    cross_shift,
    probe_weight,
    probe_bias,
    lookup_weight,
    content_weight,
    content_bias,
    merged_weight,
    merged_bias,
    feed_gain,
    feed_shift,
    up_weight,
    up_bias,
    down_weight,
    down_bias,
    cot_prompt,
    cot_cont,
):
    slab = Slab()
    low = jnp.bfloat16
    width = prompt.shape[1]
    shard = width // 8
    piece = shard // 4
    prompt_rows = prompt.shape[0]
    local_rows = prompt_rows + continued.shape[0]
    prompt_all = 8 * prompt_rows
    memory_rows = encoded.shape[0]
    quarter, side = slab.group, slab.side
    role = 2 * quarter + side

    swapped = [
        (joined(group, block), joined(block, SLAB_OF[group]))
        for group in range(4)
        for block in range(4)
    ]
    lengths = lax.ppermute(cont_lengths, (GRP, BLK), swapped)
    bounds = jnp.cumsum(lengths).astype(jnp.int32)

    own_all = slab.enter(jnp.concatenate([prompt, continued, encoded], axis=0))

    def head_columns(weight):
        mine = lax.dynamic_slice_in_dim(weight.reshape(shard, 4, 2 * shard), quarter, 1, axis=1)
        return mine.reshape(shard, 2, shard).transpose(1, 0, 2)

    small = (
        self_gain,
        self_shift,
        output_bias,
        cross_gain,
        cross_shift,
        probe_bias,
        merged_bias,
        feed_gain,
        feed_shift,
        down_bias,
        content_bias,
        query_bias,
        value_bias,
    )
    vectors = jnp.concatenate(small + (up_bias,) + (self_gain,) * 3).reshape(1, 8, 3 * shard)
    mixed_in = jnp.concatenate(
        [
            jnp.concatenate(
                [head_columns(query_weight), head_columns(key_weight), head_columns(value_weight)],
                axis=2,
            ),
            jnp.broadcast_to(vectors, (2, 8, 3 * shard)),
        ],
        axis=1,
    )
    mixed_in = jnp.broadcast_to(mixed_in[None], (4,) + mixed_in.shape)
    mixed_in = exchange(mixed_in.reshape(8, shard + 8, 3 * shard), ROW_AXES)
    own_all, mixed_in = lax.optimization_barrier((own_all, mixed_in))
    head_weights = mixed_in[:, :shard].reshape(width, 3 * shard)
    vectors = mixed_in[:, shard:].reshape(8, 24, shard)
    packed = vectors[:, : len(small)].transpose(1, 0, 2).reshape(len(small), width)
    (
        self_gain_full,
        self_shift_full,
        output_bias_full,
        cross_gain_full,
        cross_shift_full,
        probe_bias_full,
        merged_bias_full,
        feed_gain_full,
        feed_shift_full,
        down_bias_full,
        content_bias_full,
        query_bias_full,
        value_bias_full,
    ) = [packed[at].astype(jnp.float32) for at in range(len(small))]
    ups = vectors[:, len(small) : len(small) + 8].reshape(4, 2, 4, -1)
    ups = lax.dynamic_index_in_dim(ups, side, 1, keepdims=False)
    up_bias_own = lax.dynamic_index_in_dim(ups, quarter, 1, keepdims=False).reshape(width)
    up_bias_own = up_bias_own.astype(jnp.float32)

    row_groups = slab.gather(own_all)
    up_mine = lax.dynamic_index_in_dim(
        up_weight.reshape(shard, 4, 2, 4, -1), quarter, 3, keepdims=False
    )
    up_mine = up_mine.transpose(2, 0, 1, 3).reshape(2, shard, width)
    up_mine = exchange(after(up_mine, own_all), HEAD).reshape(2 * shard, width)
    down_mine = lax.dynamic_slice_in_dim(down_weight, quarter * 2 * shard, 2 * shard, axis=0)

    squares = (output_weight, probe_weight, merged_weight, lookup_weight, content_weight)
    shared = jnp.concatenate(
        [lax.dynamic_slice_in_dim(weight, quarter * piece, piece, axis=0) for weight in squares],
        axis=0,
    )
    shared = after(shared, own_all)
    shared = lax.all_gather(shared, (BLK, HEAD, GRP), axis=0, tiled=False)
    shared = shared.reshape(32, len(squares), piece, width)
    output_full, probe_full, merged_full, lookup_full, content_full = [
        shared[:, at].reshape(width, width) for at in range(len(squares))
    ]

    rows = own_all[:local_rows].astype(jnp.float32)

    def own_columns(vector):
        return lax.dynamic_slice_in_dim(vector, role * shard, shard, axis=0)

    head_bias = jnp.concatenate(
        [
            own_columns(query_bias_full),
            jnp.zeros((shard,), jnp.float32),
            own_columns(value_bias_full),
        ]
    )
    projected = [
        project(group, local_rows, self_gain_full, self_shift_full, head_weights, head_bias)
        for group in row_groups
    ]
    upstream = slab.enter(
        after(jnp.concatenate([cot_prompt, cot_cont], axis=0), own_all)
    )
    feed_weights = jnp.concatenate([up_mine, down_mine], axis=0)
    feed_weights = lax.all_gather(feed_weights, BLK, axis=0, tiled=False)
    head_groups = [pair[1] for pair in projected]
    attended, attended_low, logsum = self_forward(slab.lines, bounds, head_groups, prompt_all)
    upstream_groups = slab.gather(
        after(upstream, row_groups[2]), (head_groups[2], attended_low)
    )
    mixed = exchange(attended_low, ROLE_AXES).transpose(1, 0, 2).reshape(local_rows, width)
    first = rows + matmul(mixed, output_full) + output_bias_full
    first_unit, first_rate = norm_parts(first)
    normed_cross = (first_unit * cross_gain_full + cross_shift_full).astype(low)
    probes = (matmul(normed_cross, probe_full) + probe_bias_full).astype(low)

    memory = jnp.zeros((8 * memory_rows, width), low)
    chunks = [chunk for group in row_groups for chunk in group]
    for at, chunk in enumerate(chunks):
        memory = lax.dynamic_update_slice_in_dim(
            memory, chunk[local_rows:], slab.lines[at] * memory_rows, axis=0
        )
    lookups = matmul(memory, lookup_full).astype(low)
    contents = (matmul(memory, content_full) + content_bias_full).astype(low)
    recalled, cross_logsum = cross_forward(probes, lookups, contents)
    recalled_low = recalled.astype(low)
    second = first + matmul(recalled_low, merged_full) + merged_bias_full
    second_unit, second_rate = norm_parts(second)
    normed_feed = (second_unit * feed_gain_full + feed_shift_full).astype(low)

    before, dnormed_parts, output_parts = None, [], []
    feed_groups = slab.gather(normed_feed)
    info = quarter[None].astype(jnp.int32)
    for group, upstream_group in zip(feed_groups, upstream_groups):
        last = group is feed_groups[-1]
        output, dnormed, *before = feed(
            group, upstream_group, info, feed_weights, up_bias_own, before, last
        )
        dnormed_parts.append(dnormed)
        output_parts.append(output)
    up_gradient, down_gradient, unused = before
    dnormed_feed = slab.scatter(*dnormed_parts)
    up_gradient, down_gradient, output_parts = after(
        (up_gradient, down_gradient, output_parts), dnormed_feed
    )
    up_gradient = exchange(up_gradient, ROLE_AXES)
    down_gradient = slab.leave_quarters([down_gradient[at] for at in range(4)])

    part, feed_gain_sum, feed_shift_sum = norm_backward(
        dnormed_feed, second_unit, second_rate, feed_gain_full
    )
    dsecond = upstream.astype(jnp.float32) + part
    dsecond_low = dsecond.astype(low)
    drecalled = right_product(dsecond_low, merged_full).astype(low)
    dprobes, dmemory, encoded_gradient = cross_backward(
        probes,
        lookups,
        contents,
        drecalled,
        recalled,
        cross_logsum,
        lookup_full,
        content_full,
    )
    dnormed_cross = right_product(dprobes, probe_full)
    part, cross_gain_sum, cross_shift_sum = norm_backward(
        dnormed_cross, first_unit, first_rate, cross_gain_full
    )
    dfirst = dsecond + part
    dfirst_low = dfirst.astype(low)
    dmixed = right_product(dfirst_low, output_full).astype(low)
    dmixed = dmixed.reshape(local_rows, 8, shard).transpose(1, 0, 2)
    output = slab.scatter(*output_parts, (drecalled, dprobes, dmixed))
    output = slab.leave((second + output + down_bias_full).astype(low))
    up_gradient, down_gradient, dmixed = lax.optimization_barrier(
        (up_gradient, down_gradient, dmixed)
    )
    dmixed = exchange(dmixed, ROLE_AXES)
    up_gradient = slab.leave_columns(up_gradient)

    sums = jnp.stack(
        (
            column_sum(dfirst_low),
            cross_gain_sum,
            cross_shift_sum,
            column_sum(dprobes),
            column_sum(dsecond_low),
            feed_gain_sum,
            feed_shift_sum,
            column_sum(upstream),
        )
    )
    sums = by_role(sums.T).transpose(0, 2, 1).reshape(8, 1, width)
    sums = jnp.broadcast_to(sums, (8, 16, width))
    scattered = jnp.concatenate(
        [
            by_role(left_product(recalled_low, dsecond_low).astype(low)),
            by_role(left_product(normed_cross, dprobes).astype(low)),
            encoded_gradient.reshape(8, memory_rows, width),
            by_role(left_product(mixed, dfirst_low).astype(low)),
            sums.astype(low),
            dmemory,
        ],
        axis=1,
    )
    scattered = lax.psum_scatter(scattered, ROLE_AXES, scatter_dimension=0, tiled=False)

    dhead_groups = self_backward(
        slab.lines, bounds, head_groups, dmixed, attended, logsum, prompt_all
    )
    done = dhead_groups[0]

    dnormed = slab.scatter(
        *[
            right_product(group.reshape(-1, 3 * shard), head_weights)
            .astype(low)
            .reshape(group.shape[0], local_rows, width)
            for group in dhead_groups
        ]
    )

    up_gradient, down_gradient, output, scattered = after(
        (up_gradient, down_gradient, output, scattered), done
    )
    up_weight_gradient = settle_columns(up_gradient)
    down_weight_gradient = slab.settle(
        [part[: 2 * shard] for part in down_gradient], jnp.zeros((4, 2 * shard, width), jnp.float32)
    ).reshape(width, width)
    up_bias_gradient = slab.settle(
        [part[2 * shard, : 2 * shard] for part in down_gradient],
        jnp.zeros((4, 2 * shard), jnp.float32),
    ).reshape(width)

    encoded_end = 2 * shard + memory_rows
    squares_end = encoded_end + shard + 16
    mine_dmemory = scattered[squares_end:].reshape(2, memory_rows, 8, shard)
    mine_dmemory = mine_dmemory.transpose(0, 2, 1, 3)
    mine_dmemory = mine_dmemory.reshape(2, 8 * memory_rows, shard)

    head_gradient = [
        sum(
            left_product(normed.reshape(-1, width), group.reshape(-1, 3 * shard))
            for (normed, unused), group in zip(projected, dhead_groups)
        ),
        left_product(memory, mine_dmemory[0]),
        left_product(memory, mine_dmemory[1]),
    ]
    head_gradient = jnp.concatenate([part.astype(low) for part in head_gradient], axis=1)
    head_gradient = exchange(by_role(head_gradient, COLUMN_OF), ROLE_AXES)
    (
        query_weight_gradient,
        key_weight_gradient,
        value_weight_gradient,
        lookup_weight_gradient,
        content_weight_gradient,
    ) = settle_heads(slab.leave_columns(head_gradient))
    head_sums = sum(column_sum(group.reshape(-1, 3 * shard)) for group in dhead_groups)
    head_sums = slab.leave_own(
        jnp.stack([head_sums[:shard], head_sums[2 * shard :], column_sum(mine_dmemory[1])])
    )
    unit, rate = norm_parts(rows)
    part, self_gain_sum, self_shift_sum = norm_backward(dnormed, unit, rate, self_gain_full)
    row_gradient = jnp.concatenate([(dfirst + part).astype(low), scattered[:squares_end]], axis=0)
    row_gradient = slab.leave(row_gradient).astype(jnp.float32)
    square_gradient = row_gradient[local_rows:]
    merged_weight_gradient = square_gradient[:shard]
    probe_weight_gradient = square_gradient[shard : 2 * shard]
    encoded_gradient = square_gradient[2 * shard : encoded_end]
    output_weight_gradient = square_gradient[encoded_end : encoded_end + shard]
    small_sums = square_gradient[encoded_end + shard].reshape(8, shard)
    (
        output_bias_gradient,
        cross_gain_gradient,
        cross_shift_gradient,
        probe_bias_gradient,
        merged_bias_gradient,
        feed_gain_gradient,
        feed_shift_gradient,
        down_bias_gradient,
    ) = [small_sums[at] for at in range(8)]

    sums = by_role(jnp.stack((self_gain_sum, self_shift_sum), axis=1))
    sums = jnp.sum(exchange(sums.transpose(0, 2, 1), ROLE_AXES), axis=0)
    sums = slab.leave(sums)
    up_bias_gradient = up_bias_gradient.reshape(-1)
    query_bias_gradient, value_bias_gradient, content_bias_gradient = [
        head_sums[at] for at in range(3)
    ]
    self_gain_gradient, self_shift_gradient = sums[0], sums[1]

    return (
        (
            output[:prompt_rows],
            output[prompt_rows:],
            row_gradient[:prompt_rows],
            row_gradient[prompt_rows:local_rows],
            encoded_gradient,
            self_gain_gradient,
            self_shift_gradient,
            query_weight_gradient,
            query_bias_gradient,
            key_weight_gradient,
            value_weight_gradient,
            value_bias_gradient,
            output_weight_gradient,
            output_bias_gradient,
            cross_gain_gradient,
            cross_shift_gradient,
            probe_weight_gradient,
            probe_bias_gradient,
            lookup_weight_gradient,
            content_weight_gradient,
            content_bias_gradient,
            merged_weight_gradient,
            merged_bias_gradient,
            feed_gain_gradient,
            feed_shift_gradient,
            up_weight_gradient,
            up_bias_gradient,
            down_weight_gradient,
            down_bias_gradient,
        )
    )


def solution(mesh):
    rows, group = P(ALL_AXES, None), P(ALL_AXES)
    weight, vector = P(ROW_AXES, None), P(ROW_AXES)
    ranks = [2 if "weight" in name else 1 for name in PARAM_NAMES]
    sizes = tuple(mesh.shape[axis] for axis in ALL_AXES)
    return jax.shard_map(
        head_body if sizes == (4, 4, 2) and HEADS * HD == 8 * PAIR else token_body,
        mesh=mesh,
        in_specs=(rows, rows, rows, P(GRP))
        + tuple(weight if rank == 2 else vector for rank in ranks)
        + (rows, rows),
        out_specs=(rows,) * 5 + tuple(rows if rank == 2 else group for rank in ranks),
        check_vma=False,
    )
```

profile of v0, /device:TPU:1, one launch (start us, length us, event | category | flops | bytes accessed | tf_op | source)
XLA Modules:
  0.0 817.3 jit_solution(6741938743649873392)
XLA Ops:
  16.1 6.4 all-to-all-start
  23.6 5.3 collective-permute-start
  33.1 30.7 %collective-permute-done.refs_0_ = bf16[448,1024]{1,0:T(8,128)(2,1)S(1)} collective-permute-done((bf16[448,1024]{1,0:T(8,128)(2,1)}, bf16[448,1024]{1,0:T(8,128)(2,1)S(1)}, u32[]{:S(2)}, u32[]{:S(2)}) %collective-permute-start) | collective-permute-done | bytes 917536 | tf_op jit(solution)/shard_map/ppermute | solution.py:1363
  65.9 4.1 copy.145
  76.8 5.0 collective-permute-start.2
  83.5 3.5 all-to-all-start.2
  89.7 5.9 collective-permute-start.15
  95.8 12.6 %all-to-all-done.2 = bf16[2,128,1024]{1,2,0:T(8,128)(2,1)S(1)} async-done(((bf16[2,128,1024]{1,2,0:T(8,128)(2,1)}), bf16[2,128,1024]{1,2,0:T(8,128)(2,1)S(1)}, u32[]{:S(2)}, u32[]{:S(2)}) %all-to-all-start.2) | async-done | bytes 524320 | tf_op jit(solution)/shard_map/all_to_all | solution.py:1419
  113.3 3.9 collective-permute-start.5
  120.0 4.4 project.3
  124.4 9.0 %collective-permute-done.7 = bf16[224,1024]{1,0:T(8,128)(2,1)S(1)} collective-permute-done((bf16[224,1024]{1,0:T(8,128)(2,1)S(1)}, bf16[224,1024]{1,0:T(8,128)(2,1)S(1)}, u32[]{:S(2)}, u32[]{:S(2)}) %collective-permute-start.7) | collective-permute-done | bytes 458784 | tf_op jit(solution)/shard_map/ppermute | solution.py:1317
  137.4 6.9 project.4
  144.3 2.3 collective-permute-start.16
  147.2 4.3 project.5
  151.6 44.0 %self_forward.1 = (f32[3072,128]{1,0:T(8,128)}, bf16[8,384,128]{2,1,0:T(8,128)(2,1)}, f32[12,2,256]{2,1,0:T(2,128)}) custom-call(s32[8]{0:T(128)} %stack.102.lines_ref, s32[2]{0:T(128)} %bitcast.417, bf16[2,384,384]{2,1,0:T(8,128)(2,1)} %get-tuple-element.105.near_ref, bf16[4,384,384]{2,1,0:T(8,128)(2,1)} %get-tuple-element.106.next_ref, ...), custom_call_target="tpu_custom_call" | custom-call | flops 39600001024 | bytes 88000000 | tf_op jit(solution)/shard_map/self_forward/pallas_call | solution.py:941
  195.5 3.6 all-to-all-start.1
  201.0 9.5 %all-to-all-done.1 = bf16[8,384,128]{2,1,0:T(8,128)(2,1)S(1)} async-done(((bf16[8,384,128]{2,1,0:T(8,128)(2,1)}), bf16[8,384,128]{2,1,0:T(8,128)(2,1)S(1)}, u32[]{:S(2)}, u32[]{:S(2)}) %all-to-all-start.1) | async-done | bytes 786464 | tf_op jit(solution)/shard_map/all_to_all | solution.py:1419
  217.8 4.8 fusion.50
  224.3 2.6 convolution_convert_fusion.6.lookup_ref
  226.9 2.2 add_convert_fusion.content_ref
  231.1 9.7 %cross_forward.1 = (f32[384,1024]{1,0:T(8,128)}, f32[8,2,384]{2,1,0:T(2,128)}) custom-call(bf16[384,1024]{1,0:T(8,128)(2,1)} %add_convert_fusion.3.probe_ref, bf16[512,1024]{1,0:T(8,128)(2,1)} %convolution_convert_fusion.6.lookup_ref, bf16[512,1024]{1,0:T(8,128)(2,1)} %add_convert_fusion.content_ref), custom_call_target="tpu_custom_call" | custom-call | flops 8999999488 | bytes 20000000 | tf_op jit(solution)/shard_map/cross_forward/pallas_call | solution.py:1226
  240.9 2.5 fusion.63
  253.4 9.8 %collective-permute-done.10.refs_0_ = bf16[384,1024]{1,0:T(8,128)(2,1)} collective-permute-done((bf16[384,1024]{1,0:T(8,128)(2,1)}, bf16[384,1024]{1,0:T(8,128)(2,1)}, u32[]{:S(2)}, u32[]{:S(2)}) %collective-permute-start.10) | collective-permute-done | bytes 786464 | tf_op jit(solution)/shard_map/ppermute | solution.py:1317
  268.5 2.6 collective-permute-start.24
  272.6 22.0 %feed.3 = (bf16[2,384,1024]{2,1,0:T(8,128)(2,1)}, bf16[2,384,1024]{2,1,0:T(8,128)(2,1)}, f32[1024,1024]{1,0:T(8,128)}, f32[1024,1024]{1,0:T(8,128)}, f32[8,1024]{1,0:T(8,128)}) custom-call(s32[1]{0:T(128)} %bitcast.info_ref, bf16[384,1024]{1,0:T(8,128)(2,1)} %add_convert_fusion.2.refs_0_, bf16[384,1024]{1,0:T(8,128)(2,1)} %collective-permute-done.26.refs_1_, ...), custom_call_target="tpu_custom_call" | custom-call | flops 18900000768 | bytes 42000000 | tf_op jit(solution)/shard_map/feed/pallas_call | solution.py:1124
  296.5 39.2 %feed.4 = (bf16[4,384,1024]{2,1,0:T(8,128)(2,1)}, bf16[4,384,1024]{2,1,0:T(8,128)(2,1)}, f32[1024,1024]{1,0:T(8,128)}, f32[1024,1024]{1,0:T(8,128)}, f32[8,1024]{1,0:T(8,128)}) custom-call(s32[1]{0:T(128)} %bitcast.info_ref, bf16[384,1024]{1,0:T(8,128)(2,1)} %collective-permute-done.10.refs_0_, bf16[384,1024]{1,0:T(8,128)(2,1)} %collective-permute-done.12.refs_1_, ...), custom_call_target="tpu_custom_call" | custom-call | flops 37800001536 | bytes 84000000 | tf_op jit(solution)/shard_map/feed/pallas_call | solution.py:1124
  335.7 2.7 slice.639
  339.3 22.3 %feed.5 = (bf16[2,384,1024]{2,1,0:T(8,128)(2,1)}, bf16[2,384,1024]{2,1,0:T(8,128)(2,1)}, bf16[8,128,1024]{2,1,0:T(8,128)(2,1)}, bf16[4,272,1024]{2,1,0:T(8,128)(2,1)}, f32[8,1024]{1,0:T(8,128)}) custom-call(s32[1]{0:T(128)} %bitcast.info_ref, bf16[384,1024]{1,0:T(8,128)(2,1)} %copy-done.46, bf16[384,1024]{1,0:T(8,128)(2,1)} %copy-done.86, ...), custom_call_target="tpu_custom_call" | custom-call | flops 18900000768 | bytes 42000000 | tf_op jit(solution)/shard_map/feed/pallas_call | solution.py:1124
  371.7 6.6 collective-permute-done.29
  381.7 15.4 %collective-permute-done.31 = bf16[384,1024]{1,0:T(8,128)(2,1)S(1)} collective-permute-done((bf16[384,1024]{1,0:T(8,128)(2,1)S(1)}, bf16[384,1024]{1,0:T(8,128)(2,1)S(1)}, u32[]{:S(2)}, u32[]{:S(2)}) %collective-permute-start.31) | collective-permute-done | bytes 786464 | tf_op jit(solution)/shard_map/ppermute | solution.py:1317
  403.2 21.0 %cross_backward.1 = (bf16[384,1024]{1,0:T(8,128)(2,1)}, bf16[8,128,1024]{2,1,0:T(8,128)(2,1)}, bf16[512,1024]{1,0:T(8,128)(2,1)}) custom-call(bf16[384,1024]{1,0:T(8,128)(2,1)} %add_convert_fusion.3.probe_ref, bf16[512,1024]{1,0:T(8,128)(2,1)} %convolution_convert_fusion.6.lookup_ref, bf16[512,1024]{1,0:T(8,128)(2,1)} %add_convert_fusion.content_ref, ...), custom_call_target="tpu_custom_call" | custom-call | flops 17999998976 | bytes 40000000 | tf_op jit(solution)/shard_map/cross_backward/pallas_call | solution.py:1245
  424.3 3.6 multiply_reduce_fusion.1
  428.1 2.7 convolution_convert_fusion.2
  430.8 2.6 convolution_convert_fusion.3
  433.4 7.0 all-to-all-start.3
  440.4 3.6 convert_reduce_fusion.5
  444.1 2.9 convolution_convert_fusion.1
  464.7 3.1 slice_bitcast_fusion.10
  467.9 2.9 collective-permute-start.34
  475.6 3.1 collective-permute-start.35
  485.2 24.5 %collective-permute-done.34 = bf16[272,1024]{1,0:T(8,128)(2,1)} collective-permute-done((bf16[272,1024]{1,0:T(8,128)(2,1)}, bf16[272,1024]{1,0:T(8,128)(2,1)}, u32[]{:S(2)}, u32[]{:S(2)}) %collective-permute-start.34) | collective-permute-done | bytes 557088 | tf_op jit(solution)/shard_map/ppermute | solution.py:1389
  511.1 3.9 convert_add_fusion.1
  515.0 5.2 collective-permute-done.35
  520.2 6.3 collective-permute-done.37
  526.5 4.2 all-to-all-start.4
  530.8 4.4 collective-permute-done.43
  540.4 9.1 %all-to-all-done.4.grad_ref = bf16[8,384,128]{2,1,0:T(8,128)(2,1)} async-done(((bf16[8,384,128]{2,1,0:T(8,128)(2,1)}), bf16[8,384,128]{2,1,0:T(8,128)(2,1)}, u32[]{:S(2)}, u32[]{:S(2)}) %all-to-all-start.4) | async-done | bytes 786464 | tf_op jit(solution)/shard_map/all_to_all | solution.py:1419
  549.5 59.9 %self_backward.1 = (bf16[2,384,384]{2,1,0:T(8,128)(2,1)}, bf16[4,384,384]{2,1,0:T(8,128)(2,1)}, bf16[2,384,384]{2,1,0:T(8,128)(2,1)}) custom-call(s32[8]{0:T(128)} %stack.102.lines_ref, s32[2]{0:T(128)} %bitcast.418, bf16[2,384,384]{2,1,0:T(8,128)(2,1)} %get-tuple-element.105.near_ref, bf16[4,384,384]{2,1,0:T(8,128)(2,1)} %get-tuple-element.106.next_ref, ...), custom_call_target="tpu_custom_call" | custom-call | flops 54000001024 | bytes 120000000 | tf_op jit(solution)/shard_map/self_backward/pallas_call | solution.py:961
  620.6 2.4 fusion.22
  626.0 7.7 collective-permute-done.49
  638.1 2.8 fusion.18
  640.9 10.5 %collective-permute-start.46 = (bf16[384,1024]{1,0:T(8,128)(2,1)}, bf16[384,1024]{1,0:T(8,128)(2,1)}, u32[]{:S(2)}, u32[]{:S(2)}) collective-permute-start(bf16[384,1024]{1,0:T(8,128)(2,1)} %fusion.18), channel_id=1, source_target_pairs={{0,0},{2,16},{4,8},{6,24},{8,4},{10,20},{12,12},{14,28},{16,2},{18... | collective-permute-start | bytes 2359304 | tf_op jit(solution)/shard_map/ppermute | solution.py:1371
  651.5 9.4 %collective-permute-done.51 = bf16[384,1024]{1,0:T(8,128)(2,1)S(1)} collective-permute-done((bf16[384,1024]{1,0:T(8,128)(2,1)S(1)}, bf16[384,1024]{1,0:T(8,128)(2,1)S(1)}, u32[]{:S(2)}, u32[]{:S(2)}) %collective-permute-start.51) | collective-permute-done | bytes 786464 | tf_op jit(solution)/shard_map/ppermute | solution.py:1317
  663.7 6.5 all-to-all-start.5
  670.2 30.9 %all-to-all-done.5 = f32[8,2,128]{2,1,0:T(2,128)S(1)} async-done(((f32[8,2,128]{2,1,0:T(2,128)}), f32[8,2,128]{2,1,0:T(2,128)S(1)}, u32[]{:S(2)}, u32[]{:S(2)}) %all-to-all-start.5) | async-done | bytes 8224 | tf_op jit(solution)/shard_map/all_to_all | solution.py:1419
  701.1 9.8 %collective-permute-start.55 = (f32[2,128]{1,0:T(2,128)S(1)}, f32[2,128]{1,0:T(2,128)S(1)}, u32[]{:S(2)}, u32[]{:S(2)}) collective-permute-start(f32[2,128]{1,0:T(2,128)S(1)} %reduce_sum.265), channel_id=1, source_target_pairs={{0,0},{2,16},{4,8},{6,24},{8,4},{10,20},{12,12},{14,28},{16,2},{18... | collective-permute-start | bytes 3080 | tf_op jit(solution)/shard_map/ppermute | solution.py:1371
  722.9 2.3 pad_maximum_fusion.5
  725.2 4.2 all-to-all-start.6
  730.8 3.8 collective-permute-start.54
  734.7 2.5 broadcast_in_dim.29
  747.1 4.9 all-to-all-done.6
  754.1 3.9 settle_columns.1
  762.9 39.9 %collective-permute-done.57 = f32[3,128]{1,0:T(4,128)S(1)} collective-permute-done((f32[3,128]{1,0:T(4,128)S(1)}, f32[3,128]{1,0:T(4,128)S(1)}, u32[]{:S(2)}, u32[]{:S(2)}) %collective-permute-start.57) | collective-permute-done | bytes 1568 | tf_op jit(solution)/shard_map/ppermute | solution.py:1405
  807.5 3.1 settle_heads.1
  (497 shorter events, 183.1 us)
Async XLA Ops:
  16.1 47.7 %all-to-all-start = ((bf16[8,136,384]{2,1,0:T(8,128)(2,1)}), bf16[8,136,384]{2,1,0:T(8,128)(2,1)}, u32[]{:S(2)}, u32[]{:S(2)}) async-start(bf16[8,136,384]{2,1,0:T(8,128)(2,1)} %bitcast.10), calls=%async_computation | async-start | bytes 1671168 | tf_op jit(solution)/shard_map/all_to_all | solution.py:1419
  22.5 195.3 %all-gather.5.cloned.1.call-start = ((), (), s32[]{:S(2)}) async-start(), calls=%async_computation.9 | async-start | bytes 10813440 | tf_op jit(solution)/shard_map/all_gather | solution.py:1591
  23.6 40.2 %collective-permute-start = (bf16[448,1024]{1,0:T(8,128)(2,1)}, bf16[448,1024]{1,0:T(8,128)(2,1)S(1)}, u32[]{:S(2)}, u32[]{:S(2)}) collective-permute-start(bf16[448,1024]{1,0:T(8,128)(2,1)} %pad_maximum_fusion.7), channel_id=1, source_target_pairs={{0,0},{2,16},{4,8},{6,24},{8,4},{10,20},{12,12},{14,28},{16,2},{18... | collective-permute-start | bytes 2752520 | tf_op jit(solution)/shard_map/ppermute | solution.py:1363
  63.8 10.8 %collective-permute-start.1 = (s32[2]{0:T(128)S(1)}, s32[2]{0:T(128)S(1)}, u32[]{:S(2)}, u32[]{:S(2)}) collective-permute-start(s32[2]{0:T(128)S(1)} %copy-done.87), channel_id=1, source_target_pairs={{0,0},{2,8},{4,16},{6,24},{8,4},{10,12},{12,20},{14,28},{16,2},{18... | collective-permute-start | bytes 32 | tf_op jit(solution)/shard_map/ppermute | solution.py:1516
  75.3 34.3 %collective-permute-start.4 = (bf16[448,1024]{1,0:T(8,128)(2,1)S(1)}, bf16[448,1024]{1,0:T(8,128)(2,1)}, u32[]{:S(2)}, u32[]{:S(2)}) collective-permute-start(bf16[448,1024]{1,0:T(8,128)(2,1)S(1)} %collective-permute-done.refs_0_), channel_id=1, source_target_pairs={{16,0},{17,16},{1,17},{0,1},{24,8},{25,24},{9,25},{8,9},{18,2},{19... | collective-permute-start | bytes 2752520 | tf_op jit(solution)/shard_map/ppermute | solution.py:1320
  76.3 34.5 %collective-permute-start.3 = (bf16[448,1024]{1,0:T(8,128)(2,1)S(1)}, bf16[448,1024]{1,0:T(8,128)(2,1)}, u32[]{:S(2)}, u32[]{:S(2)}) collective-permute-start(bf16[448,1024]{1,0:T(8,128)(2,1)S(1)} %collective-permute-done.refs_0_), channel_id=1, source_target_pairs={{0,16},{16,17},{17,1},{1,0},{8,24},{24,25},{25,9},{9,8},{2,18},{18... | collective-permute-start | bytes 2752520 | tf_op jit(solution)/shard_map/ppermute | solution.py:1317
  76.8 40.5 %collective-permute-start.2 = (bf16[448,1024]{1,0:T(8,128)(2,1)S(1)}, bf16[448,1024]{1,0:T(8,128)(2,1)}, u32[]{:S(2)}, u32[]{:S(2)}) collective-permute-start(bf16[448,1024]{1,0:T(8,128)(2,1)S(1)} %collective-permute-done.refs_0_), channel_id=1, source_target_pairs={{0,8},{1,9},{8,0},{9,1},{16,24},{17,25},{24,16},{25,17},{2,10},{3,... | collective-permute-start | bytes 2752520 | tf_op jit(solution)/shard_map/ppermute | solution.py:1323
  83.5 24.8 %all-to-all-start.2 = ((bf16[2,128,1024]{1,2,0:T(8,128)(2,1)}), bf16[2,128,1024]{1,2,0:T(8,128)(2,1)S(1)}, u32[]{:S(2)}, u32[]{:S(2)}) async-start(bf16[2,128,1024]{1,2,0:T(8,128)(2,1)} %bitcast.48), calls=%async_computation.2 | async-start | bytes 1048576 | tf_op jit(solution)/shard_map/all_to_all | solution.py:1419
  87.0 185.6 %all-gather.7.cloned.1.call-start = ((), (), s32[]{:S(2)}) async-start(), calls=%async_computation.10 | async-start | bytes 5242880 | tf_op jit(solution)/shard_map/all_gather | solution.py:1617
  89.7 54.6 %collective-permute-start.15 = (bf16[384,1024]{1,0:T(8,128)(2,1)}, bf16[384,1024]{1,0:T(8,128)(2,1)}, u32[]{:S(2)}, u32[]{:S(2)}) collective-permute-start(bf16[384,1024]{1,0:T(8,128)(2,1)} %pad_maximum_fusion.8), channel_id=1, source_target_pairs={{0,0},{2,16},{4,8},{6,24},{8,4},{10,20},{12,12},{14,28},{16,2},{18... | collective-permute-start | bytes 2359304 | tf_op jit(solution)/shard_map/ppermute | solution.py:1363
  110.7 22.7 %collective-permute-start.8 = (bf16[224,1024]{1,0:T(8,128)(2,1)S(1)}, bf16[224,1024]{1,0:T(8,128)(2,1)S(1)}, u32[]{:S(2)}, u32[]{:S(2)}) collective-permute-start(bf16[224,1024]{1,0:T(8,128)(2,1)S(1)} %slice.776), channel_id=1, source_target_pairs={{16,0},{17,16},{1,17},{0,1},{24,8},{25,24},{9,25},{8,9},{18,2},{19... | collective-permute-start | bytes 1376264 | tf_op jit(solution)/shard_map/ppermute | solution.py:1320
  111.8 21.6 %collective-permute-start.7 = (bf16[224,1024]{1,0:T(8,128)(2,1)S(1)}, bf16[224,1024]{1,0:T(8,128)(2,1)S(1)}, u32[]{:S(2)}, u32[]{:S(2)}) collective-permute-start(bf16[224,1024]{1,0:T(8,128)(2,1)S(1)} %slice.775), channel_id=1, source_target_pairs={{0,16},{16,17},{17,1},{1,0},{8,24},{24,25},{25,9},{9,8},{2,18},{18... | collective-permute-start | bytes 1376264 | tf_op jit(solution)/shard_map/ppermute | solution.py:1317
  113.3 22.3 %collective-permute-start.5 = (bf16[448,1024]{1,0:T(8,128)(2,1)}, bf16[448,1024]{1,0:T(8,128)(2,1)S(1)}, u32[]{:S(2)}, u32[]{:S(2)}) collective-permute-start(bf16[448,1024]{1,0:T(8,128)(2,1)} %collective-permute-done.3.refs_0_), channel_id=1, source_target_pairs={{0,8},{1,9},{8,0},{9,1},{16,24},{17,25},{24,16},{25,17},{2,10},{3,... | collective-permute-start | bytes 2752520 | tf_op jit(solution)/shard_map/ppermute | solution.py:1323
  117.2 18.3 %collective-permute-start.6 = (bf16[448,1024]{1,0:T(8,128)(2,1)}, bf16[448,1024]{1,0:T(8,128)(2,1)S(1)}, u32[]{:S(2)}, u32[]{:S(2)}) collective-permute-start(bf16[448,1024]{1,0:T(8,128)(2,1)} %collective-permute-done.4.refs_1_), channel_id=1, source_target_pairs={{0,8},{1,9},{8,0},{9,1},{16,24},{17,25},{24,16},{25,17},{2,10},{3,... | collective-permute-start | bytes 2752520 | tf_op jit(solution)/shard_map/ppermute | solution.py:1323
  133.4 10.8 %collective-permute-start.9 = (bf16[448,1024]{1,0:T(8,128)(2,1)S(1)}, bf16[448,1024]{1,0:T(8,128)(2,1)S(1)}, u32[]{:S(2)}, u32[]{:S(2)}) collective-permute-start(bf16[448,1024]{1,0:T(8,128)(2,1)S(1)} %constant_dynamic-update-slice_fusion.refs_0_), channel_id=1, source_target_pairs={{0,8},{1,9},{8,0},{9,1},{16,24},{17,25},{24,16},{25,17},{2,10},{3,... | collective-permute-start | bytes 2752520 | tf_op jit(solution)/shard_map/ppermute | solution.py:1323
  144.3 67.4 %collective-permute-start.16 = (bf16[384,1024]{1,0:T(8,128)(2,1)}, bf16[384,1024]{1,0:T(8,128)(2,1)}, u32[]{:S(2)}, u32[]{:S(2)}) collective-permute-start(bf16[384,1024]{1,0:T(8,128)(2,1)} %collective-permute-done.15.refs_2_), channel_id=1, source_target_pairs={{0,16},{16,17},{17,1},{1,0},{8,24},{24,25},{25,9},{9,8},{2,18},{18... | collective-permute-start | bytes 2359304 | tf_op jit(solution)/shard_map/ppermute | solution.py:1317
  146.6 65.1 %collective-permute-start.17 = (bf16[384,1024]{1,0:T(8,128)(2,1)}, bf16[384,1024]{1,0:T(8,128)(2,1)}, u32[]{:S(2)}, u32[]{:S(2)}) collective-permute-start(bf16[384,1024]{1,0:T(8,128)(2,1)} %collective-permute-done.15.refs_2_), channel_id=1, source_target_pairs={{16,0},{17,16},{1,17},{0,1},{24,8},{25,24},{9,25},{8,9},{18,2},{19... | collective-permute-start | bytes 2359304 | tf_op jit(solution)/shard_map/ppermute | solution.py:1320
  146.7 64.9 %collective-permute-start.18 = (bf16[384,1024]{1,0:T(8,128)(2,1)}, bf16[384,1024]{1,0:T(8,128)(2,1)S(1)}, u32[]{:S(2)}, u32[]{:S(2)}) collective-permute-start(bf16[384,1024]{1,0:T(8,128)(2,1)} %collective-permute-done.15.refs_2_), channel_id=1, source_target_pairs={{0,8},{1,9},{8,0},{9,1},{16,24},{17,25},{24,16},{25,17},{2,10},{3,... | collective-permute-start | bytes 2359304 | tf_op jit(solution)/shard_map/ppermute | solution.py:1323
  195.5 15.0 %all-to-all-start.1 = ((bf16[8,384,128]{2,1,0:T(8,128)(2,1)}), bf16[8,384,128]{2,1,0:T(8,128)(2,1)S(1)}, u32[]{:S(2)}, u32[]{:S(2)}) async-start(bf16[8,384,128]{2,1,0:T(8,128)(2,1)} %get-tuple-element.108), calls=%async_computation.1 | async-start | bytes 1572864 | tf_op jit(solution)/shard_map/all_to_all | solution.py:1419
  213.7 37.1 %collective-permute-start.21 = (bf16[384,1024]{1,0:T(8,128)(2,1)}, bf16[384,1024]{1,0:T(8,128)(2,1)}, u32[]{:S(2)}, u32[]{:S(2)}) collective-permute-start(bf16[384,1024]{1,0:T(8,128)(2,1)} %collective-permute-done.16.refs_4_), channel_id=1, source_target_pairs={{0,8},{1,9},{8,0},{9,1},{16,24},{17,25},{24,16},{25,17},{2,10},{3,... | collective-permute-start | bytes 2359304 | tf_op jit(solution)/shard_map/ppermute | solution.py:1323
  216.1 34.7 %collective-permute-start.22 = (bf16[384,1024]{1,0:T(8,128)(2,1)}, bf16[384,1024]{1,0:T(8,128)(2,1)}, u32[]{:S(2)}, u32[]{:S(2)}) collective-permute-start(bf16[384,1024]{1,0:T(8,128)(2,1)} %collective-permute-done.17.refs_5_), channel_id=1, source_target_pairs={{0,8},{1,9},{8,0},{9,1},{16,24},{17,25},{24,16},{25,17},{2,10},{3,... | collective-permute-start | bytes 2359304 | tf_op jit(solution)/shard_map/ppermute | solution.py:1323
  216.1 30.0 %collective-permute-start.19 = (bf16[192,1024]{1,0:T(8,128)(2,1)}, bf16[192,1024]{1,0:T(8,128)(2,1)S(1)}, u32[]{:S(2)}, u32[]{:S(2)}) collective-permute-start(bf16[192,1024]{1,0:T(8,128)(2,1)} %slice.630), channel_id=1, source_target_pairs={{0,16},{16,17},{17,1},{1,0},{8,24},{24,25},{25,9},{9,8},{2,18},{18... | collective-permute-start | bytes 1179656 | tf_op jit(solution)/shard_map/ppermute | solution.py:1317
  217.2 29.3 %collective-permute-start.20 = (bf16[192,1024]{1,0:T(8,128)(2,1)}, bf16[192,1024]{1,0:T(8,128)(2,1)}, u32[]{:S(2)}, u32[]{:S(2)}) collective-permute-start(bf16[192,1024]{1,0:T(8,128)(2,1)} %slice.631), channel_id=1, source_target_pairs={{16,0},{17,16},{1,17},{0,1},{24,8},{25,24},{9,25},{8,9},{18,2},{19... | collective-permute-start | bytes 1179656 | tf_op jit(solution)/shard_map/ppermute | solution.py:1320
  245.0 18.3 %collective-permute-start.10 = (bf16[384,1024]{1,0:T(8,128)(2,1)}, bf16[384,1024]{1,0:T(8,128)(2,1)}, u32[]{:S(2)}, u32[]{:S(2)}) collective-permute-start(bf16[384,1024]{1,0:T(8,128)(2,1)} %add_convert_fusion.2.refs_0_), channel_id=1, source_target_pairs={{0,16},{16,17},{17,1},{1,0},{8,24},{24,25},{25,9},{9,8},{2,18},{18... | collective-permute-start | bytes 2359304 | tf_op jit(solution)/shard_map/ppermute | solution.py:1317
  246.1 20.3 %collective-permute-start.12 = (bf16[384,1024]{1,0:T(8,128)(2,1)}, bf16[384,1024]{1,0:T(8,128)(2,1)}, u32[]{:S(2)}, u32[]{:S(2)}) collective-permute-start(bf16[384,1024]{1,0:T(8,128)(2,1)} %add_convert_fusion.2.refs_0_), channel_id=1, source_target_pairs={{16,0},{17,16},{1,17},{0,1},{24,8},{25,24},{9,25},{8,9},{18,2},{19... | collective-permute-start | bytes 2359304 | tf_op jit(solution)/shard_map/ppermute | solution.py:1320
  246.5 24.6 %collective-permute-start.26 = (bf16[384,1024]{1,0:T(8,128)(2,1)}, bf16[384,1024]{1,0:T(8,128)(2,1)}, u32[]{:S(2)}, u32[]{:S(2)}) collective-permute-start(bf16[384,1024]{1,0:T(8,128)(2,1)} %add_convert_fusion.2.refs_0_), channel_id=1, source_target_pairs={{0,8},{1,9},{8,0},{9,1},{16,24},{17,25},{24,16},{25,17},{2,10},{3,... | collective-permute-start | bytes 2359304 | tf_op jit(solution)/shard_map/ppermute | solution.py:1323
  253.4 85.0 %collective-permute-start.23 = (bf16[384,1024]{1,0:T(8,128)(2,1)}, bf16[384,1024]{1,0:T(8,128)(2,1)}, u32[]{:S(2)}, u32[]{:S(2)}) collective-permute-start(bf16[384,1024]{1,0:T(8,128)(2,1)} %constant_dynamic-update-slice_fusion.4.refs_2_), channel_id=1, source_target_pairs={{0,8},{1,9},{8,0},{9,1},{16,24},{17,25},{24,16},{25,17},{2,10},{3,... | collective-permute-start | bytes 2359304 | tf_op jit(solution)/shard_map/ppermute | solution.py:1323
  265.0 29.6 %collective-permute-start.11 = (bf16[192,1024]{1,0:T(8,128)(2,1)}, bf16[192,1024]{1,0:T(8,128)(2,1)S(1)}, u32[]{:S(2)}, u32[]{:S(2)}) collective-permute-start(bf16[192,1024]{1,0:T(8,128)(2,1)} %slice.797), channel_id=1, source_target_pairs={{0,16},{16,17},{17,1},{1,0},{8,24},{24,25},{25,9},{9,8},{2,18},{18... | collective-permute-start | bytes 1179656 | tf_op jit(solution)/shard_map/ppermute | solution.py:1317
  268.2 26.5 %collective-permute-start.13 = (bf16[192,1024]{1,0:T(8,128)(2,1)}, bf16[192,1024]{1,0:T(8,128)(2,1)}, u32[]{:S(2)}, u32[]{:S(2)}) collective-permute-start(bf16[192,1024]{1,0:T(8,128)(2,1)} %slice.798), channel_id=1, source_target_pairs={{16,0},{17,16},{1,17},{0,1},{24,8},{25,24},{9,25},{8,9},{18,2},{19... | collective-permute-start | bytes 1179656 | tf_op jit(solution)/shard_map/ppermute | solution.py:1320
  268.5 28.0 %collective-permute-start.24 = (bf16[384,1024]{1,0:T(8,128)(2,1)}, bf16[384,1024]{1,0:T(8,128)(2,1)}, u32[]{:S(2)}, u32[]{:S(2)}) collective-permute-start(bf16[384,1024]{1,0:T(8,128)(2,1)} %collective-permute-done.10.refs_0_), channel_id=1, source_target_pairs={{0,8},{1,9},{8,0},{9,1},{16,24},{17,25},{24,16},{25,17},{2,10},{3,... | collective-permute-start | bytes 2359304 | tf_op jit(solution)/shard_map/ppermute | solution.py:1323
  271.1 25.4 %collective-permute-start.25 = (bf16[384,1024]{1,0:T(8,128)(2,1)}, bf16[384,1024]{1,0:T(8,128)(2,1)}, u32[]{:S(2)}, u32[]{:S(2)}) collective-permute-start(bf16[384,1024]{1,0:T(8,128)(2,1)} %collective-permute-done.12.refs_1_), channel_id=1, source_target_pairs={{0,8},{1,9},{8,0},{9,1},{16,24},{17,25},{24,16},{25,17},{2,10},{3,... | collective-permute-start | bytes 2359304 | tf_op jit(solution)/shard_map/ppermute | solution.py:1323
  295.7 42.7 %collective-permute-start.14 = (bf16[384,1024]{1,0:T(8,128)(2,1)S(1)}, bf16[384,1024]{1,0:T(8,128)(2,1)S(1)}, u32[]{:S(2)}, u32[]{:S(2)}) collective-permute-start(bf16[384,1024]{1,0:T(8,128)(2,1)S(1)} %constant_dynamic-update-slice_fusion.2.refs_0_), channel_id=1, source_target_pairs={{0,8},{1,9},{8,0},{9,1},{16,24},{17,25},{24,16},{25,17},{2,10},{3,... | collective-permute-start | bytes 2359304 | tf_op jit(solution)/shard_map/ppermute | solution.py:1323
  338.4 31.1 %collective-permute-start.30 = (bf16[2,384,1024]{2,1,0:T(8,128)(2,1)}, bf16[2,384,1024]{2,1,0:T(8,128)(2,1)}, u32[]{:S(2)}, u32[]{:S(2)}) collective-permute-start(bf16[2,384,1024]{2,1,0:T(8,128)(2,1)} %slice.639), channel_id=1, source_target_pairs={{0,8},{1,9},{8,0},{9,1},{16,24},{17,25},{24,16},{25,17},{2,10},{3,... | collective-permute-start | bytes 4718600 | tf_op jit(solution)/shard_map/ppermute | solution.py:1323
  365.5 16.2 %collective-permute-start.27 = (bf16[384,1024]{1,0:T(8,128)(2,1)S(1)}, bf16[384,1024]{1,0:T(8,128)(2,1)S(1)}, u32[]{:S(2)}, u32[]{:S(2)}) collective-permute-start(bf16[384,1024]{1,0:T(8,128)(2,1)S(1)} %slice_bitcast_fusion.9), channel_id=1, source_target_pairs={{0,8},{1,9},{8,0},{9,1},{16,24},{17,25},{24,16},{25,17},{2,10},{3,... | collective-permute-start | bytes 2359304 | tf_op jit(solution)/shard_map/ppermute | solution.py:1323
  367.9 10.4 %collective-permute-start.29 = (bf16[192,1024]{1,0:T(8,128)(2,1)S(1)}, bf16[192,1024]{1,0:T(8,128)(2,1)S(1)}, u32[]{:S(2)}, u32[]{:S(2)}) collective-permute-start(bf16[192,1024]{1,0:T(8,128)(2,1)S(1)} %get-tuple-element.257), channel_id=1, source_target_pairs={{0,16},{16,17},{17,1},{1,0},{8,24},{24,25},{25,9},{9,8},{2,18},{18... | collective-permute-start | bytes 1179656 | tf_op jit(solution)/shard_map/ppermute | solution.py:1317
  379.5 17.6 %collective-permute-start.31 = (bf16[384,1024]{1,0:T(8,128)(2,1)S(1)}, bf16[384,1024]{1,0:T(8,128)(2,1)S(1)}, u32[]{:S(2)}, u32[]{:S(2)}) collective-permute-start(bf16[384,1024]{1,0:T(8,128)(2,1)S(1)} %pad_maximum_fusion.9), channel_id=1, source_target_pairs={{0,16},{16,17},{17,1},{1,0},{8,24},{24,25},{25,9},{9,8},{2,18},{18... | collective-permute-start | bytes 2359304 | tf_op jit(solution)/shard_map/ppermute | solution.py:1317
  380.8 17.3 %collective-permute-start.33 = (bf16[384,1024]{1,0:T(8,128)(2,1)S(1)}, bf16[384,1024]{1,0:T(8,128)(2,1)S(1)}, u32[]{:S(2)}, u32[]{:S(2)}) collective-permute-start(bf16[384,1024]{1,0:T(8,128)(2,1)S(1)} %pad_maximum_fusion.10), channel_id=1, source_target_pairs={{16,0},{17,16},{1,17},{0,1},{24,8},{25,24},{9,25},{8,9},{18,2},{19... | collective-permute-start | bytes 2359304 | tf_op jit(solution)/shard_map/ppermute | solution.py:1320
  433.4 93.1 %all-to-all-start.3 = ((bf16[8,128,1024]{2,1,0:T(8,128)(2,1)}), bf16[8,128,1024]{2,1,0:T(8,128)(2,1)}, u32[]{:S(2)}, u32[]{:S(2)}) async-start(bf16[8,128,1024]{2,1,0:T(8,128)(2,1)} %get-tuple-element.135), calls=%async_computation.3 | async-start | bytes 4194304 | tf_op jit(solution)/shard_map/all_to_all | solution.py:1419
  440.4 273.1 %reduce-scatter.2.cloned.1.call-start = ((), (), s32[]{:S(2)}) async-start(), calls=%async_computation.8 | async-start | bytes 10911744 | tf_op jit(solution)/shard_map/reduce_scatter | solution.py:1718
  454.6 26.8 %collective-permute-start.40 = (bf16[2,384,1024]{2,1,0:T(8,128)(2,1)}, bf16[2,384,1024]{2,1,0:T(8,128)(2,1)}, u32[]{:S(2)}, u32[]{:S(2)}) collective-permute-start(bf16[2,384,1024]{2,1,0:T(8,128)(2,1)} %slice.655), channel_id=1, source_target_pairs={{0,8},{1,9},{8,0},{9,1},{16,24},{17,25},{24,16},{25,17},{2,10},{3,... | collective-permute-start | bytes 4718600 | tf_op jit(solution)/shard_map/ppermute | solution.py:1323
  456.2 22.4 %collective-permute-start.39 = (bf16[384,1024]{1,0:T(8,128)(2,1)}, bf16[384,1024]{1,0:T(8,128)(2,1)}, u32[]{:S(2)}, u32[]{:S(2)}) collective-permute-start(bf16[384,1024]{1,0:T(8,128)(2,1)} %slice_bitcast_fusion.7), channel_id=1, source_target_pairs={{0,8},{1,9},{8,0},{9,1},{16,24},{17,25},{24,16},{25,17},{2,10},{3,... | collective-permute-start | bytes 2359304 | tf_op jit(solution)/shard_map/ppermute | solution.py:1323
  457.4 21.8 %collective-permute-start.41 = (bf16[384,1024]{1,0:T(8,128)(2,1)}, bf16[384,1024]{1,0:T(8,128)(2,1)S(1)}, u32[]{:S(2)}, u32[]{:S(2)}) collective-permute-start(bf16[384,1024]{1,0:T(8,128)(2,1)} %slice_bitcast_fusion.6), channel_id=1, source_target_pairs={{0,8},{1,9},{8,0},{9,1},{16,24},{17,25},{24,16},{25,17},{2,10},{3,... | collective-permute-start | bytes 2359304 | tf_op jit(solution)/shard_map/ppermute | solution.py:1323
  467.9 41.9 %collective-permute-start.34 = (bf16[272,1024]{1,0:T(8,128)(2,1)}, bf16[272,1024]{1,0:T(8,128)(2,1)}, u32[]{:S(2)}, u32[]{:S(2)}) collective-permute-start(bf16[272,1024]{1,0:T(8,128)(2,1)} %get-tuple-element.225), channel_id=1, source_target_pairs={{0,0},{2,16},{4,8},{6,24},{8,2},{10,18},{12,10},{14,26},{16,4},{18... | collective-permute-start | bytes 1671176 | tf_op jit(solution)/shard_map/ppermute | solution.py:1389
  475.6 44.6 %collective-permute-start.35 = (bf16[272,1024]{1,0:T(8,128)(2,1)}, bf16[272,1024]{1,0:T(8,128)(2,1)}, u32[]{:S(2)}, u32[]{:S(2)}) collective-permute-start(bf16[272,1024]{1,0:T(8,128)(2,1)} %get-tuple-element.224), channel_id=1, source_target_pairs={{0,2},{2,18},{4,10},{6,26},{8,0},{10,16},{12,8},{14,24},{16,6},{18... | collective-permute-start | bytes 1671176 | tf_op jit(solution)/shard_map/ppermute | solution.py:1389
  478.7 41.5 %collective-permute-start.36 = (bf16[272,1024]{1,0:T(8,128)(2,1)}, bf16[272,1024]{1,0:T(8,128)(2,1)}, u32[]{:S(2)}, u32[]{:S(2)}) collective-permute-start(bf16[272,1024]{1,0:T(8,128)(2,1)} %get-tuple-element.223), channel_id=1, source_target_pairs={{0,4},{2,20},{4,12},{6,28},{8,6},{10,22},{12,14},{14,30},{16,0},{1... | collective-permute-start | bytes 1671176 | tf_op jit(solution)/shard_map/ppermute | solution.py:1389
  479.2 47.4 %collective-permute-start.37 = (bf16[272,1024]{1,0:T(8,128)(2,1)}, bf16[272,1024]{1,0:T(8,128)(2,1)}, u32[]{:S(2)}, u32[]{:S(2)}) collective-permute-start(bf16[272,1024]{1,0:T(8,128)(2,1)} %get-tuple-element.222), channel_id=1, source_target_pairs={{0,6},{2,22},{4,14},{6,30},{8,4},{10,20},{12,12},{14,28},{16,2},{1... | collective-permute-start | bytes 1671176 | tf_op jit(solution)/shard_map/ppermute | solution.py:1389
  484.1 46.7 %collective-permute-start.42 = (bf16[192,1024]{1,0:T(8,128)(2,1)}, bf16[192,1024]{1,0:T(8,128)(2,1)S(1)}, u32[]{:S(2)}, u32[]{:S(2)}) collective-permute-start(bf16[192,1024]{1,0:T(8,128)(2,1)} %get-tuple-element.256), channel_id=1, source_target_pairs={{0,16},{16,17},{17,1},{1,0},{8,24},{24,25},{25,9},{9,8},{2,18},{18... | collective-permute-start | bytes 1179656 | tf_op jit(solution)/shard_map/ppermute | solution.py:1317
  509.7 25.5 %collective-permute-start.43 = (bf16[192,1024]{1,0:T(8,128)(2,1)}, bf16[192,1024]{1,0:T(8,128)(2,1)}, u32[]{:S(2)}, u32[]{:S(2)}) collective-permute-start(bf16[192,1024]{1,0:T(8,128)(2,1)} %get-tuple-element.255), channel_id=1, source_target_pairs={{16,0},{17,16},{1,17},{0,1},{24,8},{25,24},{9,25},{8,9},{18,2},{19... | collective-permute-start | bytes 1179656 | tf_op jit(solution)/shard_map/ppermute | solution.py:1320
  526.5 22.9 %all-to-all-start.4 = ((bf16[8,384,128]{2,1,0:T(8,128)(2,1)}), bf16[8,384,128]{2,1,0:T(8,128)(2,1)}, u32[]{:S(2)}, u32[]{:S(2)}) async-start(bf16[8,384,128]{2,1,0:T(8,128)(2,1)} %bitcast.323), calls=%async_computation.5 | async-start | bytes 1572864 | tf_op jit(solution)/shard_map/all_to_all | solution.py:1419
  537.9 98.6 %collective-permute-start.45 = (bf16[384,1024]{1,0:T(8,128)(2,1)}, bf16[384,1024]{1,0:T(8,128)(2,1)S(1)}, u32[]{:S(2)}, u32[]{:S(2)}) collective-permute-start(bf16[384,1024]{1,0:T(8,128)(2,1)} %pad_maximum_fusion.12), channel_id=1, source_target_pairs={{16,0},{17,16},{1,17},{0,1},{24,8},{25,24},{9,25},{8,9},{18,2},{19... | collective-permute-start | bytes 2359304 | tf_op jit(solution)/shard_map/ppermute | solution.py:1320
  538.8 98.4 %collective-permute-start.44 = (bf16[384,1024]{1,0:T(8,128)(2,1)}, bf16[384,1024]{1,0:T(8,128)(2,1)S(1)}, u32[]{:S(2)}, u32[]{:S(2)}) collective-permute-start(bf16[384,1024]{1,0:T(8,128)(2,1)} %pad_maximum_fusion.11), channel_id=1, source_target_pairs={{0,16},{16,17},{17,1},{1,0},{8,24},{24,25},{25,9},{9,8},{2,18},{18... | collective-permute-start | bytes 2359304 | tf_op jit(solution)/shard_map/ppermute | solution.py:1317
  611.6 11.4 %collective-permute-start.48 = (bf16[384,1024]{1,0:T(8,128)(2,1)S(1)}, bf16[384,1024]{1,0:T(8,128)(2,1)S(1)}, u32[]{:S(2)}, u32[]{:S(2)}) collective-permute-start(bf16[384,1024]{1,0:T(8,128)(2,1)S(1)} %slice.832), channel_id=1, source_target_pairs={{0,8},{1,9},{8,0},{9,1},{16,24},{17,25},{24,16},{25,17},{2,10},{3,... | collective-permute-start | bytes 2359304 | tf_op jit(solution)/shard_map/ppermute | solution.py:1323
  618.9 32.5 %collective-permute-start.47 = (bf16[384,1024]{1,0:T(8,128)(2,1)S(1)}, bf16[384,1024]{1,0:T(8,128)(2,1)S(1)}, u32[]{:S(2)}, u32[]{:S(2)}) collective-permute-start(bf16[384,1024]{1,0:T(8,128)(2,1)S(1)} %slice.830), channel_id=1, source_target_pairs={{0,8},{1,9},{8,0},{9,1},{16,24},{17,25},{24,16},{25,17},{2,10},{3,... | collective-permute-start | bytes 2359304 | tf_op jit(solution)/shard_map/ppermute | solution.py:1323
  623.5 10.5 %collective-permute-start.52 = (bf16[192,1024]{1,0:T(8,128)(2,1)S(1)}, bf16[192,1024]{1,0:T(8,128)(2,1)S(1)}, u32[]{:S(2)}, u32[]{:S(2)}) collective-permute-start(bf16[192,1024]{1,0:T(8,128)(2,1)S(1)} %get-tuple-element.253), channel_id=1, source_target_pairs={{16,0},{17,16},{1,17},{0,1},{24,8},{25,24},{9,25},{8,9},{18,2},{19... | collective-permute-start | bytes 1179656 | tf_op jit(solution)/shard_map/ppermute | solution.py:1320
  634.3 26.5 %collective-permute-start.51 = (bf16[384,1024]{1,0:T(8,128)(2,1)S(1)}, bf16[384,1024]{1,0:T(8,128)(2,1)S(1)}, u32[]{:S(2)}, u32[]{:S(2)}) collective-permute-start(bf16[384,1024]{1,0:T(8,128)(2,1)S(1)} %pad_maximum_fusion.13), channel_id=1, source_target_pairs={{0,16},{16,17},{17,1},{1,0},{8,24},{24,25},{25,9},{9,8},{2,18},{18... | collective-permute-start | bytes 2359304 | tf_op jit(solution)/shard_map/ppermute | solution.py:1317
  636.4 24.4 %collective-permute-start.53 = (bf16[384,1024]{1,0:T(8,128)(2,1)S(1)}, bf16[384,1024]{1,0:T(8,128)(2,1)S(1)}, u32[]{:S(2)}, u32[]{:S(2)}) collective-permute-start(bf16[384,1024]{1,0:T(8,128)(2,1)S(1)} %pad_maximum_fusion.14), channel_id=1, source_target_pairs={{16,0},{17,16},{1,17},{0,1},{24,8},{25,24},{9,25},{8,9},{18,2},{19... | collective-permute-start | bytes 2359304 | tf_op jit(solution)/shard_map/ppermute | solution.py:1320
  636.5 77.0 %collective-permute-start.38 = (bf16[8,128,1024]{2,1,0:T(8,128)(2,1)}, bf16[8,128,1024]{2,1,0:T(8,128)(2,1)}, u32[]{:S(2)}, u32[]{:S(2)}) collective-permute-start(bf16[8,128,1024]{2,1,0:T(8,128)(2,1)} %all-to-all-done.3), channel_id=1, source_target_pairs={{0,2},{2,18},{4,10},{6,26},{8,6},{10,22},{12,14},{14,30},{16,0},{1... | collective-permute-start | bytes 6291464 | tf_op jit(solution)/shard_map/ppermute | solution.py:1379
  640.9 72.5 %collective-permute-start.46 = (bf16[384,1024]{1,0:T(8,128)(2,1)}, bf16[384,1024]{1,0:T(8,128)(2,1)}, u32[]{:S(2)}, u32[]{:S(2)}) collective-permute-start(bf16[384,1024]{1,0:T(8,128)(2,1)} %fusion.18), channel_id=1, source_target_pairs={{0,0},{2,16},{4,8},{6,24},{8,4},{10,20},{12,12},{14,28},{16,2},{18... | collective-permute-start | bytes 2359304 | tf_op jit(solution)/shard_map/ppermute | solution.py:1371
  663.7 37.4 %all-to-all-start.5 = ((f32[8,2,128]{2,1,0:T(2,128)}), f32[8,2,128]{2,1,0:T(2,128)S(1)}, u32[]{:S(2)}, u32[]{:S(2)}) async-start(f32[8,2,128]{2,1,0:T(2,128)} %copy.155), calls=%async_computation.6 | async-start | bytes 16384 | tf_op jit(solution)/shard_map/all_to_all | solution.py:1419
  701.1 11.8 %collective-permute-start.55 = (f32[2,128]{1,0:T(2,128)S(1)}, f32[2,128]{1,0:T(2,128)S(1)}, u32[]{:S(2)}, u32[]{:S(2)}) collective-permute-start(f32[2,128]{1,0:T(2,128)S(1)} %reduce_sum.265), channel_id=1, source_target_pairs={{0,0},{2,16},{4,8},{6,24},{8,4},{10,20},{12,12},{14,28},{16,2},{18... | collective-permute-start | bytes 3080 | tf_op jit(solution)/shard_map/ppermute | solution.py:1371
  725.2 26.8 %all-to-all-start.6 = ((bf16[8,128,640]{2,1,0:T(8,128)(2,1)}), bf16[8,128,640]{2,1,0:T(8,128)(2,1)}, u32[]{:S(2)}, u32[]{:S(2)}) async-start(bf16[8,128,640]{2,1,0:T(8,128)(2,1)} %bitcast.135), calls=%async_computation.7 | async-start | bytes 2621440 | tf_op jit(solution)/shard_map/all_to_all | solution.py:1419
  730.8 72.5 %collective-permute-start.54 = (bf16[848,1024]{1,0:T(8,128)(2,1)}, bf16[848,1024]{1,0:T(8,128)(2,1)S(1)}, u32[]{:S(2)}, u32[]{:S(2)}) collective-permute-start(bf16[848,1024]{1,0:T(8,128)(2,1)} %pad_maximum_fusion.3), channel_id=1, source_target_pairs={{0,0},{2,16},{4,8},{6,24},{8,4},{10,20},{12,12},{14,28},{16,2},{18... | collective-permute-start | bytes 5210120 | tf_op jit(solution)/shard_map/ppermute | solution.py:1371
  752.0 55.4 %collective-permute-start.56 = (bf16[8,128,640]{2,1,0:T(8,128)(2,1)}, bf16[8,128,640]{2,1,0:T(8,128)(2,1)}, u32[]{:S(2)}, u32[]{:S(2)}) collective-permute-start(bf16[8,128,640]{2,1,0:T(8,128)(2,1)} %all-to-all-done.6), channel_id=1, source_target_pairs={{0,2},{2,18},{4,10},{6,26},{8,6},{10,22},{12,14},{14,30},{16,0},{1... | collective-permute-start | bytes 3932168 | tf_op jit(solution)/shard_map/ppermute | solution.py:1379
  752.1 50.7 %collective-permute-start.57 = (f32[3,128]{1,0:T(4,128)S(1)}, f32[3,128]{1,0:T(4,128)S(1)}, u32[]{:S(2)}, u32[]{:S(2)}) collective-permute-start(f32[3,128]{1,0:T(4,128)S(1)} %pad_maximum_fusion.20), channel_id=1, source_target_pairs={{0,0},{1,1},{2,16},{3,17},{4,8},{5,9},{6,24},{7,25},{8,2},{9,3},{1... | collective-permute-start | bytes 4616 | tf_op jit(solution)/shard_map/ppermute | solution.py:1405
  (95 other events, 1228.3 us)
Sparse Core Ops, SparseCore 0:
  63.9 123.7 all-gather.4
  189.9 82.6 all-gather.6
  464.8 116.9 reduce-scatter.1
where the time goes:
time: 830 us; the launch traced here: 817 us
  Pallas kernels  241 us (29%)
  waiting for transfers between devices  240 us (29%)
  starting transfers between devices  125 us (15%)
  local copies, waits for them, and re-layouts  106 us (13%)
  other arithmetic  53.8 us (6%)
  matrix products  35.8 us (4%)
  between operations  15.9 us (2%)
    pallas_call x3, Pallas kernels, feed(): pl.pallas_call(functools.partial(feed_kernel, count, first, last), grid_s...  83.5 us
    all_to_all x7, waiting for transfers between devices, exchange(): return lax.all_to_all(values, axes, split_axis=0, concat_axis=0, tiled=True)  66.9 us
    pallas_call x1, Pallas kernels, self_backward(): pl.pallas_call(functools.partial(self_backward_kernel, prompt_all), out_s...  59.9 us
    ppermute x12, waiting for transfers between devices, up(): return lax.ppermute(values, ROLE_AXES, self.forward)  57.8 us
    pallas_call x1, Pallas kernels, self_forward(): pl.pallas_call(functools.partial(self_forward_kernel, prompt_all), out_sh...  44 us
    ppermute x1, waiting for transfers between devices, leave_own(): return lax.ppermute(values, ALL_AXES, moves)  39.9 us
    ppermute x4, waiting for transfers between devices, leave_quarters(): result.append(lax.ppermute(piece, (GRP, BLK), moves))  36 us
    all_to_all x7, starting transfers between devices, exchange(): return lax.all_to_all(values, axes, split_axis=0, concat_axis=0, tiled=True)  35.3 us
  transfers between devices with their start and end apart: 68, of which 22 were waited for; matrix products, arithmetic and copies ran while one was open for 18% of the time, Pallas kernels for 27%

commit v1 on v0

--- a/solution.py
+++ b/solution.py
@@ -1017,39 +1017,14 @@
     )(*chunks, gain[None], shift[None], weight, bias[None])
 
 
-def feed_kernel(count, first, last, info_ref, *refs):
-    chunks, refs = refs[:count], refs[count:]
-    upstreams, refs = refs[:count], refs[count:]
-    weights_ref, bias_ref = refs[:2]
-    refs = refs[2:]
-    if not first:
-        up_before, down_before, sum_before = refs[:3]
-        refs = refs[3:]
-    out_ref, dnormed_ref, up_after, down_after, sum_after = refs[:5]
-    chunk, upstream_chunk, up_sum, down_sum, bias_sum, sems = refs[5:]
-    at = pl.program_id(0)
-
-    def carried():
-        return (
-            pltpu.make_async_copy(up_before, up_sum, sems.at[0]),
-            pltpu.make_async_copy(down_before, down_sum, sems.at[1]),
-        )
-
-    @pl.when(at == 0)
-    def begin():
-        if first:
-            up_sum[...] = jnp.zeros_like(up_sum)
-            down_sum[...] = jnp.zeros_like(down_sum)
-            bias_sum[...] = jnp.zeros_like(bias_sum)
-        else:
-            for copy in carried():
-                copy.start()
-            bias_sum[...] = sum_before[...]
-
-    pick(chunks, chunk)
-    pick(upstreams, upstream_chunk)
-    feed = chunk[...]
-    upstream = upstream_chunk[...]
+def feed_kernel(count, *refs):
+    chunks, upstreams = refs[:count], refs[count : 2 * count]
+    weights_ref, bias_ref = refs[2 * count : 2 * count + 2]
+    sums_ref, feed_ref, upstream_ref, active_ref, dhidden_ref = refs[2 * count + 2 :]
+    pick(chunks, feed_ref.at[0])
+    pick(upstreams, upstream_ref.at[0])
+    feed = feed_ref[0]
+    upstream = upstream_ref[0]
     blocks, both, width = weights_ref.shape
     step = both // 2
     out = None
@@ -1062,88 +1037,34 @@
         active = (hidden * tail).astype(jnp.bfloat16)
         slope = tail + hidden * jnp.exp(-0.5 * hidden * hidden) * (1.0 / math.sqrt(2.0 * math.pi))
         dhidden = (dot(upstream, down, NT) * slope).astype(jnp.bfloat16)
-        if low == 0 and not first:
-
-            @pl.when(at == 0)
-            def arrive():
-                for copy in carried():
-                    copy.wait()
-
-        bias_sum[0:1, where] += jnp.sum(dhidden.astype(jnp.float32), axis=0, keepdims=True)
-        up_sum[:, where] += dot(feed, dhidden, TN)
-        down_sum[where] += dot(active, upstream, TN)
+        active_ref[0, :, where] = active
+        dhidden_ref[0, :, where] = dhidden
         term, dterm = dot(active, down), dot(dhidden, up, NT)
         out, dnormed = (term, dterm) if out is None else (out + term, dnormed + dterm)
-    out_ref[0] = out.astype(jnp.bfloat16)
-    dnormed_ref[0] = dnormed.astype(jnp.bfloat16)
-
-    @pl.when(at == count - 1)
-    def end():
-        sum_after[...] = bias_sum[...]
-        if last:
-            rows = up_sum.shape[0] // 8
-            for role in range(8):
-                line = 2 * COLUMN_OF[role // 2] + role % 2
-                where = slice(line * rows, (line + 1) * rows)
-                up_after[role] = up_sum[where].astype(jnp.bfloat16)
-            quarter = info_ref[0]
-            for block in range(4):
-                where = slice(block * step, (block + 1) * step)
-                slot = block ^ quarter
-                down_after[slot, :step] = down_sum[where].astype(jnp.bfloat16)
-                down_after[slot, step:, :step] = jnp.broadcast_to(
-                    bias_sum[0:1, where], (16, step)
-                ).astype(jnp.bfloat16)
-        else:
-            pltpu.sync_copy(up_sum, up_after)
-            pltpu.sync_copy(down_sum, down_after)
-
-
-def feed(chunks, upstreams, info, weights, bias, before, last):
+    rows = feed.shape[0]
+    sums_ref[0, :rows] = dnormed.astype(jnp.bfloat16)
+    sums_ref[0, rows:] = out.astype(jnp.bfloat16)
+
+
+def feed(chunks, upstreams, weights, bias):
     count = len(chunks)
     rows, width = chunks[0].shape
     columns = bias.shape[0]
-    first = before is None
-    anywhere = pl.BlockSpec(memory_space=pl.ANY)
-
-    sums = jax.ShapeDtypeStruct((8, columns), jnp.float32)
-    out_shape = [
-        jax.ShapeDtypeStruct((count, rows, width), jnp.bfloat16),
-        jax.ShapeDtypeStruct((count, rows, width), jnp.bfloat16),
-    ]
-    if last:
-        shapes = ((8, width // 8, columns), (4, columns // 4 + 16, width))
-        out_shape += [jax.ShapeDtypeStruct(shape, jnp.bfloat16) for shape in shapes]
-        sum_specs = [fixed(shape) for shape in shapes]
-    else:
-        shapes = ((width, columns), (columns, width))
-        out_shape += [jax.ShapeDtypeStruct(shape, jnp.float32) for shape in shapes]
-        sum_specs = [anywhere, anywhere]
-    extra = [] if first else [anywhere, anywhere, fixed((8, columns))]
-    carried = () if first else before
     return pl.pallas_call(
-        functools.partial(feed_kernel, count, first, last),
-        grid_spec=pltpu.PrefetchScalarGridSpec(
-            num_scalar_prefetch=1,
-            grid=(count,),
-            in_specs=[fixed((rows, width))] * (2 * count)
-            + [fixed(weights.shape), fixed((1, columns))]
-            + extra,
-            out_specs=[stepped((rows, width)), stepped((rows, width))] + sum_specs + [fixed((8, columns))],
-            scratch_shapes=[
-                pltpu.VMEM((rows, width), jnp.bfloat16),
-                pltpu.VMEM((rows, width), jnp.bfloat16),
-                pltpu.VMEM((width, columns), jnp.float32),
-                pltpu.VMEM((columns, width), jnp.float32),
-                pltpu.VMEM((8, columns), jnp.float32),
-                pltpu.SemaphoreType.DMA((2,)),
-            ],
-        ),
-        out_shape=out_shape + [sums],
+        functools.partial(feed_kernel, count),
+        grid=(count,),
+        in_specs=[fixed((rows, width))] * (2 * count)
+        + [fixed(weights.shape), fixed((1, columns))],
+        out_specs=[stepped((2 * rows, width))]
+        + [stepped((rows, width))] * 2
+        + [stepped((rows, columns))] * 2,
+        out_shape=[jax.ShapeDtypeStruct((count, 2 * rows, width), jnp.bfloat16)]
+        + [jax.ShapeDtypeStruct((count, rows, width), jnp.bfloat16)] * 2
+        + [jax.ShapeDtypeStruct((count, rows, columns), jnp.bfloat16)] * 2,
         compiler_params=pltpu.CompilerParams(vmem_limit_bytes=VMEM_BYTES),
-        cost_estimate=cost(10.5 * count),
+        cost_estimate=cost(6.5 * count),
         name="feed",
-    )(info, *chunks, *upstreams, weights, bias[None], *carried)
+    )(*chunks, *upstreams, weights, bias[None])
 
 
 def cross_forward_kernel(probe_ref, lookup_ref, content_ref, out_ref, lse_ref):
@@ -1344,7 +1265,7 @@
         sent = (self.up(last[:half].astype(low)), self.down(last[half:].astype(low)))
         if gates[1] is not None:
             sent = after(sent, gates[1])
-        left, right = sent
+        self.mark = left, right = sent
         pair = after_parts[0:2].astype(wide) + swaps[1]
         behind, ahead = pair[0], pair[1]
         left = jnp.concatenate([left + ahead[:half], ahead[half:]], axis=0).astype(low)
@@ -1640,23 +1561,38 @@
     second_unit, second_rate = norm_parts(second)
     normed_feed = (second_unit * feed_gain_full + feed_shift_full).astype(low)
 
-    before, dnormed_parts, output_parts = None, [], []
-    feed_groups = slab.gather(normed_feed)
-    info = quarter[None].astype(jnp.int32)
-    for group, upstream_group in zip(feed_groups, upstream_groups):
-        last = group is feed_groups[-1]
-        output, dnormed, *before = feed(
-            group, upstream_group, info, feed_weights, up_bias_own, before, last
-        )
-        dnormed_parts.append(dnormed)
-        output_parts.append(output)
-    up_gradient, down_gradient, unused = before
-    dnormed_feed = slab.scatter(*dnormed_parts)
-    up_gradient, down_gradient, output_parts = after(
-        (up_gradient, down_gradient, output_parts), dnormed_feed
-    )
+    fed = [
+        feed(group, upstream_group, feed_weights, up_bias_own)
+        for group, upstream_group in zip(slab.gather(normed_feed), upstream_groups)
+    ]
+    dnormed_feed = slab.scatter(*[parts[0] for parts in fed])
+    output = second + dnormed_feed[local_rows:] + down_bias_full
+    dnormed_feed = dnormed_feed[:local_rows]
+
+    kept = after([parts[1:] for parts in fed], slab.mark)
+
+    def summed(left, right):
+        return sum(
+            left_product(parts[left].reshape(-1, width), parts[right].reshape(-1, width))
+            for parts in kept
+        ).astype(low)
+
+    down_gradient = summed(2, 1).reshape(4, 2 * shard, width)
+    up_sum = sum(column_sum(parts[3].reshape(-1, width)) for parts in kept).astype(low)
+    up_sum = jnp.broadcast_to(
+        jnp.pad(up_sum.reshape(4, 1, 2 * shard), ((0, 0), (0, 0), (0, width - 2 * shard))),
+        (4, 16, width),
+    )
+    down_gradient = jnp.concatenate([down_gradient, up_sum], axis=1)
+    down_gradient = after(down_gradient, dnormed_feed)
+    down_gradient = slab.leave_quarters(
+        [
+            lax.dynamic_index_in_dim(down_gradient, quarter ^ at, 0, keepdims=False)
+            for at in range(4)
+        ]
+    )
+    up_gradient = after(by_role(summed(0, 3), COLUMN_OF), dnormed_feed)
     up_gradient = exchange(up_gradient, ROLE_AXES)
-    down_gradient = slab.leave_quarters([down_gradient[at] for at in range(4)])
 
     part, feed_gain_sum, feed_shift_sum = norm_backward(
         dnormed_feed, second_unit, second_rate, feed_gain_full
@@ -1674,7 +1610,7 @@
         lookup_full,
         content_full,
     )
-    dnormed_cross = right_product(dprobes, probe_full)
+    dnormed_cross = right_product(after(dprobes, (up_gradient, down_gradient)), probe_full)
     part, cross_gain_sum, cross_shift_sum = norm_backward(
         dnormed_cross, first_unit, first_rate, cross_gain_full
     )
@@ -1682,13 +1618,8 @@
     dfirst_low = dfirst.astype(low)
     dmixed = right_product(dfirst_low, output_full).astype(low)
     dmixed = dmixed.reshape(local_rows, 8, shard).transpose(1, 0, 2)
-    output = slab.scatter(*output_parts, (drecalled, dprobes, dmixed))
-    output = slab.leave((second + output + down_bias_full).astype(low))
-    up_gradient, down_gradient, dmixed = lax.optimization_barrier(
-        (up_gradient, down_gradient, dmixed)
-    )
     dmixed = exchange(dmixed, ROLE_AXES)
-    up_gradient = slab.leave_columns(up_gradient)
+    up_gradient = slab.leave_columns(after(up_gradient, dmixed))
 
     sums = jnp.stack(
         (
@@ -1721,6 +1652,7 @@
         slab.lines, bounds, head_groups, dmixed, attended, logsum, prompt_all
     )
     done = dhead_groups[0]
+    output = slab.leave(after(output.astype(low), done))
 
     dnormed = slab.scatter(
         *[
@@ -1731,8 +1663,8 @@
         ]
     )
 
-    up_gradient, down_gradient, output, scattered = after(
-        (up_gradient, down_gradient, output, scattered), done
+    up_gradient, down_gradient, scattered = after(
+        (up_gradient, down_gradient, scattered), done
     )
     up_weight_gradient = settle_columns(up_gradient)
     down_weight_gradient = slab.settle(
@@ -1791,7 +1723,8 @@
         down_bias_gradient,
     ) = [small_sums[at] for at in range(8)]
 
-    sums = by_role(jnp.stack((self_gain_sum, self_shift_sum), axis=1))
+    sums = after(jnp.stack((self_gain_sum, self_shift_sum), axis=1), head_gradient)
+    sums = by_role(sums)
     sums = jnp.sum(exchange(sums.transpose(0, 2, 1), ROLE_AXES), axis=0)
     sums = slab.leave(sums)
     up_bias_gradient = up_bias_gradient.reshape(-1)

time: 830 us -> 792 us (0.954)
  Pallas kernels: 241 us -> 202 us
  waiting for transfers between devices: 240 us -> 215 us
  matrix products: 35.8 us -> 51.7 us
    ppermute x1, waiting for transfers between devices: 39.9 us -> 0.01 us  [leave_own(): return lax.ppermute(values, ALL_AXES, moves)]
    ppermute x12 -> x10, waiting for transfers between devices: 6.63 us -> 46 us  [down(): return lax.ppermute(values, ROLE_AXES, self.reverse)]
    pallas_call x3, Pallas kernels: 83.5 us -> 47.6 us  [feed(): pl.pallas_call(functools.partial(feed_kernel, count), grid=(count,), in_s...]
    ppermute x4, waiting for transfers between devices: 36 us -> 20.4 us  [leave_quarters(): result.append(lax.ppermute(piece, (GRP, BLK), moves))]
    dot_general x8 -> x14, matrix products: 13 us -> 28.5 us  [left_product(): jnp.einsum('rd,re->de', left, right, preferred_element_type=jnp.float32)]
    unnamed x217 -> x191, local copies, waits for them, and re-layouts: 34.6 us -> 48.7 us
    ppermute x12 -> x10, waiting for transfers between devices: 57.8 us -> 45.8 us  [up(): return lax.ppermute(values, ROLE_AXES, self.forward)]
    ppermute x21 -> x18, starting transfers between devices: 19.6 us -> 14.1 us  [swap(): return lax.ppermute(values, ROLE_AXES, self.cores)]
  transfers between devices with their start and end apart: 68 -> 61, of which waited for: 22 -> 20; matrix products, arithmetic and copies ran while one was open for 18% -> 20% of each run, Pallas kernels for 27% -> 26%
where the time goes in v1:
time: 792 us; the launch traced here: 777 us
  waiting for transfers between devices  215 us (27%)
  Pallas kernels  202 us (26%)
  starting transfers between devices  132 us (17%)
  local copies, waits for them, and re-layouts  113 us (14%)
  matrix products  51.7 us (7%)
  other arithmetic  47.1 us (6%)
  between operations  16.1 us (2%)
    all_to_all x7, waiting for transfers between devices, exchange(): return lax.all_to_all(values, axes, split_axis=0, concat_axis=0, tiled=True)  62.9 us
    pallas_call x1, Pallas kernels, self_backward(): pl.pallas_call(functools.partial(self_backward_kernel, prompt_all), out_s...  58.4 us
    unnamed x191, local copies, waits for them, and re-layouts  48.7 us
    pallas_call x3, Pallas kernels, feed(): pl.pallas_call(functools.partial(feed_kernel, count), grid=(count,), in_s...  47.6 us
    ppermute x10, waiting for transfers between devices, down(): return lax.ppermute(values, ROLE_AXES, self.reverse)  46 us
    ppermute x10, waiting for transfers between devices, up(): return lax.ppermute(values, ROLE_AXES, self.forward)  45.8 us
    pallas_call x1, Pallas kernels, self_forward(): pl.pallas_call(functools.partial(self_forward_kernel, prompt_all), out_sh...  42.4 us
    all_to_all x7, starting transfers between devices, exchange(): return lax.all_to_all(values, axes, split_axis=0, concat_axis=0, tiled=True)  40.2 us
  transfers between devices with their start and end apart: 61, of which 20 were waited for; matrix products, arithmetic and copies ran while one was open for 20% of the time, Pallas kernels for 26%

profile of v1, /device:TPU:1, one launch (start us, length us, event | category | flops | bytes accessed | tf_op | source)
XLA Modules:
  0.0 776.9 jit_solution(5086132348438019476)
XLA Ops:
  26.5 6.4 all-to-all-start
  33.9 5.3 collective-permute-start
  43.5 30.7 %collective-permute-done.refs_0_ = bf16[448,1024]{1,0:T(8,128)(2,1)S(1)} collective-permute-done((bf16[448,1024]{1,0:T(8,128)(2,1)}, bf16[448,1024]{1,0:T(8,128)(2,1)S(1)}, u32[]{:S(2)}, u32[]{:S(2)}) %collective-permute-start) | collective-permute-done | bytes 917536 | tf_op jit(solution)/shard_map/ppermute | solution.py:1284
  76.3 4.1 copy.169
  85.7 6.2 collective-permute-start.3
  93.6 3.5 all-to-all-start.2
  99.8 6.1 collective-permute-start.11
  106.1 16.0 %all-to-all-done.2 = bf16[2,128,1024]{1,2,0:T(8,128)(2,1)S(1)} async-done(((bf16[2,128,1024]{1,2,0:T(8,128)(2,1)}), bf16[2,128,1024]{1,2,0:T(8,128)(2,1)S(1)}, u32[]{:S(2)}, u32[]{:S(2)}) %all-to-all-start.2) | async-done | bytes 524320 | tf_op jit(solution)/shard_map/all_to_all | solution.py:1340
  124.6 3.1 collective-permute-start.7
  129.1 3.0 collective-permute-start.5
  135.0 4.4 project.3
  139.3 8.1 %collective-permute-done.7 = bf16[224,1024]{1,0:T(8,128)(2,1)S(1)} collective-permute-done((bf16[224,1024]{1,0:T(8,128)(2,1)S(1)}, bf16[224,1024]{1,0:T(8,128)(2,1)S(1)}, u32[]{:S(2)}, u32[]{:S(2)}) %collective-permute-start.7) | collective-permute-done | bytes 458784 | tf_op jit(solution)/shard_map/ppermute | solution.py:1238
  150.5 7.3 project.4
  158.7 4.4 project.5
  163.1 42.4 %self_forward.1 = (f32[3072,128]{1,0:T(8,128)}, bf16[8,384,128]{2,1,0:T(8,128)(2,1)}, f32[12,2,256]{2,1,0:T(2,128)}) custom-call(s32[8]{0:T(128)} %stack.105.lines_ref, s32[2]{0:T(128)} %bitcast.436, bf16[2,384,384]{2,1,0:T(8,128)(2,1)} %get-tuple-element.105.near_ref, bf16[4,384,384]{2,1,0:T(8,128)(2,1)} %get-tuple-element.106.next_ref, ...), custom_call_target="tpu_custom_call" | custom-call | flops 39600001024 | bytes 88000000 | tf_op jit(solution)/shard_map/self_forward/pallas_call | solution.py:941
  205.6 5.3 all-to-all-start.1
  215.4 7.3 all-to-all-done.1
  223.9 4.9 fusion.39
  230.3 2.7 convolution_convert_fusion.6.lookup_ref
  237.3 9.7 %cross_forward.1 = (f32[384,1024]{1,0:T(8,128)}, f32[8,2,384]{2,1,0:T(2,128)}) custom-call(bf16[384,1024]{1,0:T(8,128)(2,1)} %add_convert_fusion.3.probe_ref, bf16[512,1024]{1,0:T(8,128)(2,1)} %convolution_convert_fusion.6.lookup_ref, bf16[512,1024]{1,0:T(8,128)(2,1)} %add_convert_fusion.content_ref), custom_call_target="tpu_custom_call" | custom-call | flops 8999999488 | bytes 20000000 | tf_op jit(solution)/shard_map/cross_forward/pallas_call | solution.py:1147
  255.5 13.5 %collective-permute-done.16.refs_0_ = bf16[384,1024]{1,0:T(8,128)(2,1)S(1)} collective-permute-done((bf16[384,1024]{1,0:T(8,128)(2,1)S(1)}, bf16[384,1024]{1,0:T(8,128)(2,1)S(1)}, u32[]{:S(2)}, u32[]{:S(2)}) %collective-permute-start.16) | collective-permute-done | bytes 786464 | tf_op jit(solution)/shard_map/ppermute | solution.py:1238
  271.1 6.4 collective-permute-done.21
  279.3 3.5 collective-permute-start.25
  282.8 3.1 collective-permute-done.17
  292.2 12.7 %feed.4 = (bf16[2,768,1024]{2,1,0:T(8,128)(2,1)}, bf16[2,384,1024]{2,1,0:T(8,128)(2,1)}, bf16[2,384,1024]{2,1,0:T(8,128)(2,1)}, bf16[2,384,1024]{2,1,0:T(8,128)(2,1)}, bf16[2,384,1024]{2,1,0:T(8,128)(2,1)}) custom-call(bf16[384,1024]{1,0:T(8,128)(2,1)} %constant_dynamic-update-slice_fusion.2.refs_0_, bf16[384,1024]{1,0:T(8,128)(2,1)} %collective-permute-done.20.refs_1_, ...), custom_call_target="tpu_custom_call" | custom-call | flops 11699999744 | bytes 26000000 | tf_op jit(solution)/shard_map/feed/pallas_call | solution.py:1053
  305.0 2.7 slice_bitcast_fusion.2
  308.6 12.8 %feed.3 = (bf16[2,768,1024]{2,1,0:T(8,128)(2,1)}, bf16[2,384,1024]{2,1,0:T(8,128)(2,1)}, bf16[2,384,1024]{2,1,0:T(8,128)(2,1)}, bf16[2,384,1024]{2,1,0:T(8,128)(2,1)}, bf16[2,384,1024]{2,1,0:T(8,128)(2,1)}) custom-call(bf16[384,1024]{1,0:T(8,128)(2,1)} %copy-done.39, bf16[384,1024]{1,0:T(8,128)(2,1)} %collective-permute-done.10.refs_1_, ...), custom_call_target="tpu_custom_call" | custom-call | flops 11699999744 | bytes 26000000 | tf_op jit(solution)/shard_map/feed/pallas_call | solution.py:1053
  321.3 2.8 slice_bitcast_fusion.3
  329.8 22.1 %feed.5 = (bf16[4,768,1024]{2,1,0:T(8,128)(2,1)}, bf16[4,384,1024]{2,1,0:T(8,128)(2,1)}, bf16[4,384,1024]{2,1,0:T(8,128)(2,1)}, bf16[4,384,1024]{2,1,0:T(8,128)(2,1)}, bf16[4,384,1024]{2,1,0:T(8,128)(2,1)}) custom-call(bf16[384,1024]{1,0:T(8,128)(2,1)} %copy-done.47, bf16[384,1024]{1,0:T(8,128)(2,1)} %copy-done.48, bf16[384,1024]{1,0:T(8,128)(2,1)} %copy-done.62, ...), custom_call_target="tpu_custom_call" | custom-call | flops 23399999488 | bytes 52000000 | tf_op jit(solution)/shard_map/feed/pallas_call | solution.py:1053
  351.9 4.0 slice.599
  360.0 3.9 fusion.56
  363.9 3.6 fusion.57
  371.1 5.4 fusion.55
  376.5 3.5 fusion.38
  390.0 28.2 %collective-permute-done.33 = bf16[768,1024]{1,0:T(8,128)(2,1)S(1)} collective-permute-done((bf16[768,1024]{1,0:T(8,128)(2,1)S(1)}, bf16[768,1024]{1,0:T(8,128)(2,1)S(1)}, u32[]{:S(2)}, u32[]{:S(2)}) %collective-permute-start.33) | collective-permute-done | bytes 1572896 | tf_op jit(solution)/shard_map/ppermute | solution.py:1241
  418.2 2.8 fusion.4
  421.7 3.0 convert_reduce_fusion.6
  426.7 2.6 convolution_convert_fusion.3
  429.3 5.3 all-to-all-start.3
  434.8 2.9 dynamic-slice_bitcast_fusion
  437.6 4.8 collective-permute-start.34
  448.3 20.5 %cross_backward.1 = (bf16[384,1024]{1,0:T(8,128)(2,1)}, bf16[8,128,1024]{2,1,0:T(8,128)(2,1)}, bf16[512,1024]{1,0:T(8,128)(2,1)}) custom-call(bf16[384,1024]{1,0:T(8,128)(2,1)} %add_convert_fusion.3.probe_ref, bf16[512,1024]{1,0:T(8,128)(2,1)} %convolution_convert_fusion.6.lookup_ref, bf16[512,1024]{1,0:T(8,128)(2,1)} %add_convert_fusion.content_ref, ...), custom_call_target="tpu_custom_call" | custom-call | flops 17999998976 | bytes 40000000 | tf_op jit(solution)/shard_map/cross_backward/pallas_call | solution.py:1166
  476.3 5.4 collective-permute-done.34
  481.6 11.9 %collective-permute-done.35 = bf16[272,1024]{1,0:T(8,128)(2,1)} collective-permute-done((bf16[272,1024]{1,0:T(8,128)(2,1)}, bf16[272,1024]{1,0:T(8,128)(2,1)}, u32[]{:S(2)}, u32[]{:S(2)}) %collective-permute-start.35) | collective-permute-done | bytes 557088 | tf_op jit(solution)/shard_map/ppermute | solution.py:1310
  493.5 3.1 collective-permute-done.37
  496.7 3.0 multiply_reduce_fusion.1
  509.4 2.6 convolution_convert_fusion.7
  513.5 3.8 all-to-all-start.4
  517.8 10.6 %all-to-all-done.4.grad_ref = bf16[8,384,128]{2,1,0:T(8,128)(2,1)S(1)} async-done(((bf16[8,384,128]{2,1,0:T(8,128)(2,1)}), bf16[8,384,128]{2,1,0:T(8,128)(2,1)S(1)}, u32[]{:S(2)}, u32[]{:S(2)}) %all-to-all-start.4) | async-done | bytes 786464 | tf_op jit(solution)/shard_map/all_to_all | solution.py:1340
  529.3 58.4 %self_backward.1 = (bf16[2,384,384]{2,1,0:T(8,128)(2,1)}, bf16[4,384,384]{2,1,0:T(8,128)(2,1)}, bf16[2,384,384]{2,1,0:T(8,128)(2,1)}) custom-call(s32[8]{0:T(128)} %stack.105.lines_ref, s32[2]{0:T(128)} %bitcast.437, bf16[2,384,384]{2,1,0:T(8,128)(2,1)} %get-tuple-element.105.near_ref, bf16[4,384,384]{2,1,0:T(8,128)(2,1)} %get-tuple-element.106.next_ref, ...), custom_call_target="tpu_custom_call" | custom-call | flops 54000001024 | bytes 120000000 | tf_op jit(solution)/shard_map/self_backward/pallas_call | solution.py:961
  587.7 6.8 collective-permute-start.38
  594.5 3.1 convolution_convert_fusion
  608.7 14.4 %collective-permute-done.41 = bf16[192,1024]{1,0:T(8,128)(2,1)S(1)} collective-permute-done((bf16[192,1024]{1,0:T(8,128)(2,1)S(1)}, bf16[192,1024]{1,0:T(8,128)(2,1)S(1)}, u32[]{:S(2)}, u32[]{:S(2)}) %collective-permute-start.41) | collective-permute-done | bytes 393248 | tf_op jit(solution)/shard_map/ppermute | solution.py:1238
  630.1 17.7 %collective-permute-done.45 = bf16[384,1024]{1,0:T(8,128)(2,1)S(1)} collective-permute-done((bf16[384,1024]{1,0:T(8,128)(2,1)S(1)}, bf16[384,1024]{1,0:T(8,128)(2,1)S(1)}, u32[]{:S(2)}, u32[]{:S(2)}) %collective-permute-start.45) | collective-permute-done | bytes 786464 | tf_op jit(solution)/shard_map/ppermute | solution.py:1241
  649.9 7.6 collective-permute-done.46.pieces_ref
  660.1 8.2 %collective-permute-start.47 = (bf16[848,1024]{1,0:T(8,128)(2,1)S(1)}, bf16[848,1024]{1,0:T(8,128)(2,1)S(1)}, u32[]{:S(2)}, u32[]{:S(2)}) collective-permute-start(bf16[848,1024]{1,0:T(8,128)(2,1)S(1)} %pad_maximum_fusion.5), channel_id=1, source_target_pairs={{0,0},{2,16},{4,8},{6,24},{8,4},{10,20},{12,12},{14,28},{16,2},{18... | collective-permute-start | bytes 5210120 | tf_op jit(solution)/shard_map/ppermute | solution.py:1292
  680.2 7.5 all-to-all-start.5
  703.0 3.9 settle_columns.1
  706.9 14.2 %all-to-all-done.5 = bf16[8,128,640]{2,1,0:T(8,128)(2,1)} async-done(((bf16[8,128,640]{2,1,0:T(8,128)(2,1)}), bf16[8,128,640]{2,1,0:T(8,128)(2,1)}, u32[]{:S(2)}, u32[]{:S(2)}) %all-to-all-start.5) | async-done | bytes 1310752 | tf_op jit(solution)/shard_map/all_to_all | solution.py:1340
  721.0 3.1 collective-permute-start.49
  724.8 8.5 %all-to-all-start.6 = ((f32[8,2,128]{2,1,0:T(2,128)}), f32[8,2,128]{2,1,0:T(2,128)S(1)}, u32[]{:S(2)}, u32[]{:S(2)}) async-start(f32[8,2,128]{2,1,0:T(2,128)} %copy.193), calls=%async_computation.7 | async-start | bytes 16384 | tf_op jit(solution)/shard_map/all_to_all | solution.py:1340
  734.7 14.9 %all-to-all-done.6 = f32[8,2,128]{2,1,0:T(2,128)S(1)} async-done(((f32[8,2,128]{2,1,0:T(2,128)}), f32[8,2,128]{2,1,0:T(2,128)S(1)}, u32[]{:S(2)}, u32[]{:S(2)}) %all-to-all-start.6) | async-done | bytes 8224 | tf_op jit(solution)/shard_map/all_to_all | solution.py:1340
  749.6 11.3 %collective-permute-start.48 = (f32[2,128]{1,0:T(2,128)S(1)}, f32[2,128]{1,0:T(2,128)S(1)}, u32[]{:S(2)}, u32[]{:S(2)}) collective-permute-start(f32[2,128]{1,0:T(2,128)S(1)} %reduce_sum.295), channel_id=1, source_target_pairs={{0,0},{2,16},{4,8},{6,24},{8,4},{10,20},{12,12},{14,28},{16,2},{18... | collective-permute-start | bytes 3080 | tf_op jit(solution)/shard_map/ppermute | solution.py:1292
  766.8 3.1 settle_heads.1
  (465 shorter events, 186.9 us)
Async XLA Ops:
  7.2 75.7 %copy-start = (bf16[1024,1024]{1,0:T(8,128)(2,1)S(1)}, bf16[1024,1024]{1,0:T(8,128)(2,1)}, u32[]{:S(2)}) copy-start(bf16[1024,1024]{1,0:T(8,128)(2,1)} %param.56) | copy-start | bytes 6291460
  26.5 47.7 %all-to-all-start = ((bf16[8,136,384]{2,1,0:T(8,128)(2,1)}), bf16[8,136,384]{2,1,0:T(8,128)(2,1)}, u32[]{:S(2)}, u32[]{:S(2)}) async-start(bf16[8,136,384]{2,1,0:T(8,128)(2,1)} %bitcast.9), calls=%async_computation | async-start | bytes 1671168 | tf_op jit(solution)/shard_map/all_to_all | solution.py:1340
  32.9 191.0 %all-gather.5.cloned.1.call-start = ((), (), s32[]{:S(2)}) async-start(), calls=%async_computation.9 | async-start | bytes 10813440 | tf_op jit(solution)/shard_map/all_gather | solution.py:1512
  33.9 40.2 %collective-permute-start = (bf16[448,1024]{1,0:T(8,128)(2,1)}, bf16[448,1024]{1,0:T(8,128)(2,1)S(1)}, u32[]{:S(2)}, u32[]{:S(2)}) collective-permute-start(bf16[448,1024]{1,0:T(8,128)(2,1)} %pad_maximum_fusion.11), channel_id=1, source_target_pairs={{0,0},{2,16},{4,8},{6,24},{8,4},{10,20},{12,12},{14,28},{16,2},{18... | collective-permute-start | bytes 2752520 | tf_op jit(solution)/shard_map/ppermute | solution.py:1284
  74.2 10.8 %collective-permute-start.1 = (s32[2]{0:T(128)S(1)}, s32[2]{0:T(128)S(1)}, u32[]{:S(2)}, u32[]{:S(2)}) collective-permute-start(s32[2]{0:T(128)S(1)} %copy-done.64), channel_id=1, source_target_pairs={{0,0},{2,8},{4,16},{6,24},{8,4},{10,12},{12,20},{14,28},{16,2},{18... | collective-permute-start | bytes 32 | tf_op jit(solution)/shard_map/ppermute | solution.py:1437
  85.7 46.4 %collective-permute-start.2 = (bf16[448,1024]{1,0:T(8,128)(2,1)S(1)}, bf16[448,1024]{1,0:T(8,128)(2,1)}, u32[]{:S(2)}, u32[]{:S(2)}) collective-permute-start(bf16[448,1024]{1,0:T(8,128)(2,1)S(1)} %collective-permute-done.refs_0_), channel_id=1, source_target_pairs={{0,8},{1,9},{8,0},{9,1},{16,24},{17,25},{24,16},{25,17},{2,10},{3,... | collective-permute-start | bytes 2752520 | tf_op jit(solution)/shard_map/ppermute | solution.py:1244
  85.7 37.9 %collective-permute-start.3 = (bf16[448,1024]{1,0:T(8,128)(2,1)S(1)}, bf16[448,1024]{1,0:T(8,128)(2,1)}, u32[]{:S(2)}, u32[]{:S(2)}) collective-permute-start(bf16[448,1024]{1,0:T(8,128)(2,1)S(1)} %collective-permute-done.refs_0_), channel_id=1, source_target_pairs={{0,16},{16,17},{17,1},{1,0},{8,24},{24,25},{25,9},{9,8},{2,18},{18... | collective-permute-start | bytes 2752520 | tf_op jit(solution)/shard_map/ppermute | solution.py:1238
  91.9 35.8 %collective-permute-start.4 = (bf16[448,1024]{1,0:T(8,128)(2,1)S(1)}, bf16[448,1024]{1,0:T(8,128)(2,1)}, u32[]{:S(2)}, u32[]{:S(2)}) collective-permute-start(bf16[448,1024]{1,0:T(8,128)(2,1)S(1)} %collective-permute-done.refs_0_), channel_id=1, source_target_pairs={{16,0},{17,16},{1,17},{0,1},{24,8},{25,24},{9,25},{8,9},{18,2},{19... | collective-permute-start | bytes 2752520 | tf_op jit(solution)/shard_map/ppermute | solution.py:1241
  93.6 28.5 %all-to-all-start.2 = ((bf16[2,128,1024]{1,2,0:T(8,128)(2,1)}), bf16[2,128,1024]{1,2,0:T(8,128)(2,1)S(1)}, u32[]{:S(2)}, u32[]{:S(2)}) async-start(bf16[2,128,1024]{1,2,0:T(8,128)(2,1)} %bitcast.47), calls=%async_computation.2 | async-start | bytes 1048576 | tf_op jit(solution)/shard_map/all_to_all | solution.py:1340
  97.1 194.4 %all-gather.7.cloned.1.call-start = ((), (), s32[]{:S(2)}) async-start(), calls=%async_computation.10 | async-start | bytes 5242880 | tf_op jit(solution)/shard_map/all_gather | solution.py:1538
  99.8 112.0 %collective-permute-start.11 = (bf16[384,1024]{1,0:T(8,128)(2,1)}, bf16[384,1024]{1,0:T(8,128)(2,1)}, u32[]{:S(2)}, u32[]{:S(2)}) collective-permute-start(bf16[384,1024]{1,0:T(8,128)(2,1)} %pad_maximum_fusion.12), channel_id=1, source_target_pairs={{0,0},{2,16},{4,8},{6,24},{8,4},{10,20},{12,12},{14,28},{16,2},{18... | collective-permute-start | bytes 2359304 | tf_op jit(solution)/shard_map/ppermute | solution.py:1284
  124.6 22.8 %collective-permute-start.7 = (bf16[224,1024]{1,0:T(8,128)(2,1)S(1)}, bf16[224,1024]{1,0:T(8,128)(2,1)S(1)}, u32[]{:S(2)}, u32[]{:S(2)}) collective-permute-start(bf16[224,1024]{1,0:T(8,128)(2,1)S(1)} %slice.725), channel_id=1, source_target_pairs={{0,16},{16,17},{17,1},{1,0},{8,24},{24,25},{25,9},{9,8},{2,18},{18... | collective-permute-start | bytes 1376264 | tf_op jit(solution)/shard_map/ppermute | solution.py:1238
  128.8 18.7 %collective-permute-start.8 = (bf16[224,1024]{1,0:T(8,128)(2,1)S(1)}, bf16[224,1024]{1,0:T(8,128)(2,1)S(1)}, u32[]{:S(2)}, u32[]{:S(2)}) collective-permute-start(bf16[224,1024]{1,0:T(8,128)(2,1)S(1)} %slice.726), channel_id=1, source_target_pairs={{16,0},{17,16},{1,17},{0,1},{24,8},{25,24},{9,25},{8,9},{18,2},{19... | collective-permute-start | bytes 1376264 | tf_op jit(solution)/shard_map/ppermute | solution.py:1241
  129.1 19.5 %collective-permute-start.5 = (bf16[448,1024]{1,0:T(8,128)(2,1)}, bf16[448,1024]{1,0:T(8,128)(2,1)S(1)}, u32[]{:S(2)}, u32[]{:S(2)}) collective-permute-start(bf16[448,1024]{1,0:T(8,128)(2,1)} %collective-permute-done.3.refs_0_), channel_id=1, source_target_pairs={{0,8},{1,9},{8,0},{9,1},{16,24},{17,25},{24,16},{25,17},{2,10},{3,... | collective-permute-start | bytes 2752520 | tf_op jit(solution)/shard_map/ppermute | solution.py:1244
  132.1 16.5 %collective-permute-start.6 = (bf16[448,1024]{1,0:T(8,128)(2,1)}, bf16[448,1024]{1,0:T(8,128)(2,1)S(1)}, u32[]{:S(2)}, u32[]{:S(2)}) collective-permute-start(bf16[448,1024]{1,0:T(8,128)(2,1)} %collective-permute-done.4.refs_1_), channel_id=1, source_target_pairs={{0,8},{1,9},{8,0},{9,1},{16,24},{17,25},{24,16},{25,17},{2,10},{3,... | collective-permute-start | bytes 2752520 | tf_op jit(solution)/shard_map/ppermute | solution.py:1244
  147.6 10.3 %collective-permute-start.9 = (bf16[448,1024]{1,0:T(8,128)(2,1)S(1)}, bf16[448,1024]{1,0:T(8,128)(2,1)S(1)}, u32[]{:S(2)}, u32[]{:S(2)}) collective-permute-start(bf16[448,1024]{1,0:T(8,128)(2,1)S(1)} %constant_dynamic-update-slice_fusion.refs_0_), channel_id=1, source_target_pairs={{0,8},{1,9},{8,0},{9,1},{16,24},{17,25},{24,16},{25,17},{2,10},{3,... | collective-permute-start | bytes 2752520 | tf_op jit(solution)/shard_map/ppermute | solution.py:1244
  205.6 17.1 %all-to-all-start.1 = ((bf16[8,384,128]{2,1,0:T(8,128)(2,1)}), bf16[8,384,128]{2,1,0:T(8,128)(2,1)S(1)}, u32[]{:S(2)}, u32[]{:S(2)}) async-start(bf16[8,384,128]{2,1,0:T(8,128)(2,1)} %get-tuple-element.108), calls=%async_computation.1 | async-start | bytes 1572864 | tf_op jit(solution)/shard_map/all_to_all | solution.py:1340
  211.8 40.0 %collective-permute-start.12 = (bf16[384,1024]{1,0:T(8,128)(2,1)}, bf16[384,1024]{1,0:T(8,128)(2,1)}, u32[]{:S(2)}, u32[]{:S(2)}) collective-permute-start(bf16[384,1024]{1,0:T(8,128)(2,1)} %collective-permute-done.11.refs_2_), channel_id=1, source_target_pairs={{0,16},{16,17},{17,1},{1,0},{8,24},{24,25},{25,9},{9,8},{2,18},{18... | collective-permute-start | bytes 2359304 | tf_op jit(solution)/shard_map/ppermute | solution.py:1238
  213.2 38.5 %collective-permute-start.13 = (bf16[384,1024]{1,0:T(8,128)(2,1)}, bf16[384,1024]{1,0:T(8,128)(2,1)}, u32[]{:S(2)}, u32[]{:S(2)}) collective-permute-start(bf16[384,1024]{1,0:T(8,128)(2,1)} %collective-permute-done.11.refs_2_), channel_id=1, source_target_pairs={{16,0},{17,16},{1,17},{0,1},{24,8},{25,24},{9,25},{8,9},{18,2},{19... | collective-permute-start | bytes 2359304 | tf_op jit(solution)/shard_map/ppermute | solution.py:1241
  213.8 37.9 %collective-permute-start.14 = (bf16[384,1024]{1,0:T(8,128)(2,1)}, bf16[384,1024]{1,0:T(8,128)(2,1)}, u32[]{:S(2)}, u32[]{:S(2)}) collective-permute-start(bf16[384,1024]{1,0:T(8,128)(2,1)} %collective-permute-done.11.refs_2_), channel_id=1, source_target_pairs={{0,8},{1,9},{8,0},{9,1},{16,24},{17,25},{24,16},{25,17},{2,10},{3,... | collective-permute-start | bytes 2359304 | tf_op jit(solution)/shard_map/ppermute | solution.py:1244
  250.2 18.8 %collective-permute-start.16 = (bf16[384,1024]{1,0:T(8,128)(2,1)S(1)}, bf16[384,1024]{1,0:T(8,128)(2,1)S(1)}, u32[]{:S(2)}, u32[]{:S(2)}) collective-permute-start(bf16[384,1024]{1,0:T(8,128)(2,1)S(1)} %add_convert_fusion.2.refs_0_), channel_id=1, source_target_pairs={{0,16},{16,17},{17,1},{1,0},{8,24},{24,25},{25,9},{9,8},{2,18},{18... | collective-permute-start | bytes 2359304 | tf_op jit(solution)/shard_map/ppermute | solution.py:1238
  251.1 18.9 %collective-permute-start.18 = (bf16[384,1024]{1,0:T(8,128)(2,1)S(1)}, bf16[384,1024]{1,0:T(8,128)(2,1)S(1)}, u32[]{:S(2)}, u32[]{:S(2)}) collective-permute-start(bf16[384,1024]{1,0:T(8,128)(2,1)S(1)} %add_convert_fusion.2.refs_0_), channel_id=1, source_target_pairs={{16,0},{17,16},{1,17},{0,1},{24,8},{25,24},{9,25},{8,9},{18,2},{19... | collective-permute-start | bytes 2359304 | tf_op jit(solution)/shard_map/ppermute | solution.py:1241
  251.8 25.9 %collective-permute-start.23 = (bf16[384,1024]{1,0:T(8,128)(2,1)}, bf16[384,1024]{1,0:T(8,128)(2,1)S(1)}, u32[]{:S(2)}, u32[]{:S(2)}) collective-permute-start(bf16[384,1024]{1,0:T(8,128)(2,1)} %collective-permute-done.12.refs_4_), channel_id=1, source_target_pairs={{0,8},{1,9},{8,0},{9,1},{16,24},{17,25},{24,16},{25,17},{2,10},{3,... | collective-permute-start | bytes 2359304 | tf_op jit(solution)/shard_map/ppermute | solution.py:1244
  252.8 24.9 %collective-permute-start.24 = (bf16[384,1024]{1,0:T(8,128)(2,1)}, bf16[384,1024]{1,0:T(8,128)(2,1)S(1)}, u32[]{:S(2)}, u32[]{:S(2)}) collective-permute-start(bf16[384,1024]{1,0:T(8,128)(2,1)} %collective-permute-done.13.refs_5_), channel_id=1, source_target_pairs={{0,8},{1,9},{8,0},{9,1},{16,24},{17,25},{24,16},{25,17},{2,10},{3,... | collective-permute-start | bytes 2359304 | tf_op jit(solution)/shard_map/ppermute | solution.py:1244
  253.9 23.6 %collective-permute-start.21 = (bf16[192,1024]{1,0:T(8,128)(2,1)S(1)}, bf16[192,1024]{1,0:T(8,128)(2,1)S(1)}, u32[]{:S(2)}, u32[]{:S(2)}) collective-permute-start(bf16[192,1024]{1,0:T(8,128)(2,1)S(1)} %slice.593), channel_id=1, source_target_pairs={{0,16},{16,17},{17,1},{1,0},{8,24},{24,25},{25,9},{9,8},{2,18},{18... | collective-permute-start | bytes 1179656 | tf_op jit(solution)/shard_map/ppermute | solution.py:1238
  269.1 8.6 %collective-permute-start.22 = (bf16[192,1024]{1,0:T(8,128)(2,1)S(1)}, bf16[192,1024]{1,0:T(8,128)(2,1)S(1)}, u32[]{:S(2)}, u32[]{:S(2)}) collective-permute-start(bf16[192,1024]{1,0:T(8,128)(2,1)S(1)} %slice.594), channel_id=1, source_target_pairs={{16,0},{17,16},{1,17},{0,1},{24,8},{25,24},{9,25},{8,9},{18,2},{19... | collective-permute-start | bytes 1179656 | tf_op jit(solution)/shard_map/ppermute | solution.py:1241
  269.9 16.0 %collective-permute-start.17 = (bf16[192,1024]{1,0:T(8,128)(2,1)S(1)}, bf16[192,1024]{1,0:T(8,128)(2,1)S(1)}, u32[]{:S(2)}, u32[]{:S(2)}) collective-permute-start(bf16[192,1024]{1,0:T(8,128)(2,1)S(1)} %slice.748), channel_id=1, source_target_pairs={{0,16},{16,17},{17,1},{1,0},{8,24},{24,25},{25,9},{9,8},{2,18},{18... | collective-permute-start | bytes 1179656 | tf_op jit(solution)/shard_map/ppermute | solution.py:1238
  277.5 9.2 %collective-permute-start.19 = (bf16[192,1024]{1,0:T(8,128)(2,1)S(1)}, bf16[192,1024]{1,0:T(8,128)(2,1)S(1)}, u32[]{:S(2)}, u32[]{:S(2)}) collective-permute-start(bf16[192,1024]{1,0:T(8,128)(2,1)S(1)} %slice.749), channel_id=1, source_target_pairs={{16,0},{17,16},{1,17},{0,1},{24,8},{25,24},{9,25},{8,9},{18,2},{19... | collective-permute-start | bytes 1179656 | tf_op jit(solution)/shard_map/ppermute | solution.py:1241
  279.3 12.1 %collective-permute-start.25 = (bf16[384,1024]{1,0:T(8,128)(2,1)}, bf16[384,1024]{1,0:T(8,128)(2,1)}, u32[]{:S(2)}, u32[]{:S(2)}) collective-permute-start(bf16[384,1024]{1,0:T(8,128)(2,1)} %constant_dynamic-update-slice_fusion.4.refs_2_), channel_id=1, source_target_pairs={{0,8},{1,9},{8,0},{9,1},{16,24},{17,25},{24,16},{25,17},{2,10},{3,... | collective-permute-start | bytes 2359304 | tf_op jit(solution)/shard_map/ppermute | solution.py:1244
  287.5 4.8 collective-permute-start.20
  291.4 17.2 %collective-permute-start.10 = (bf16[384,1024]{1,0:T(8,128)(2,1)}, bf16[384,1024]{1,0:T(8,128)(2,1)}, u32[]{:S(2)}, u32[]{:S(2)}) collective-permute-start(bf16[384,1024]{1,0:T(8,128)(2,1)} %copy-done.39), channel_id=1, source_target_pairs={{0,8},{1,9},{8,0},{9,1},{16,24},{17,25},{24,16},{25,17},{2,10},{3,... | collective-permute-start | bytes 2359304 | tf_op jit(solution)/shard_map/ppermute | solution.py:1244
  307.7 16.6 %collective-permute-start.26 = (bf16[768,1024]{1,0:T(8,128)(2,1)}, bf16[768,1024]{1,0:T(8,128)(2,1)}, u32[]{:S(2)}, u32[]{:S(2)}) collective-permute-start(bf16[768,1024]{1,0:T(8,128)(2,1)} %slice_bitcast_fusion.2), channel_id=1, source_target_pairs={{0,8},{1,9},{8,0},{9,1},{16,24},{17,25},{24,16},{25,17},{2,10},{3,... | collective-permute-start | bytes 4718600 | tf_op jit(solution)/shard_map/ppermute | solution.py:1244
  308.0 20.0 %collective-permute-start.28 = (bf16[384,1024]{1,0:T(8,128)(2,1)}, bf16[384,1024]{1,0:T(8,128)(2,1)S(1)}, u32[]{:S(2)}, u32[]{:S(2)}) collective-permute-start(bf16[384,1024]{1,0:T(8,128)(2,1)} %copy-done.47), channel_id=1, source_target_pairs={{0,8},{1,9},{8,0},{9,1},{16,24},{17,25},{24,16},{25,17},{2,10},{3,... | collective-permute-start | bytes 2359304 | tf_op jit(solution)/shard_map/ppermute | solution.py:1244
  308.2 19.9 %collective-permute-start.29 = (bf16[384,1024]{1,0:T(8,128)(2,1)}, bf16[384,1024]{1,0:T(8,128)(2,1)S(1)}, u32[]{:S(2)}, u32[]{:S(2)}) collective-permute-start(bf16[384,1024]{1,0:T(8,128)(2,1)} %copy-done.48), channel_id=1, source_target_pairs={{0,8},{1,9},{8,0},{9,1},{16,24},{17,25},{24,16},{25,17},{2,10},{3,... | collective-permute-start | bytes 2359304 | tf_op jit(solution)/shard_map/ppermute | solution.py:1244
  324.2 65.8 %collective-permute-start.15 = (bf16[768,1024]{1,0:T(8,128)(2,1)}, bf16[768,1024]{1,0:T(8,128)(2,1)}, u32[]{:S(2)}, u32[]{:S(2)}) collective-permute-start(bf16[768,1024]{1,0:T(8,128)(2,1)} %slice_bitcast_fusion.3), channel_id=1, source_target_pairs={{0,8},{1,9},{8,0},{9,1},{16,24},{17,25},{24,16},{25,17},{2,10},{3,... | collective-permute-start | bytes 4718600 | tf_op jit(solution)/shard_map/ppermute | solution.py:1244
  326.5 30.4 %collective-permute-start.27 = (bf16[384,1024]{1,0:T(8,128)(2,1)S(1)}, bf16[384,1024]{1,0:T(8,128)(2,1)S(1)}, u32[]{:S(2)}, u32[]{:S(2)}) collective-permute-start(bf16[384,1024]{1,0:T(8,128)(2,1)S(1)} %get-tuple-element.246), channel_id=1, source_target_pairs={{0,16},{16,17},{17,1},{1,0},{8,24},{24,25},{25,9},{9,8},{2,18},{18... | collective-permute-start | bytes 2359304 | tf_op jit(solution)/shard_map/ppermute | solution.py:1238
  327.6 29.3 %collective-permute-start.32 = (bf16[384,1024]{1,0:T(8,128)(2,1)S(1)}, bf16[384,1024]{1,0:T(8,128)(2,1)S(1)}, u32[]{:S(2)}, u32[]{:S(2)}) collective-permute-start(bf16[384,1024]{1,0:T(8,128)(2,1)S(1)} %get-tuple-element.247), channel_id=1, source_target_pairs={{16,0},{17,16},{1,17},{0,1},{24,8},{25,24},{9,25},{8,9},{18,2},{19... | collective-permute-start | bytes 2359304 | tf_op jit(solution)/shard_map/ppermute | solution.py:1241
  355.9 20.5 %collective-permute-start.30 = (bf16[2,768,1024]{2,1,0:T(8,128)(2,1)}, bf16[2,768,1024]{2,1,0:T(8,128)(2,1)}, u32[]{:S(2)}, u32[]{:S(2)}) collective-permute-start(bf16[2,768,1024]{2,1,0:T(8,128)(2,1)} %slice.599), channel_id=1, source_target_pairs={{0,8},{1,9},{8,0},{9,1},{16,24},{17,25},{24,16},{25,17},{2,10},{3,... | collective-permute-start | bytes 9437192 | tf_op jit(solution)/shard_map/ppermute | solution.py:1244
  382.1 36.1 %collective-permute-start.33 = (bf16[768,1024]{1,0:T(8,128)(2,1)S(1)}, bf16[768,1024]{1,0:T(8,128)(2,1)S(1)}, u32[]{:S(2)}, u32[]{:S(2)}) collective-permute-start(bf16[768,1024]{1,0:T(8,128)(2,1)S(1)} %pad_maximum_fusion.7), channel_id=1, source_target_pairs={{16,0},{17,16},{1,17},{0,1},{24,8},{25,24},{9,25},{8,9},{18,2},{19... | collective-permute-start | bytes 4718600 | tf_op jit(solution)/shard_map/ppermute | solution.py:1241
  382.4 35.8 %collective-permute-start.31 = (bf16[768,1024]{1,0:T(8,128)(2,1)S(1)}, bf16[768,1024]{1,0:T(8,128)(2,1)S(1)}, u32[]{:S(2)}, u32[]{:S(2)}) collective-permute-start(bf16[768,1024]{1,0:T(8,128)(2,1)S(1)} %pad_maximum_fusion.6), channel_id=1, source_target_pairs={{0,16},{16,17},{17,1},{1,0},{8,24},{24,25},{25,9},{9,8},{2,18},{18... | collective-permute-start | bytes 4718600 | tf_op jit(solution)/shard_map/ppermute | solution.py:1238
  429.3 67.4 %all-to-all-start.3 = ((bf16[8,128,1024]{2,1,0:T(8,128)(2,1)}), bf16[8,128,1024]{2,1,0:T(8,128)(2,1)}, u32[]{:S(2)}, u32[]{:S(2)}) async-start(bf16[8,128,1024]{2,1,0:T(8,128)(2,1)} %bitcast.328), calls=%async_computation.3 | async-start | bytes 4194304 | tf_op jit(solution)/shard_map/all_to_all | solution.py:1340
  434.6 222.9 %reduce-scatter.2.cloned.1.call-start = ((), (), s32[]{:S(2)}) async-start(), calls=%async_computation.8 | async-start | bytes 10911744 | tf_op jit(solution)/shard_map/reduce_scatter | solution.py:1649
  437.6 44.0 %collective-permute-start.34 = (bf16[272,1024]{1,0:T(8,128)(2,1)}, bf16[272,1024]{1,0:T(8,128)(2,1)}, u32[]{:S(2)}, u32[]{:S(2)}) collective-permute-start(bf16[272,1024]{1,0:T(8,128)(2,1)} %get-tuple-element.223), channel_id=1, source_target_pairs={{0,0},{2,16},{4,8},{6,24},{8,2},{10,18},{12,10},{14,26},{16,4},{18... | collective-permute-start | bytes 1671176 | tf_op jit(solution)/shard_map/ppermute | solution.py:1310
  442.4 51.1 %collective-permute-start.35 = (bf16[272,1024]{1,0:T(8,128)(2,1)}, bf16[272,1024]{1,0:T(8,128)(2,1)}, u32[]{:S(2)}, u32[]{:S(2)}) collective-permute-start(bf16[272,1024]{1,0:T(8,128)(2,1)} %get-tuple-element.222), channel_id=1, source_target_pairs={{0,2},{2,18},{4,10},{6,26},{8,0},{10,16},{12,8},{14,24},{16,6},{18... | collective-permute-start | bytes 1671176 | tf_op jit(solution)/shard_map/ppermute | solution.py:1310
  443.7 49.8 %collective-permute-start.36 = (bf16[272,1024]{1,0:T(8,128)(2,1)S(1)}, bf16[272,1024]{1,0:T(8,128)(2,1)}, u32[]{:S(2)}, u32[]{:S(2)}) collective-permute-start(bf16[272,1024]{1,0:T(8,128)(2,1)S(1)} %get-tuple-element.221), channel_id=1, source_target_pairs={{0,4},{2,20},{4,12},{6,28},{8,6},{10,22},{12,14},{14,30},{16,0},{1... | collective-permute-start | bytes 1671176 | tf_op jit(solution)/shard_map/ppermute | solution.py:1310
  445.9 50.7 %collective-permute-start.37 = (bf16[272,1024]{1,0:T(8,128)(2,1)S(1)}, bf16[272,1024]{1,0:T(8,128)(2,1)}, u32[]{:S(2)}, u32[]{:S(2)}) collective-permute-start(bf16[272,1024]{1,0:T(8,128)(2,1)S(1)} %get-tuple-element.220), channel_id=1, source_target_pairs={{0,6},{2,22},{4,14},{6,30},{8,4},{10,20},{12,12},{14,28},{16,2},{1... | collective-permute-start | bytes 1671176 | tf_op jit(solution)/shard_map/ppermute | solution.py:1310
  513.5 14.9 %all-to-all-start.4 = ((bf16[8,384,128]{2,1,0:T(8,128)(2,1)}), bf16[8,384,128]{2,1,0:T(8,128)(2,1)S(1)}, u32[]{:S(2)}, u32[]{:S(2)}) async-start(bf16[8,384,128]{2,1,0:T(8,128)(2,1)} %bitcast.79), calls=%async_computation.4 | async-start | bytes 1572864 | tf_op jit(solution)/shard_map/all_to_all | solution.py:1340
  529.3 58.4 %copy-start.31 = (bf16[384,1024]{1,0:T(8,128)(2,1)S(1)}, bf16[384,1024]{1,0:T(8,128)(2,1)}, u32[]{:S(2)}) copy-start(bf16[384,1024]{1,0:T(8,128)(2,1)} %get-tuple-element.156) | copy-start | bytes 2359300
  529.3 65.2 %copy-start.36 = (bf16[8,128,384]{2,1,0:T(8,128)(2,1)S(1)}, bf16[8,128,384]{2,1,0:T(8,128)(2,1)}, u32[]{:S(2)}) copy-start(bf16[8,128,384]{2,1,0:T(8,128)(2,1)} %slice.562) | copy-start | bytes 2359300
  587.7 40.9 %collective-permute-start.38 = (bf16[384,1024]{1,0:T(8,128)(2,1)S(1)}, bf16[384,1024]{1,0:T(8,128)(2,1)S(1)}, u32[]{:S(2)}, u32[]{:S(2)}) collective-permute-start(bf16[384,1024]{1,0:T(8,128)(2,1)S(1)} %copy-done.31), channel_id=1, source_target_pairs={{0,0},{2,16},{4,8},{6,24},{8,4},{10,20},{12,12},{14,28},{16,2},{18... | collective-permute-start | bytes 2359304 | tf_op jit(solution)/shard_map/ppermute | solution.py:1292
  594.4 63.1 %collective-permute-start.46 = (bf16[8,128,1024]{2,1,0:T(8,128)(2,1)}, bf16[8,128,1024]{2,1,0:T(8,128)(2,1)}, u32[]{:S(2)}, u32[]{:S(2)}) collective-permute-start(bf16[8,128,1024]{2,1,0:T(8,128)(2,1)} %all-to-all-done.3), channel_id=1, source_target_pairs={{0,2},{2,18},{4,10},{6,26},{8,6},{10,22},{12,14},{14,30},{16,0},{1... | collective-permute-start | bytes 6291464 | tf_op jit(solution)/shard_map/ppermute | solution.py:1300
  598.0 9.6 %collective-permute-start.42 = (bf16[2,384,1024]{2,1,0:T(8,128)(2,1)S(1)}, bf16[2,384,1024]{2,1,0:T(8,128)(2,1)S(1)}, u32[]{:S(2)}, u32[]{:S(2)}) collective-permute-start(bf16[2,384,1024]{2,1,0:T(8,128)(2,1)S(1)} %bitcast.366), channel_id=1, source_target_pairs={{0,8},{1,9},{8,0},{9,1},{16,24},{17,25},{24,16},{25,17},{2,10},{3,... | collective-permute-start | bytes 4718600 | tf_op jit(solution)/shard_map/ppermute | solution.py:1244
  599.8 6.1 collective-permute-start.40
  602.3 27.8 %collective-permute-start.39 = (bf16[384,1024]{1,0:T(8,128)(2,1)S(1)}, bf16[384,1024]{1,0:T(8,128)(2,1)S(1)}, u32[]{:S(2)}, u32[]{:S(2)}) collective-permute-start(bf16[384,1024]{1,0:T(8,128)(2,1)S(1)} %slice.766), channel_id=1, source_target_pairs={{0,8},{1,9},{8,0},{9,1},{16,24},{17,25},{24,16},{25,17},{2,10},{3,... | collective-permute-start | bytes 2359304 | tf_op jit(solution)/shard_map/ppermute | solution.py:1244
  606.3 16.8 %collective-permute-start.41 = (bf16[192,1024]{1,0:T(8,128)(2,1)S(1)}, bf16[192,1024]{1,0:T(8,128)(2,1)S(1)}, u32[]{:S(2)}, u32[]{:S(2)}) collective-permute-start(bf16[192,1024]{1,0:T(8,128)(2,1)S(1)} %get-tuple-element.252), channel_id=1, source_target_pairs={{0,16},{16,17},{17,1},{1,0},{8,24},{24,25},{25,9},{9,8},{2,18},{18... | collective-permute-start | bytes 1179656 | tf_op jit(solution)/shard_map/ppermute | solution.py:1238
  607.5 15.6 %collective-permute-start.44 = (bf16[192,1024]{1,0:T(8,128)(2,1)S(1)}, bf16[192,1024]{1,0:T(8,128)(2,1)S(1)}, u32[]{:S(2)}, u32[]{:S(2)}) collective-permute-start(bf16[192,1024]{1,0:T(8,128)(2,1)S(1)} %get-tuple-element.253), channel_id=1, source_target_pairs={{16,0},{17,16},{1,17},{0,1},{24,8},{25,24},{9,25},{8,9},{18,2},{19... | collective-permute-start | bytes 1179656 | tf_op jit(solution)/shard_map/ppermute | solution.py:1241
  623.4 24.4 %collective-permute-start.45 = (bf16[384,1024]{1,0:T(8,128)(2,1)S(1)}, bf16[384,1024]{1,0:T(8,128)(2,1)S(1)}, u32[]{:S(2)}, u32[]{:S(2)}) collective-permute-start(bf16[384,1024]{1,0:T(8,128)(2,1)S(1)} %pad_maximum_fusion.14), channel_id=1, source_target_pairs={{16,0},{17,16},{1,17},{0,1},{24,8},{25,24},{9,25},{8,9},{18,2},{19... | collective-permute-start | bytes 2359304 | tf_op jit(solution)/shard_map/ppermute | solution.py:1241
  625.3 22.5 %collective-permute-start.43 = (bf16[384,1024]{1,0:T(8,128)(2,1)S(1)}, bf16[384,1024]{1,0:T(8,128)(2,1)S(1)}, u32[]{:S(2)}, u32[]{:S(2)}) collective-permute-start(bf16[384,1024]{1,0:T(8,128)(2,1)S(1)} %pad_maximum_fusion.13), channel_id=1, source_target_pairs={{0,16},{16,17},{17,1},{1,0},{8,24},{24,25},{25,9},{9,8},{2,18},{18... | collective-permute-start | bytes 2359304 | tf_op jit(solution)/shard_map/ppermute | solution.py:1238
  660.1 102.6 %collective-permute-start.47 = (bf16[848,1024]{1,0:T(8,128)(2,1)S(1)}, bf16[848,1024]{1,0:T(8,128)(2,1)S(1)}, u32[]{:S(2)}, u32[]{:S(2)}) collective-permute-start(bf16[848,1024]{1,0:T(8,128)(2,1)S(1)} %pad_maximum_fusion.5), channel_id=1, source_target_pairs={{0,0},{2,16},{4,8},{6,24},{8,4},{10,20},{12,12},{14,28},{16,2},{18... | collective-permute-start | bytes 5210120 | tf_op jit(solution)/shard_map/ppermute | solution.py:1292
  680.2 40.8 %all-to-all-start.5 = ((bf16[8,128,640]{2,1,0:T(8,128)(2,1)}), bf16[8,128,640]{2,1,0:T(8,128)(2,1)}, u32[]{:S(2)}, u32[]{:S(2)}) async-start(bf16[8,128,640]{2,1,0:T(8,128)(2,1)} %bitcast.131), calls=%async_computation.6 | async-start | bytes 2621440 | tf_op jit(solution)/shard_map/all_to_all | solution.py:1340
  687.8 73.2 %collective-permute-start.50 = (f32[3,128]{1,0:T(4,128)S(1)}, f32[3,128]{1,0:T(4,128)S(1)}, u32[]{:S(2)}, u32[]{:S(2)}) collective-permute-start(f32[3,128]{1,0:T(4,128)S(1)} %pad_maximum_fusion.20), channel_id=1, source_target_pairs={{0,0},{1,1},{2,16},{3,17},{4,8},{5,9},{6,24},{7,25},{8,2},{9,3},{1... | collective-permute-start | bytes 4616 | tf_op jit(solution)/shard_map/ppermute | solution.py:1326
  721.0 45.8 %collective-permute-start.49 = (bf16[8,128,640]{2,1,0:T(8,128)(2,1)}, bf16[8,128,640]{2,1,0:T(8,128)(2,1)}, u32[]{:S(2)}, u32[]{:S(2)}) collective-permute-start(bf16[8,128,640]{2,1,0:T(8,128)(2,1)} %all-to-all-done.5), channel_id=1, source_target_pairs={{0,2},{2,18},{4,10},{6,26},{8,6},{10,22},{12,14},{14,30},{16,0},{1... | collective-permute-start | bytes 3932168 | tf_op jit(solution)/shard_map/ppermute | solution.py:1300
  724.8 24.8 %all-to-all-start.6 = ((f32[8,2,128]{2,1,0:T(2,128)}), f32[8,2,128]{2,1,0:T(2,128)S(1)}, u32[]{:S(2)}, u32[]{:S(2)}) async-start(f32[8,2,128]{2,1,0:T(2,128)} %copy.193), calls=%async_computation.7 | async-start | bytes 16384 | tf_op jit(solution)/shard_map/all_to_all | solution.py:1340
  749.6 12.5 %collective-permute-start.48 = (f32[2,128]{1,0:T(2,128)S(1)}, f32[2,128]{1,0:T(2,128)S(1)}, u32[]{:S(2)}, u32[]{:S(2)}) collective-permute-start(f32[2,128]{1,0:T(2,128)S(1)} %reduce_sum.295), channel_id=1, source_target_pairs={{0,0},{2,16},{4,8},{6,24},{8,4},{10,20},{12,12},{14,28},{16,2},{18... | collective-permute-start | bytes 3080 | tf_op jit(solution)/shard_map/ppermute | solution.py:1292
  (75 other events, 498.0 us)
Sparse Core Ops, SparseCore 0:
  74.3 113.5 all-gather.4
  190.1 78.8 all-gather.6
  509.4 78.2 reduce-scatter.1

commit v2 on v1

--- a/solution.py
+++ b/solution.py
@@ -644,7 +644,7 @@
 NT = (((1,), (1,)), ((), ()))
 TN = (((0,), (0,)), ((), ()))
 PAIR = 2 * HD
-TILE = 256
+TILE = 512
 VMEM_BYTES = 56 * 1024 * 1024
 
 
@@ -949,7 +949,7 @@
         out_specs=tuple(in_vmem(3)),
         scratch_shapes=[natural] * 4,
         compiler_params=pltpu.CompilerParams(vmem_limit_bytes=VMEM_BYTES),
-        cost_estimate=cost(44),
+        cost_estimate=cost(25),
         name="self_forward",
     )(lines, bounds, *groups)
 
@@ -965,7 +965,7 @@
         out_specs=tuple(in_vmem(3)),
         scratch_shapes=[natural] * 5 + [wide] * 2,
         compiler_params=pltpu.CompilerParams(vmem_limit_bytes=VMEM_BYTES),
-        cost_estimate=cost(60),
+        cost_estimate=cost(37),
         name="self_backward",
     )(lines, bounds, *groups, grad, att, lse)
 
@@ -1087,12 +1087,10 @@
     grad_ref,
     out_ref,
     lse_ref,
-    lookup_weight_ref,
-    content_weight_ref,
     dprobe_ref,
     dmemory_ref,
-    dencoded_ref,
-    dencoded,
+    dlookup_ref,
+    dcontent_ref,
 ):
     query = split_heads(probe_ref[...] * jnp.bfloat16(HD**-0.5))
     key = lookup_ref[...]
@@ -1121,19 +1119,8 @@
         columns = slice(block * PAIR, (block + 1) * PAIR)
         dmemory_ref[0, :rows, columns] = dlookup[block * rows : (block + 1) * rows]
         dmemory_ref[0, rows:, columns] = dcontent[block * rows : (block + 1) * rows]
-    term = dot(dlookup, lookup_weight_ref[...], NT) + dot(dcontent, content_weight_ref[...], NT)
-
-    @pl.when(pl.program_id(0) == 0)
-    def begin():
-        dencoded[...] = term
-
-    @pl.when(pl.program_id(0) > 0)
-    def more():
-        dencoded[...] += term
-
-    @pl.when(pl.program_id(0) == 7)
-    def end():
-        dencoded_ref[...] = dencoded[...].astype(jnp.bfloat16)
+    dlookup_ref[...] = dlookup
+    dcontent_ref[...] = dcontent
 
 
 def pair_block(rows):
@@ -1159,7 +1146,7 @@
     )(probes, lookups, contents)
 
 
-def cross_backward(probes, lookups, contents, grad, recalled, lse, lookup_weight, content_weight):
+def cross_backward(probes, lookups, contents, grad, recalled, lse):
     rows, width = probes.shape
     memory = lookups.shape[0]
     pairs = width // PAIR
@@ -1170,6 +1157,7 @@
             jax.ShapeDtypeStruct((rows, width), jnp.bfloat16),
             jax.ShapeDtypeStruct((pairs, 2 * memory // 8, width), jnp.bfloat16),
             jax.ShapeDtypeStruct((memory, width), jnp.bfloat16),
+            jax.ShapeDtypeStruct((memory, width), jnp.bfloat16),
         ),
         in_specs=[
             pair_block(rows),
@@ -1178,19 +1166,17 @@
             pair_block(rows),
             pair_block(rows),
             pl.BlockSpec((1, 2, rows), lambda at: (at, 0, 0)),
-            pair_block(width),
-            pair_block(width),
         ],
         out_specs=(
             pair_block(rows),
             pl.BlockSpec((1, 2 * memory // 8, width), lambda at: (at, 0, 0)),
-            fixed((memory, width)),
+            pair_block(memory),
+            pair_block(memory),
         ),
-        scratch_shapes=[pltpu.VMEM((memory, width), jnp.float32)],
         compiler_params=pltpu.CompilerParams(vmem_limit_bytes=VMEM_BYTES),
-        cost_estimate=cost(20),
+        cost_estimate=cost(13),
         name="cross_backward",
-    )(probes, lookups, contents, grad, recalled, lse, lookup_weight, content_weight)
+    )(probes, lookups, contents, grad, recalled, lse)
 
 
 def norm_parts(values):
@@ -1600,16 +1586,13 @@
     dsecond = upstream.astype(jnp.float32) + part
     dsecond_low = dsecond.astype(low)
     drecalled = right_product(dsecond_low, merged_full).astype(low)
-    dprobes, dmemory, encoded_gradient = cross_backward(
-        probes,
-        lookups,
-        contents,
-        drecalled,
-        recalled,
-        cross_logsum,
-        lookup_full,
-        content_full,
-    )
+    dprobes, dmemory, dlookups, dcontents = cross_backward(
+        probes, lookups, contents, drecalled, recalled, cross_logsum
+    )
+    encoded_gradient = right_product(dlookups, lookup_full) + right_product(
+        dcontents, content_full
+    )
+    encoded_gradient = encoded_gradient.astype(low)
     dnormed_cross = right_product(after(dprobes, (up_gradient, down_gradient)), probe_full)
     part, cross_gain_sum, cross_shift_sum = norm_backward(
         dnormed_cross, first_unit, first_rate, cross_gain_full

time: 792 us -> 767 us (0.968)
  Pallas kernels: 202 us -> 155 us
  starting transfers between devices: 132 us -> 151 us
    all_to_all x7, starting transfers between devices: 40.2 us -> 63.7 us  [exchange(): return lax.all_to_all(values, axes, split_axis=0, concat_axis=0, tiled=True)]
    pallas_call x1, Pallas kernels: 58.4 us -> 36.7 us  [self_backward(): pl.pallas_call(functools.partial(self_backward_kernel, prompt_all), out_s...]
    pallas_call x1, Pallas kernels: 42.4 us -> 24.9 us  [self_forward(): pl.pallas_call(functools.partial(self_forward_kernel, prompt_all), out_sh...]
    ppermute x3, starting transfers between devices: 26.2 us -> 16.3 us  [leave(): return lax.ppermute(values, (GRP, BLK), moves)]
    ppermute x10, waiting for transfers between devices: 45.8 us -> 54.5 us  [up(): return lax.ppermute(values, ROLE_AXES, self.forward)]
    all_to_all x7, waiting for transfers between devices: 62.9 us -> 54.6 us  [exchange(): return lax.all_to_all(values, axes, split_axis=0, concat_axis=0, tiled=True)]
    unnamed x191 -> x201, local copies, waits for them, and re-layouts: 48.7 us -> 50.3 us
  transfers between devices with their start and end apart: 61 -> 61, of which waited for: 20 -> 20; matrix products, arithmetic and copies ran while one was open for 20% -> 20% of each run, Pallas kernels for 26% -> 20%
where the time goes in v2:
time: 767 us; the launch traced here: 755 us
  waiting for transfers between devices  218 us (28%)
  Pallas kernels  155 us (20%)
  starting transfers between devices  151 us (20%)
  local copies, waits for them, and re-layouts  114 us (15%)
  matrix products  55.4 us (7%)
  other arithmetic  46.1 us (6%)
  between operations  16.2 us (2%)
    all_to_all x7, starting transfers between devices, exchange(): return lax.all_to_all(values, axes, split_axis=0, concat_axis=0, tiled=True)  63.7 us
    all_to_all x7, waiting for transfers between devices, exchange(): return lax.all_to_all(values, axes, split_axis=0, concat_axis=0, tiled=True)  54.6 us
    ppermute x10, waiting for transfers between devices, up(): return lax.ppermute(values, ROLE_AXES, self.forward)  54.5 us
    ppermute x10, waiting for transfers between devices, down(): return lax.ppermute(values, ROLE_AXES, self.reverse)  53.8 us
    unnamed x201, local copies, waits for them, and re-layouts  50.3 us
    pallas_call x3, Pallas kernels, feed(): pl.pallas_call(functools.partial(feed_kernel, count), grid=(count,), in_s...  47.5 us
    pallas_call x1, Pallas kernels, self_backward(): pl.pallas_call(functools.partial(self_backward_kernel, prompt_all), out_s...  36.7 us
    ppermute x2, waiting for transfers between devices, enter(): return lax.ppermute(values, (GRP, BLK), moves)  30.7 us
  transfers between devices with their start and end apart: 61, of which 20 were waited for; matrix products, arithmetic and copies ran while one was open for 20% of the time, Pallas kernels for 20%

profile of v2, /device:TPU:1, one launch (start us, length us, event | category | flops | bytes accessed | tf_op | source)
XLA Modules:
  0.0 754.5 jit_solution(10322782270751629083)
XLA Ops:
  26.5 6.4 all-to-all-start
  33.9 5.3 collective-permute-start
  43.5 30.7 %collective-permute-done.refs_0_ = bf16[448,1024]{1,0:T(8,128)(2,1)S(1)} collective-permute-done((bf16[448,1024]{1,0:T(8,128)(2,1)}, bf16[448,1024]{1,0:T(8,128)(2,1)S(1)}, u32[]{:S(2)}, u32[]{:S(2)}) %collective-permute-start) | collective-permute-done | bytes 917536 | tf_op jit(solution)/shard_map/ppermute | solution.py:1270
  76.3 4.1 copy.159
  85.7 6.2 collective-permute-start.3
  93.6 3.5 all-to-all-start.2
  99.8 6.1 collective-permute-start.11
  106.1 16.0 %all-to-all-done.2 = bf16[2,128,1024]{1,2,0:T(8,128)(2,1)S(1)} async-done(((bf16[2,128,1024]{1,2,0:T(8,128)(2,1)}), bf16[2,128,1024]{1,2,0:T(8,128)(2,1)S(1)}, u32[]{:S(2)}, u32[]{:S(2)}) %all-to-all-start.2) | async-done | bytes 524320 | tf_op jit(solution)/shard_map/all_to_all | solution.py:1326
  124.6 3.1 collective-permute-start.7
  129.1 3.0 collective-permute-start.5
  134.9 4.4 project.3
  139.3 8.2 %collective-permute-done.7 = bf16[224,1024]{1,0:T(8,128)(2,1)S(1)} collective-permute-done((bf16[224,1024]{1,0:T(8,128)(2,1)S(1)}, bf16[224,1024]{1,0:T(8,128)(2,1)S(1)}, u32[]{:S(2)}, u32[]{:S(2)}) %collective-permute-start.7) | collective-permute-done | bytes 458784 | tf_op jit(solution)/shard_map/ppermute | solution.py:1224
  150.5 7.3 project.4
  158.8 4.4 project.5
  163.2 24.9 %self_forward.1 = (f32[3072,128]{1,0:T(8,128)}, bf16[8,384,128]{2,1,0:T(8,128)(2,1)}, f32[6,2,512]{2,1,0:T(2,128)}) custom-call(s32[8]{0:T(128)} %stack.105.lines_ref, s32[2]{0:T(128)} %bitcast.436, bf16[2,384,384]{2,1,0:T(8,128)(2,1)} %get-tuple-element.106.near_ref, bf16[4,384,384]{2,1,0:T(8,128)(2,1)} %get-tuple-element.107.next_ref, ...), custom_call_target="tpu_custom_call" | custom-call | flops 22499999744 | bytes 50000000 | tf_op jit(solution)/shard_map/self_forward/pallas_call | solution.py:941
  188.1 5.3 all-to-all-start.1
  197.8 7.4 all-to-all-done.1
  206.4 4.9 fusion.39
  212.8 2.7 convolution_convert_fusion.6.lookup_ref
  219.8 9.8 %cross_forward.1 = (f32[384,1024]{1,0:T(8,128)}, f32[8,2,384]{2,1,0:T(2,128)}) custom-call(bf16[384,1024]{1,0:T(8,128)(2,1)} %add_convert_fusion.4.probe_ref, bf16[512,1024]{1,0:T(8,128)(2,1)} %convolution_convert_fusion.6.lookup_ref, bf16[512,1024]{1,0:T(8,128)(2,1)} %add_convert_fusion.1.content_ref), custom_call_target="tpu_custom_call" | custom-call | flops 8999999488 | bytes 20000000 | tf_op jit(solution)/shard_map/cross_forward/pallas_call | solution.py:1134
  238.0 13.7 %collective-permute-done.16.refs_0_ = bf16[384,1024]{1,0:T(8,128)(2,1)S(1)} collective-permute-done((bf16[384,1024]{1,0:T(8,128)(2,1)S(1)}, bf16[384,1024]{1,0:T(8,128)(2,1)S(1)}, u32[]{:S(2)}, u32[]{:S(2)}) %collective-permute-start.16) | collective-permute-done | bytes 786464 | tf_op jit(solution)/shard_map/ppermute | solution.py:1224
  253.5 6.6 collective-permute-done.21
  262.2 3.1 collective-permute-start.25
  265.3 3.2 collective-permute-done.17
  274.9 12.7 %feed.4 = (bf16[2,768,1024]{2,1,0:T(8,128)(2,1)}, bf16[2,384,1024]{2,1,0:T(8,128)(2,1)}, bf16[2,384,1024]{2,1,0:T(8,128)(2,1)}, bf16[2,384,1024]{2,1,0:T(8,128)(2,1)}, bf16[2,384,1024]{2,1,0:T(8,128)(2,1)}) custom-call(bf16[384,1024]{1,0:T(8,128)(2,1)} %constant_dynamic-update-slice_fusion.2.refs_0_, bf16[384,1024]{1,0:T(8,128)(2,1)} %collective-permute-done.20.refs_1_, ...), custom_call_target="tpu_custom_call" | custom-call | flops 11699999744 | bytes 26000000 | tf_op jit(solution)/shard_map/feed/pallas_call | solution.py:1053
  287.6 2.7 slice_bitcast_fusion.2
  291.2 12.8 %feed.3 = (bf16[2,768,1024]{2,1,0:T(8,128)(2,1)}, bf16[2,384,1024]{2,1,0:T(8,128)(2,1)}, bf16[2,384,1024]{2,1,0:T(8,128)(2,1)}, bf16[2,384,1024]{2,1,0:T(8,128)(2,1)}, bf16[2,384,1024]{2,1,0:T(8,128)(2,1)}) custom-call(bf16[384,1024]{1,0:T(8,128)(2,1)} %copy-done.40, bf16[384,1024]{1,0:T(8,128)(2,1)} %collective-permute-done.10.refs_1_, ...), custom_call_target="tpu_custom_call" | custom-call | flops 11699999744 | bytes 26000000 | tf_op jit(solution)/shard_map/feed/pallas_call | solution.py:1053
  304.0 2.8 slice_bitcast_fusion.3
  312.5 22.0 %feed.5 = (bf16[4,768,1024]{2,1,0:T(8,128)(2,1)}, bf16[4,384,1024]{2,1,0:T(8,128)(2,1)}, bf16[4,384,1024]{2,1,0:T(8,128)(2,1)}, bf16[4,384,1024]{2,1,0:T(8,128)(2,1)}, bf16[4,384,1024]{2,1,0:T(8,128)(2,1)}) custom-call(bf16[384,1024]{1,0:T(8,128)(2,1)} %copy-done.50, bf16[384,1024]{1,0:T(8,128)(2,1)} %copy-done.51, bf16[384,1024]{1,0:T(8,128)(2,1)} %copy-done.65, ...), custom_call_target="tpu_custom_call" | custom-call | flops 23399999488 | bytes 52000000 | tf_op jit(solution)/shard_map/feed/pallas_call | solution.py:1053
  334.5 4.0 slice.599
  342.6 3.9 fusion.56
  346.5 3.6 fusion.57
  353.6 5.4 fusion.55
  359.1 3.5 fusion.38
  372.6 28.2 %collective-permute-done.33 = bf16[768,1024]{1,0:T(8,128)(2,1)S(1)} collective-permute-done((bf16[768,1024]{1,0:T(8,128)(2,1)S(1)}, bf16[768,1024]{1,0:T(8,128)(2,1)S(1)}, u32[]{:S(2)}, u32[]{:S(2)}) %collective-permute-start.33) | collective-permute-done | bytes 1572896 | tf_op jit(solution)/shard_map/ppermute | solution.py:1227
  400.8 2.8 fusion.4
  404.3 3.0 convert_reduce_fusion.6
  409.3 2.6 convolution_convert_fusion.3
  411.9 5.3 all-to-all-start.3
  419.2 4.6 collective-permute-start.34
  423.9 3.4 collective-permute-start.36
  429.4 13.1 %cross_backward.1 = (bf16[384,1024]{1,0:T(8,128)(2,1)}, bf16[8,128,1024]{2,1,0:T(8,128)(2,1)}, bf16[512,1024]{1,0:T(8,128)(2,1)}, bf16[512,1024]{1,0:T(8,128)(2,1)}) custom-call(bf16[384,1024]{1,0:T(8,128)(2,1)} %add_convert_fusion.4.probe_ref, bf16[512,1024]{1,0:T(8,128)(2,1)} %convolution_convert_fusion.6.lookup_ref, ...), custom_call_target="tpu_custom_call" | custom-call | flops 11699999744 | bytes 26000000 | tf_op jit(solution)/shard_map/cross_backward/pallas_call | solution.py:1153
  442.5 2.5 convolution_convert_fusion.2
  455.2 7.4 collective-permute-done.34
  462.7 11.5 %collective-permute-done.35 = bf16[272,1024]{1,0:T(8,128)(2,1)} collective-permute-done((bf16[272,1024]{1,0:T(8,128)(2,1)S(1)}, bf16[272,1024]{1,0:T(8,128)(2,1)}, u32[]{:S(2)}, u32[]{:S(2)}) %collective-permute-start.35) | collective-permute-done | bytes 557088 | tf_op jit(solution)/shard_map/ppermute | solution.py:1296
  474.2 3.4 collective-permute-done.37
  477.6 3.0 multiply_reduce_fusion.1
  490.3 2.6 convolution_convert_fusion.7
  494.4 3.7 all-to-all-start.4
  498.7 10.4 %all-to-all-done.4.grad_ref = bf16[8,384,128]{2,1,0:T(8,128)(2,1)S(1)} async-done(((bf16[8,384,128]{2,1,0:T(8,128)(2,1)}), bf16[8,384,128]{2,1,0:T(8,128)(2,1)S(1)}, u32[]{:S(2)}, u32[]{:S(2)}) %all-to-all-start.4) | async-done | bytes 786464 | tf_op jit(solution)/shard_map/all_to_all | solution.py:1326
  509.9 36.7 %self_backward.1 = (bf16[2,384,384]{2,1,0:T(8,128)(2,1)}, bf16[4,384,384]{2,1,0:T(8,128)(2,1)}, bf16[2,384,384]{2,1,0:T(8,128)(2,1)}) custom-call(s32[8]{0:T(128)} %stack.105.lines_ref, s32[2]{0:T(128)} %bitcast.437, bf16[2,384,384]{2,1,0:T(8,128)(2,1)} %get-tuple-element.106.near_ref, bf16[4,384,384]{2,1,0:T(8,128)(2,1)} %get-tuple-element.107.next_ref, ...), custom_call_target="tpu_custom_call" | custom-call | flops 33300000768 | bytes 74000000 | tf_op jit(solution)/shard_map/self_backward/pallas_call | solution.py:961
  546.7 4.1 collective-permute-start.38
  552.7 3.1 convolution_convert_fusion
  566.9 22.6 %collective-permute-done.41 = bf16[192,1024]{1,0:T(8,128)(2,1)S(1)} collective-permute-done((bf16[192,1024]{1,0:T(8,128)(2,1)S(1)}, bf16[192,1024]{1,0:T(8,128)(2,1)S(1)}, u32[]{:S(2)}, u32[]{:S(2)}) %collective-permute-start.41) | collective-permute-done | bytes 393248 | tf_op jit(solution)/shard_map/ppermute | solution.py:1224
  596.3 25.2 %collective-permute-done.45 = bf16[384,1024]{1,0:T(8,128)(2,1)S(1)} collective-permute-done((bf16[384,1024]{1,0:T(8,128)(2,1)S(1)}, bf16[384,1024]{1,0:T(8,128)(2,1)S(1)}, u32[]{:S(2)}, u32[]{:S(2)}) %collective-permute-start.45) | collective-permute-done | bytes 786464 | tf_op jit(solution)/shard_map/ppermute | solution.py:1227
  626.1 6.7 collective-permute-start.47
  644.7 36.3 %all-to-all-start.5 = ((bf16[8,128,640]{2,1,0:T(8,128)(2,1)}), bf16[8,128,640]{2,1,0:T(8,128)(2,1)}, u32[]{:S(2)}, u32[]{:S(2)}) async-start(bf16[8,128,640]{2,1,0:T(8,128)(2,1)} %bitcast.131), calls=%async_computation.6 | async-start | bytes 2621440 | tf_op jit(solution)/shard_map/all_to_all | solution.py:1326
  681.0 6.0 collective-permute-start.50
  699.1 3.9 settle_columns.1
  703.0 3.7 collective-permute-start.49
  707.4 3.3 all-to-all-start.6
  712.1 20.9 %all-to-all-done.6 = f32[8,2,128]{2,1,0:T(2,128)S(1)} async-done(((f32[8,2,128]{2,1,0:T(2,128)}), f32[8,2,128]{2,1,0:T(2,128)S(1)}, u32[]{:S(2)}, u32[]{:S(2)}) %all-to-all-start.6) | async-done | bytes 8224 | tf_op jit(solution)/shard_map/all_to_all | solution.py:1326
  733.0 5.6 collective-permute-start.48
  744.4 3.1 settle_heads.1
  (477 shorter events, 186.2 us)
Async XLA Ops:
  7.2 75.7 %copy-start = (bf16[1024,1024]{1,0:T(8,128)(2,1)S(1)}, bf16[1024,1024]{1,0:T(8,128)(2,1)}, u32[]{:S(2)}) copy-start(bf16[1024,1024]{1,0:T(8,128)(2,1)} %param.56) | copy-start | bytes 6291460
  26.5 47.7 %all-to-all-start = ((bf16[8,136,384]{2,1,0:T(8,128)(2,1)}), bf16[8,136,384]{2,1,0:T(8,128)(2,1)}, u32[]{:S(2)}, u32[]{:S(2)}) async-start(bf16[8,136,384]{2,1,0:T(8,128)(2,1)} %bitcast.9), calls=%async_computation | async-start | bytes 1671168 | tf_op jit(solution)/shard_map/all_to_all | solution.py:1326
  32.9 41.3 %copy-start.67 = (s32[2]{0:T(128)S(1)}, s32[2]{0:T(128)}, u32[]{:S(2)}) copy-start(s32[2]{0:T(128)} %param.33) | copy-start | bytes 28
  32.9 173.5 %all-gather.5.cloned.1.call-start = ((), (), s32[]{:S(2)}) async-start(), calls=%async_computation.9 | async-start | bytes 10813440 | tf_op jit(solution)/shard_map/all_gather | solution.py:1498
  33.9 40.2 %collective-permute-start = (bf16[448,1024]{1,0:T(8,128)(2,1)}, bf16[448,1024]{1,0:T(8,128)(2,1)S(1)}, u32[]{:S(2)}, u32[]{:S(2)}) collective-permute-start(bf16[448,1024]{1,0:T(8,128)(2,1)} %pad_maximum_fusion.11), channel_id=1, source_target_pairs={{0,0},{2,16},{4,8},{6,24},{8,4},{10,20},{12,12},{14,28},{16,2},{18... | collective-permute-start | bytes 2752520 | tf_op jit(solution)/shard_map/ppermute | solution.py:1270
  74.2 10.8 %collective-permute-start.1 = (s32[2]{0:T(128)S(1)}, s32[2]{0:T(128)S(1)}, u32[]{:S(2)}, u32[]{:S(2)}) collective-permute-start(s32[2]{0:T(128)S(1)} %copy-done.67), channel_id=1, source_target_pairs={{0,0},{2,8},{4,16},{6,24},{8,4},{10,12},{12,20},{14,28},{16,2},{18... | collective-permute-start | bytes 32 | tf_op jit(solution)/shard_map/ppermute | solution.py:1423
  85.7 46.4 %collective-permute-start.2 = (bf16[448,1024]{1,0:T(8,128)(2,1)S(1)}, bf16[448,1024]{1,0:T(8,128)(2,1)}, u32[]{:S(2)}, u32[]{:S(2)}) collective-permute-start(bf16[448,1024]{1,0:T(8,128)(2,1)S(1)} %collective-permute-done.refs_0_), channel_id=1, source_target_pairs={{0,8},{1,9},{8,0},{9,1},{16,24},{17,25},{24,16},{25,17},{2,10},{3,... | collective-permute-start | bytes 2752520 | tf_op jit(solution)/shard_map/ppermute | solution.py:1230
  85.7 37.9 %collective-permute-start.3 = (bf16[448,1024]{1,0:T(8,128)(2,1)S(1)}, bf16[448,1024]{1,0:T(8,128)(2,1)}, u32[]{:S(2)}, u32[]{:S(2)}) collective-permute-start(bf16[448,1024]{1,0:T(8,128)(2,1)S(1)} %collective-permute-done.refs_0_), channel_id=1, source_target_pairs={{0,16},{16,17},{17,1},{1,0},{8,24},{24,25},{25,9},{9,8},{2,18},{18... | collective-permute-start | bytes 2752520 | tf_op jit(solution)/shard_map/ppermute | solution.py:1224
  91.9 35.8 %collective-permute-start.4 = (bf16[448,1024]{1,0:T(8,128)(2,1)S(1)}, bf16[448,1024]{1,0:T(8,128)(2,1)}, u32[]{:S(2)}, u32[]{:S(2)}) collective-permute-start(bf16[448,1024]{1,0:T(8,128)(2,1)S(1)} %collective-permute-done.refs_0_), channel_id=1, source_target_pairs={{16,0},{17,16},{1,17},{0,1},{24,8},{25,24},{9,25},{8,9},{18,2},{19... | collective-permute-start | bytes 2752520 | tf_op jit(solution)/shard_map/ppermute | solution.py:1227
  93.6 28.5 %all-to-all-start.2 = ((bf16[2,128,1024]{1,2,0:T(8,128)(2,1)}), bf16[2,128,1024]{1,2,0:T(8,128)(2,1)S(1)}, u32[]{:S(2)}, u32[]{:S(2)}) async-start(bf16[2,128,1024]{1,2,0:T(8,128)(2,1)} %bitcast.47), calls=%async_computation.2 | async-start | bytes 1048576 | tf_op jit(solution)/shard_map/all_to_all | solution.py:1326
  97.1 177.0 %all-gather.7.cloned.1.call-start = ((), (), s32[]{:S(2)}) async-start(), calls=%async_computation.10 | async-start | bytes 5242880 | tf_op jit(solution)/shard_map/all_gather | solution.py:1524
  99.8 94.5 %collective-permute-start.11 = (bf16[384,1024]{1,0:T(8,128)(2,1)}, bf16[384,1024]{1,0:T(8,128)(2,1)}, u32[]{:S(2)}, u32[]{:S(2)}) collective-permute-start(bf16[384,1024]{1,0:T(8,128)(2,1)} %pad_maximum_fusion.12), channel_id=1, source_target_pairs={{0,0},{2,16},{4,8},{6,24},{8,4},{10,20},{12,12},{14,28},{16,2},{18... | collective-permute-start | bytes 2359304 | tf_op jit(solution)/shard_map/ppermute | solution.py:1270
  124.6 22.8 %collective-permute-start.7 = (bf16[224,1024]{1,0:T(8,128)(2,1)S(1)}, bf16[224,1024]{1,0:T(8,128)(2,1)S(1)}, u32[]{:S(2)}, u32[]{:S(2)}) collective-permute-start(bf16[224,1024]{1,0:T(8,128)(2,1)S(1)} %slice.725), channel_id=1, source_target_pairs={{0,16},{16,17},{17,1},{1,0},{8,24},{24,25},{25,9},{9,8},{2,18},{18... | collective-permute-start | bytes 1376264 | tf_op jit(solution)/shard_map/ppermute | solution.py:1224
  128.8 18.7 %collective-permute-start.8 = (bf16[224,1024]{1,0:T(8,128)(2,1)S(1)}, bf16[224,1024]{1,0:T(8,128)(2,1)S(1)}, u32[]{:S(2)}, u32[]{:S(2)}) collective-permute-start(bf16[224,1024]{1,0:T(8,128)(2,1)S(1)} %slice.726), channel_id=1, source_target_pairs={{16,0},{17,16},{1,17},{0,1},{24,8},{25,24},{9,25},{8,9},{18,2},{19... | collective-permute-start | bytes 1376264 | tf_op jit(solution)/shard_map/ppermute | solution.py:1227
  129.1 19.6 %collective-permute-start.5 = (bf16[448,1024]{1,0:T(8,128)(2,1)}, bf16[448,1024]{1,0:T(8,128)(2,1)S(1)}, u32[]{:S(2)}, u32[]{:S(2)}) collective-permute-start(bf16[448,1024]{1,0:T(8,128)(2,1)} %collective-permute-done.3.refs_0_), channel_id=1, source_target_pairs={{0,8},{1,9},{8,0},{9,1},{16,24},{17,25},{24,16},{25,17},{2,10},{3,... | collective-permute-start | bytes 2752520 | tf_op jit(solution)/shard_map/ppermute | solution.py:1230
  132.1 16.6 %collective-permute-start.6 = (bf16[448,1024]{1,0:T(8,128)(2,1)}, bf16[448,1024]{1,0:T(8,128)(2,1)S(1)}, u32[]{:S(2)}, u32[]{:S(2)}) collective-permute-start(bf16[448,1024]{1,0:T(8,128)(2,1)} %collective-permute-done.4.refs_1_), channel_id=1, source_target_pairs={{0,8},{1,9},{8,0},{9,1},{16,24},{17,25},{24,16},{25,17},{2,10},{3,... | collective-permute-start | bytes 2752520 | tf_op jit(solution)/shard_map/ppermute | solution.py:1230
  147.6 10.3 %collective-permute-start.9 = (bf16[448,1024]{1,0:T(8,128)(2,1)S(1)}, bf16[448,1024]{1,0:T(8,128)(2,1)S(1)}, u32[]{:S(2)}, u32[]{:S(2)}) collective-permute-start(bf16[448,1024]{1,0:T(8,128)(2,1)S(1)} %constant_dynamic-update-slice_fusion.refs_0_), channel_id=1, source_target_pairs={{0,8},{1,9},{8,0},{9,1},{16,24},{17,25},{24,16},{25,17},{2,10},{3,... | collective-permute-start | bytes 2752520 | tf_op jit(solution)/shard_map/ppermute | solution.py:1230
  188.1 17.1 %all-to-all-start.1 = ((bf16[8,384,128]{2,1,0:T(8,128)(2,1)}), bf16[8,384,128]{2,1,0:T(8,128)(2,1)S(1)}, u32[]{:S(2)}, u32[]{:S(2)}) async-start(bf16[8,384,128]{2,1,0:T(8,128)(2,1)} %get-tuple-element.109), calls=%async_computation.1 | async-start | bytes 1572864 | tf_op jit(solution)/shard_map/all_to_all | solution.py:1326
  194.3 40.0 %collective-permute-start.12 = (bf16[384,1024]{1,0:T(8,128)(2,1)}, bf16[384,1024]{1,0:T(8,128)(2,1)}, u32[]{:S(2)}, u32[]{:S(2)}) collective-permute-start(bf16[384,1024]{1,0:T(8,128)(2,1)} %collective-permute-done.11.refs_2_), channel_id=1, source_target_pairs={{0,16},{16,17},{17,1},{1,0},{8,24},{24,25},{25,9},{9,8},{2,18},{18... | collective-permute-start | bytes 2359304 | tf_op jit(solution)/shard_map/ppermute | solution.py:1224
  195.7 38.5 %collective-permute-start.13 = (bf16[384,1024]{1,0:T(8,128)(2,1)}, bf16[384,1024]{1,0:T(8,128)(2,1)}, u32[]{:S(2)}, u32[]{:S(2)}) collective-permute-start(bf16[384,1024]{1,0:T(8,128)(2,1)} %collective-permute-done.11.refs_2_), channel_id=1, source_target_pairs={{16,0},{17,16},{1,17},{0,1},{24,8},{25,24},{9,25},{8,9},{18,2},{19... | collective-permute-start | bytes 2359304 | tf_op jit(solution)/shard_map/ppermute | solution.py:1227
  196.2 38.1 %collective-permute-start.14 = (bf16[384,1024]{1,0:T(8,128)(2,1)}, bf16[384,1024]{1,0:T(8,128)(2,1)}, u32[]{:S(2)}, u32[]{:S(2)}) collective-permute-start(bf16[384,1024]{1,0:T(8,128)(2,1)} %collective-permute-done.11.refs_2_), channel_id=1, source_target_pairs={{0,8},{1,9},{8,0},{9,1},{16,24},{17,25},{24,16},{25,17},{2,10},{3,... | collective-permute-start | bytes 2359304 | tf_op jit(solution)/shard_map/ppermute | solution.py:1230
  232.7 19.0 %collective-permute-start.16 = (bf16[384,1024]{1,0:T(8,128)(2,1)S(1)}, bf16[384,1024]{1,0:T(8,128)(2,1)S(1)}, u32[]{:S(2)}, u32[]{:S(2)}) collective-permute-start(bf16[384,1024]{1,0:T(8,128)(2,1)S(1)} %add_convert_fusion.3.refs_0_), channel_id=1, source_target_pairs={{0,16},{16,17},{17,1},{1,0},{8,24},{24,25},{25,9},{9,8},{2,18},{18... | collective-permute-start | bytes 2359304 | tf_op jit(solution)/shard_map/ppermute | solution.py:1224
  233.5 19.1 %collective-permute-start.18 = (bf16[384,1024]{1,0:T(8,128)(2,1)S(1)}, bf16[384,1024]{1,0:T(8,128)(2,1)S(1)}, u32[]{:S(2)}, u32[]{:S(2)}) collective-permute-start(bf16[384,1024]{1,0:T(8,128)(2,1)S(1)} %add_convert_fusion.3.refs_0_), channel_id=1, source_target_pairs={{16,0},{17,16},{1,17},{0,1},{24,8},{25,24},{9,25},{8,9},{18,2},{19... | collective-permute-start | bytes 2359304 | tf_op jit(solution)/shard_map/ppermute | solution.py:1227
  234.3 26.3 %collective-permute-start.23 = (bf16[384,1024]{1,0:T(8,128)(2,1)}, bf16[384,1024]{1,0:T(8,128)(2,1)S(1)}, u32[]{:S(2)}, u32[]{:S(2)}) collective-permute-start(bf16[384,1024]{1,0:T(8,128)(2,1)} %collective-permute-done.12.refs_4_), channel_id=1, source_target_pairs={{0,8},{1,9},{8,0},{9,1},{16,24},{17,25},{24,16},{25,17},{2,10},{3,... | collective-permute-start | bytes 2359304 | tf_op jit(solution)/shard_map/ppermute | solution.py:1230
  235.2 25.4 %collective-permute-start.24 = (bf16[384,1024]{1,0:T(8,128)(2,1)}, bf16[384,1024]{1,0:T(8,128)(2,1)S(1)}, u32[]{:S(2)}, u32[]{:S(2)}) collective-permute-start(bf16[384,1024]{1,0:T(8,128)(2,1)} %collective-permute-done.13.refs_5_), channel_id=1, source_target_pairs={{0,8},{1,9},{8,0},{9,1},{16,24},{17,25},{24,16},{25,17},{2,10},{3,... | collective-permute-start | bytes 2359304 | tf_op jit(solution)/shard_map/ppermute | solution.py:1230
  236.3 23.8 %collective-permute-start.21 = (bf16[192,1024]{1,0:T(8,128)(2,1)S(1)}, bf16[192,1024]{1,0:T(8,128)(2,1)S(1)}, u32[]{:S(2)}, u32[]{:S(2)}) collective-permute-start(bf16[192,1024]{1,0:T(8,128)(2,1)S(1)} %slice.593), channel_id=1, source_target_pairs={{0,16},{16,17},{17,1},{1,0},{8,24},{24,25},{25,9},{9,8},{2,18},{18... | collective-permute-start | bytes 1179656 | tf_op jit(solution)/shard_map/ppermute | solution.py:1224
  251.7 8.9 %collective-permute-start.22 = (bf16[192,1024]{1,0:T(8,128)(2,1)S(1)}, bf16[192,1024]{1,0:T(8,128)(2,1)S(1)}, u32[]{:S(2)}, u32[]{:S(2)}) collective-permute-start(bf16[192,1024]{1,0:T(8,128)(2,1)S(1)} %slice.594), channel_id=1, source_target_pairs={{16,0},{17,16},{1,17},{0,1},{24,8},{25,24},{9,25},{8,9},{18,2},{19... | collective-permute-start | bytes 1179656 | tf_op jit(solution)/shard_map/ppermute | solution.py:1227
  252.6 16.0 %collective-permute-start.17 = (bf16[192,1024]{1,0:T(8,128)(2,1)S(1)}, bf16[192,1024]{1,0:T(8,128)(2,1)S(1)}, u32[]{:S(2)}, u32[]{:S(2)}) collective-permute-start(bf16[192,1024]{1,0:T(8,128)(2,1)S(1)} %slice.748), channel_id=1, source_target_pairs={{0,16},{16,17},{17,1},{1,0},{8,24},{24,25},{25,9},{9,8},{2,18},{18... | collective-permute-start | bytes 1179656 | tf_op jit(solution)/shard_map/ppermute | solution.py:1224
  260.1 9.2 %collective-permute-start.19 = (bf16[192,1024]{1,0:T(8,128)(2,1)S(1)}, bf16[192,1024]{1,0:T(8,128)(2,1)S(1)}, u32[]{:S(2)}, u32[]{:S(2)}) collective-permute-start(bf16[192,1024]{1,0:T(8,128)(2,1)S(1)} %slice.749), channel_id=1, source_target_pairs={{16,0},{17,16},{1,17},{0,1},{24,8},{25,24},{9,25},{8,9},{18,2},{19... | collective-permute-start | bytes 1179656 | tf_op jit(solution)/shard_map/ppermute | solution.py:1227
  262.2 11.9 %collective-permute-start.25 = (bf16[384,1024]{1,0:T(8,128)(2,1)}, bf16[384,1024]{1,0:T(8,128)(2,1)}, u32[]{:S(2)}, u32[]{:S(2)}) collective-permute-start(bf16[384,1024]{1,0:T(8,128)(2,1)} %constant_dynamic-update-slice_fusion.4.refs_2_), channel_id=1, source_target_pairs={{0,8},{1,9},{8,0},{9,1},{16,24},{17,25},{24,16},{25,17},{2,10},{3,... | collective-permute-start | bytes 2359304 | tf_op jit(solution)/shard_map/ppermute | solution.py:1230
  270.1 4.8 collective-permute-start.20
  274.1 17.1 %collective-permute-start.10 = (bf16[384,1024]{1,0:T(8,128)(2,1)}, bf16[384,1024]{1,0:T(8,128)(2,1)}, u32[]{:S(2)}, u32[]{:S(2)}) collective-permute-start(bf16[384,1024]{1,0:T(8,128)(2,1)} %copy-done.40), channel_id=1, source_target_pairs={{0,8},{1,9},{8,0},{9,1},{16,24},{17,25},{24,16},{25,17},{2,10},{3,... | collective-permute-start | bytes 2359304 | tf_op jit(solution)/shard_map/ppermute | solution.py:1230
  290.3 16.6 %collective-permute-start.26 = (bf16[768,1024]{1,0:T(8,128)(2,1)}, bf16[768,1024]{1,0:T(8,128)(2,1)}, u32[]{:S(2)}, u32[]{:S(2)}) collective-permute-start(bf16[768,1024]{1,0:T(8,128)(2,1)} %slice_bitcast_fusion.2), channel_id=1, source_target_pairs={{0,8},{1,9},{8,0},{9,1},{16,24},{17,25},{24,16},{25,17},{2,10},{3,... | collective-permute-start | bytes 4718600 | tf_op jit(solution)/shard_map/ppermute | solution.py:1230
  290.7 20.0 %collective-permute-start.28 = (bf16[384,1024]{1,0:T(8,128)(2,1)}, bf16[384,1024]{1,0:T(8,128)(2,1)S(1)}, u32[]{:S(2)}, u32[]{:S(2)}) collective-permute-start(bf16[384,1024]{1,0:T(8,128)(2,1)} %copy-done.50), channel_id=1, source_target_pairs={{0,8},{1,9},{8,0},{9,1},{16,24},{17,25},{24,16},{25,17},{2,10},{3,... | collective-permute-start | bytes 2359304 | tf_op jit(solution)/shard_map/ppermute | solution.py:1230
  290.8 19.9 %collective-permute-start.29 = (bf16[384,1024]{1,0:T(8,128)(2,1)}, bf16[384,1024]{1,0:T(8,128)(2,1)S(1)}, u32[]{:S(2)}, u32[]{:S(2)}) collective-permute-start(bf16[384,1024]{1,0:T(8,128)(2,1)} %copy-done.51), channel_id=1, source_target_pairs={{0,8},{1,9},{8,0},{9,1},{16,24},{17,25},{24,16},{25,17},{2,10},{3,... | collective-permute-start | bytes 2359304 | tf_op jit(solution)/shard_map/ppermute | solution.py:1230
  306.8 65.8 %collective-permute-start.15 = (bf16[768,1024]{1,0:T(8,128)(2,1)}, bf16[768,1024]{1,0:T(8,128)(2,1)}, u32[]{:S(2)}, u32[]{:S(2)}) collective-permute-start(bf16[768,1024]{1,0:T(8,128)(2,1)} %slice_bitcast_fusion.3), channel_id=1, source_target_pairs={{0,8},{1,9},{8,0},{9,1},{16,24},{17,25},{24,16},{25,17},{2,10},{3,... | collective-permute-start | bytes 4718600 | tf_op jit(solution)/shard_map/ppermute | solution.py:1230
  309.2 30.3 %collective-permute-start.27 = (bf16[384,1024]{1,0:T(8,128)(2,1)S(1)}, bf16[384,1024]{1,0:T(8,128)(2,1)S(1)}, u32[]{:S(2)}, u32[]{:S(2)}) collective-permute-start(bf16[384,1024]{1,0:T(8,128)(2,1)S(1)} %get-tuple-element.248), channel_id=1, source_target_pairs={{0,16},{16,17},{17,1},{1,0},{8,24},{24,25},{25,9},{9,8},{2,18},{18... | collective-permute-start | bytes 2359304 | tf_op jit(solution)/shard_map/ppermute | solution.py:1224
  310.2 29.3 %collective-permute-start.32 = (bf16[384,1024]{1,0:T(8,128)(2,1)S(1)}, bf16[384,1024]{1,0:T(8,128)(2,1)S(1)}, u32[]{:S(2)}, u32[]{:S(2)}) collective-permute-start(bf16[384,1024]{1,0:T(8,128)(2,1)S(1)} %get-tuple-element.249), channel_id=1, source_target_pairs={{16,0},{17,16},{1,17},{0,1},{24,8},{25,24},{9,25},{8,9},{18,2},{19... | collective-permute-start | bytes 2359304 | tf_op jit(solution)/shard_map/ppermute | solution.py:1227
  338.5 20.5 %collective-permute-start.30 = (bf16[2,768,1024]{2,1,0:T(8,128)(2,1)}, bf16[2,768,1024]{2,1,0:T(8,128)(2,1)}, u32[]{:S(2)}, u32[]{:S(2)}) collective-permute-start(bf16[2,768,1024]{2,1,0:T(8,128)(2,1)} %slice.599), channel_id=1, source_target_pairs={{0,8},{1,9},{8,0},{9,1},{16,24},{17,25},{24,16},{25,17},{2,10},{3,... | collective-permute-start | bytes 9437192 | tf_op jit(solution)/shard_map/ppermute | solution.py:1230
  364.7 36.1 %collective-permute-start.33 = (bf16[768,1024]{1,0:T(8,128)(2,1)S(1)}, bf16[768,1024]{1,0:T(8,128)(2,1)S(1)}, u32[]{:S(2)}, u32[]{:S(2)}) collective-permute-start(bf16[768,1024]{1,0:T(8,128)(2,1)S(1)} %pad_maximum_fusion.7), channel_id=1, source_target_pairs={{16,0},{17,16},{1,17},{0,1},{24,8},{25,24},{9,25},{8,9},{18,2},{19... | collective-permute-start | bytes 4718600 | tf_op jit(solution)/shard_map/ppermute | solution.py:1227
  365.0 35.8 %collective-permute-start.31 = (bf16[768,1024]{1,0:T(8,128)(2,1)S(1)}, bf16[768,1024]{1,0:T(8,128)(2,1)S(1)}, u32[]{:S(2)}, u32[]{:S(2)}) collective-permute-start(bf16[768,1024]{1,0:T(8,128)(2,1)S(1)} %pad_maximum_fusion.6), channel_id=1, source_target_pairs={{0,16},{16,17},{17,1},{1,0},{8,24},{24,25},{25,9},{9,8},{2,18},{18... | collective-permute-start | bytes 4718600 | tf_op jit(solution)/shard_map/ppermute | solution.py:1224
  411.9 65.7 %all-to-all-start.3 = ((bf16[8,128,1024]{2,1,0:T(8,128)(2,1)}), bf16[8,128,1024]{2,1,0:T(8,128)(2,1)}, u32[]{:S(2)}, u32[]{:S(2)}) async-start(bf16[8,128,1024]{2,1,0:T(8,128)(2,1)} %bitcast.328), calls=%async_computation.3 | async-start | bytes 4194304 | tf_op jit(solution)/shard_map/all_to_all | solution.py:1326
  417.2 206.3 %reduce-scatter.2.cloned.1.call-start = ((), (), s32[]{:S(2)}) async-start(), calls=%async_computation.8 | async-start | bytes 10911744 | tf_op jit(solution)/shard_map/reduce_scatter | solution.py:1632
  419.2 43.4 %collective-permute-start.34 = (bf16[272,1024]{1,0:T(8,128)(2,1)S(1)}, bf16[272,1024]{1,0:T(8,128)(2,1)S(1)}, u32[]{:S(2)}, u32[]{:S(2)}) collective-permute-start(bf16[272,1024]{1,0:T(8,128)(2,1)S(1)} %get-tuple-element.225), channel_id=1, source_target_pairs={{0,0},{2,16},{4,8},{6,24},{8,2},{10,18},{12,10},{14,26},{16,4},{18... | collective-permute-start | bytes 1671176 | tf_op jit(solution)/shard_map/ppermute | solution.py:1296
  423.8 50.3 %collective-permute-start.35 = (bf16[272,1024]{1,0:T(8,128)(2,1)S(1)}, bf16[272,1024]{1,0:T(8,128)(2,1)}, u32[]{:S(2)}, u32[]{:S(2)}) collective-permute-start(bf16[272,1024]{1,0:T(8,128)(2,1)S(1)} %get-tuple-element.224), channel_id=1, source_target_pairs={{0,2},{2,18},{4,10},{6,26},{8,0},{10,16},{12,8},{14,24},{16,6},{18... | collective-permute-start | bytes 1671176 | tf_op jit(solution)/shard_map/ppermute | solution.py:1296
  423.9 50.3 %collective-permute-start.36 = (bf16[272,1024]{1,0:T(8,128)(2,1)S(1)}, bf16[272,1024]{1,0:T(8,128)(2,1)}, u32[]{:S(2)}, u32[]{:S(2)}) collective-permute-start(bf16[272,1024]{1,0:T(8,128)(2,1)S(1)} %get-tuple-element.223), channel_id=1, source_target_pairs={{0,4},{2,20},{4,12},{6,28},{8,6},{10,22},{12,14},{14,30},{16,0},{1... | collective-permute-start | bytes 1671176 | tf_op jit(solution)/shard_map/ppermute | solution.py:1296
  427.3 50.3 %collective-permute-start.37 = (bf16[272,1024]{1,0:T(8,128)(2,1)S(1)}, bf16[272,1024]{1,0:T(8,128)(2,1)}, u32[]{:S(2)}, u32[]{:S(2)}) collective-permute-start(bf16[272,1024]{1,0:T(8,128)(2,1)S(1)} %get-tuple-element.222), channel_id=1, source_target_pairs={{0,6},{2,22},{4,14},{6,30},{8,4},{10,20},{12,12},{14,28},{16,2},{1... | collective-permute-start | bytes 1671176 | tf_op jit(solution)/shard_map/ppermute | solution.py:1296
  494.4 14.7 %all-to-all-start.4 = ((bf16[8,384,128]{2,1,0:T(8,128)(2,1)}), bf16[8,384,128]{2,1,0:T(8,128)(2,1)S(1)}, u32[]{:S(2)}, u32[]{:S(2)}) async-start(bf16[8,384,128]{2,1,0:T(8,128)(2,1)} %bitcast.79), calls=%async_computation.4 | async-start | bytes 1572864 | tf_op jit(solution)/shard_map/all_to_all | solution.py:1326
  509.9 42.8 %copy-start.37 = (bf16[8,128,384]{2,1,0:T(8,128)(2,1)S(1)}, bf16[8,128,384]{2,1,0:T(8,128)(2,1)}, u32[]{:S(2)}) copy-start(bf16[8,128,384]{2,1,0:T(8,128)(2,1)} %slice.562) | copy-start | bytes 2359300
  546.7 48.0 %collective-permute-start.38 = (bf16[384,1024]{1,0:T(8,128)(2,1)S(1)}, bf16[384,1024]{1,0:T(8,128)(2,1)S(1)}, u32[]{:S(2)}, u32[]{:S(2)}) collective-permute-start(bf16[384,1024]{1,0:T(8,128)(2,1)S(1)} %copy-done.32), channel_id=1, source_target_pairs={{0,0},{2,16},{4,8},{6,24},{8,4},{10,20},{12,12},{14,28},{16,2},{18... | collective-permute-start | bytes 2359304 | tf_op jit(solution)/shard_map/ppermute | solution.py:1278
  550.8 72.7 %collective-permute-start.46 = (bf16[8,128,1024]{2,1,0:T(8,128)(2,1)}, bf16[8,128,1024]{2,1,0:T(8,128)(2,1)}, u32[]{:S(2)}, u32[]{:S(2)}) collective-permute-start(bf16[8,128,1024]{2,1,0:T(8,128)(2,1)} %all-to-all-done.3), channel_id=1, source_target_pairs={{0,2},{2,18},{4,10},{6,26},{8,6},{10,22},{12,14},{14,30},{16,0},{1... | collective-permute-start | bytes 6291464 | tf_op jit(solution)/shard_map/ppermute | solution.py:1286
  556.2 9.4 %collective-permute-start.42 = (bf16[2,384,1024]{2,1,0:T(8,128)(2,1)S(1)}, bf16[2,384,1024]{2,1,0:T(8,128)(2,1)S(1)}, u32[]{:S(2)}, u32[]{:S(2)}) collective-permute-start(bf16[2,384,1024]{2,1,0:T(8,128)(2,1)S(1)} %bitcast.366), channel_id=1, source_target_pairs={{0,8},{1,9},{8,0},{9,1},{16,24},{17,25},{24,16},{25,17},{2,10},{3,... | collective-permute-start | bytes 4718600 | tf_op jit(solution)/shard_map/ppermute | solution.py:1230
  558.0 6.1 collective-permute-start.40
  560.5 35.7 %collective-permute-start.39 = (bf16[384,1024]{1,0:T(8,128)(2,1)S(1)}, bf16[384,1024]{1,0:T(8,128)(2,1)S(1)}, u32[]{:S(2)}, u32[]{:S(2)}) collective-permute-start(bf16[384,1024]{1,0:T(8,128)(2,1)S(1)} %slice.766), channel_id=1, source_target_pairs={{0,8},{1,9},{8,0},{9,1},{16,24},{17,25},{24,16},{25,17},{2,10},{3,... | collective-permute-start | bytes 2359304 | tf_op jit(solution)/shard_map/ppermute | solution.py:1230
  564.5 25.0 %collective-permute-start.41 = (bf16[192,1024]{1,0:T(8,128)(2,1)S(1)}, bf16[192,1024]{1,0:T(8,128)(2,1)S(1)}, u32[]{:S(2)}, u32[]{:S(2)}) collective-permute-start(bf16[192,1024]{1,0:T(8,128)(2,1)S(1)} %get-tuple-element.254), channel_id=1, source_target_pairs={{0,16},{16,17},{17,1},{1,0},{8,24},{24,25},{25,9},{9,8},{2,18},{18... | collective-permute-start | bytes 1179656 | tf_op jit(solution)/shard_map/ppermute | solution.py:1224
  565.5 24.0 %collective-permute-start.44 = (bf16[192,1024]{1,0:T(8,128)(2,1)S(1)}, bf16[192,1024]{1,0:T(8,128)(2,1)S(1)}, u32[]{:S(2)}, u32[]{:S(2)}) collective-permute-start(bf16[192,1024]{1,0:T(8,128)(2,1)S(1)} %get-tuple-element.255), channel_id=1, source_target_pairs={{16,0},{17,16},{1,17},{0,1},{24,8},{25,24},{9,25},{8,9},{18,2},{19... | collective-permute-start | bytes 1179656 | tf_op jit(solution)/shard_map/ppermute | solution.py:1227
  589.9 31.6 %collective-permute-start.45 = (bf16[384,1024]{1,0:T(8,128)(2,1)S(1)}, bf16[384,1024]{1,0:T(8,128)(2,1)S(1)}, u32[]{:S(2)}, u32[]{:S(2)}) collective-permute-start(bf16[384,1024]{1,0:T(8,128)(2,1)S(1)} %pad_maximum_fusion.14), channel_id=1, source_target_pairs={{16,0},{17,16},{1,17},{0,1},{24,8},{25,24},{9,25},{8,9},{18,2},{19... | collective-permute-start | bytes 2359304 | tf_op jit(solution)/shard_map/ppermute | solution.py:1227
  591.6 29.9 %collective-permute-start.43 = (bf16[384,1024]{1,0:T(8,128)(2,1)S(1)}, bf16[384,1024]{1,0:T(8,128)(2,1)S(1)}, u32[]{:S(2)}, u32[]{:S(2)}) collective-permute-start(bf16[384,1024]{1,0:T(8,128)(2,1)S(1)} %pad_maximum_fusion.13), channel_id=1, source_target_pairs={{0,16},{16,17},{17,1},{1,0},{8,24},{24,25},{25,9},{9,8},{2,18},{18... | collective-permute-start | bytes 2359304 | tf_op jit(solution)/shard_map/ppermute | solution.py:1224
  626.1 114.2 %collective-permute-start.47 = (bf16[848,1024]{1,0:T(8,128)(2,1)S(1)}, bf16[848,1024]{1,0:T(8,128)(2,1)S(1)}, u32[]{:S(2)}, u32[]{:S(2)}) collective-permute-start(bf16[848,1024]{1,0:T(8,128)(2,1)S(1)} %pad_maximum_fusion.5), channel_id=1, source_target_pairs={{0,0},{2,16},{4,8},{6,24},{8,4},{10,20},{12,12},{14,28},{16,2},{18... | collective-permute-start | bytes 5210120 | tf_op jit(solution)/shard_map/ppermute | solution.py:1278
  644.7 58.3 %all-to-all-start.5 = ((bf16[8,128,640]{2,1,0:T(8,128)(2,1)}), bf16[8,128,640]{2,1,0:T(8,128)(2,1)}, u32[]{:S(2)}, u32[]{:S(2)}) async-start(bf16[8,128,640]{2,1,0:T(8,128)(2,1)} %bitcast.131), calls=%async_computation.6 | async-start | bytes 2621440 | tf_op jit(solution)/shard_map/all_to_all | solution.py:1326
  681.0 57.5 %collective-permute-start.50 = (f32[3,128]{1,0:T(4,128)S(1)}, f32[3,128]{1,0:T(4,128)S(1)}, u32[]{:S(2)}, u32[]{:S(2)}) collective-permute-start(f32[3,128]{1,0:T(4,128)S(1)} %pad_maximum_fusion.20), channel_id=1, source_target_pairs={{0,0},{1,1},{2,16},{3,17},{4,8},{5,9},{6,24},{7,25},{8,2},{9,3},{1... | collective-permute-start | bytes 4616 | tf_op jit(solution)/shard_map/ppermute | solution.py:1312
  703.0 41.4 %collective-permute-start.49 = (bf16[8,128,640]{2,1,0:T(8,128)(2,1)}, bf16[8,128,640]{2,1,0:T(8,128)(2,1)}, u32[]{:S(2)}, u32[]{:S(2)}) collective-permute-start(bf16[8,128,640]{2,1,0:T(8,128)(2,1)} %all-to-all-done.5), channel_id=1, source_target_pairs={{0,2},{2,18},{4,10},{6,26},{8,6},{10,22},{12,14},{14,30},{16,0},{1... | collective-permute-start | bytes 3932168 | tf_op jit(solution)/shard_map/ppermute | solution.py:1286
  707.4 25.6 %all-to-all-start.6 = ((f32[8,2,128]{2,1,0:T(2,128)}), f32[8,2,128]{2,1,0:T(2,128)S(1)}, u32[]{:S(2)}, u32[]{:S(2)}) async-start(f32[8,2,128]{2,1,0:T(2,128)} %copy.183), calls=%async_computation.7 | async-start | bytes 16384 | tf_op jit(solution)/shard_map/all_to_all | solution.py:1326
  733.0 6.8 collective-permute-start.48
  (80 other events, 508.6 us)
Sparse Core Ops, SparseCore 0:
  74.3 113.5 all-gather.4
  190.1 78.9 all-gather.6
  490.3 96.1 reduce-scatter.1

commit v3 on v2

--- a/solution.py
+++ b/solution.py
@@ -1068,16 +1068,18 @@
 
 
 def cross_forward_kernel(probe_ref, lookup_ref, content_ref, out_ref, lse_ref):
-    query = split_heads(probe_ref[...] * jnp.bfloat16(HD**-0.5))
-    key = lookup_ref[...]
-    values = split_heads(content_ref[...], 1.0)
-    rows = query[0].shape[0]
+    rows = probe_ref.shape[0]
     start = (jnp.full((rows, 1), floor_value, jnp.float32), jnp.zeros((rows, PAIR), jnp.float32))
-    states = [fold(start, query[side], key, values[side]) for side in range(2)]
-    result, lse0, lse1 = close(*states)
-    out_ref[...] = result
-    lse_ref[0, 0:1, :] = lse0
-    lse_ref[0, 1:2, :] = lse1
+    for pair in range(lse_ref.shape[0]):
+        columns = slice(pair * PAIR, (pair + 1) * PAIR)
+        query = split_heads(probe_ref[:, columns] * jnp.bfloat16(HD**-0.5))
+        key = lookup_ref[:, columns]
+        values = split_heads(content_ref[:, columns], 1.0)
+        states = [fold(start, query[side], key, values[side]) for side in range(2)]
+        result, lse0, lse1 = close(*states)
+        out_ref[:, columns] = result
+        lse_ref[pair, 0:1, :] = lse0
+        lse_ref[pair, 1:2, :] = lse1
 
 
 def cross_backward_kernel(
@@ -1123,8 +1125,8 @@
     dcontent_ref[...] = dcontent
 
 
-def pair_block(rows):
-    return pl.BlockSpec((rows, PAIR), lambda at: (0, at))
+def pair_block(rows, pairs=1):
+    return pl.BlockSpec((rows, pairs * PAIR), lambda at: (0, at))
 
 
 def cross_forward(probes, lookups, contents):
@@ -1133,13 +1135,13 @@
     pairs = width // PAIR
     return pl.pallas_call(
         cross_forward_kernel,
-        grid=(pairs,),
+        grid=(pairs // 2,),
         out_shape=(
             jax.ShapeDtypeStruct((rows, width), jnp.float32),
             jax.ShapeDtypeStruct((pairs, 2, rows), jnp.float32),
         ),
-        in_specs=[pair_block(rows), pair_block(memory), pair_block(memory)],
-        out_specs=(pair_block(rows), pl.BlockSpec((1, 2, rows), lambda at: (at, 0, 0))),
+        in_specs=[pair_block(rows, 2), pair_block(memory, 2), pair_block(memory, 2)],
+        out_specs=(pair_block(rows, 2), pl.BlockSpec((2, 2, rows), lambda at: (at, 0, 0))),
         compiler_params=pltpu.CompilerParams(vmem_limit_bytes=VMEM_BYTES),
         cost_estimate=cost(10),
         name="cross_forward",

time: 767 us -> 767 us (level)
  transfers between devices with their start and end apart: 61 -> 61, of which waited for: 20 -> 19; matrix products, arithmetic and copies ran while one was open for 20% -> 20% of each run, Pallas kernels for 20% -> 20%
where the time goes in v3:
time: 767 us; the launch traced here: 754 us
  waiting for transfers between devices  218 us (28%)
  Pallas kernels  155 us (20%)
  starting transfers between devices  151 us (20%)
  local copies, waits for them, and re-layouts  114 us (15%)
  matrix products  55.4 us (7%)
  other arithmetic  46.1 us (6%)
  between operations  16.2 us (2%)
    all_to_all x7, starting transfers between devices, exchange(): return lax.all_to_all(values, axes, split_axis=0, concat_axis=0, tiled=True)  63.7 us
    all_to_all x7, waiting for transfers between devices, exchange(): return lax.all_to_all(values, axes, split_axis=0, concat_axis=0, tiled=True)  54.7 us
    ppermute x10, waiting for transfers between devices, up(): return lax.ppermute(values, ROLE_AXES, self.forward)  54.4 us
    ppermute x10, waiting for transfers between devices, down(): return lax.ppermute(values, ROLE_AXES, self.reverse)  53.8 us
    unnamed x201, local copies, waits for them, and re-layouts  50.3 us
    pallas_call x3, Pallas kernels, feed(): pl.pallas_call(functools.partial(feed_kernel, count), grid=(count,), in_s...  47.5 us
    pallas_call x1, Pallas kernels, self_backward(): pl.pallas_call(functools.partial(self_backward_kernel, prompt_all), out_s...  36.8 us
    ppermute x2, waiting for transfers between devices, enter(): return lax.ppermute(values, (GRP, BLK), moves)  30.7 us
  transfers between devices with their start and end apart: 61, of which 19 were waited for; matrix products, arithmetic and copies ran while one was open for 20% of the time, Pallas kernels for 20%

profile of v3, /device:TPU:1, one launch (start us, length us, event | category | flops | bytes accessed | tf_op | source)
XLA Modules:
  0.0 754.3 jit_solution(17343923284800979045)
XLA Ops:
  26.5 6.4 all-to-all-start
  33.9 5.3 collective-permute-start
  43.5 30.7 %collective-permute-done.refs_0_ = bf16[448,1024]{1,0:T(8,128)(2,1)S(1)} collective-permute-done((bf16[448,1024]{1,0:T(8,128)(2,1)}, bf16[448,1024]{1,0:T(8,128)(2,1)S(1)}, u32[]{:S(2)}, u32[]{:S(2)}) %collective-permute-start) | collective-permute-done | bytes 917536 | tf_op jit(solution)/shard_map/ppermute | solution.py:1272
  76.3 4.1 copy.159
  85.7 6.2 collective-permute-start.3
  93.6 3.5 all-to-all-start.2
  99.8 6.1 collective-permute-start.11
  106.1 16.0 %all-to-all-done.2 = bf16[2,128,1024]{1,2,0:T(8,128)(2,1)S(1)} async-done(((bf16[2,128,1024]{1,2,0:T(8,128)(2,1)}), bf16[2,128,1024]{1,2,0:T(8,128)(2,1)S(1)}, u32[]{:S(2)}, u32[]{:S(2)}) %all-to-all-start.2) | async-done | bytes 524320 | tf_op jit(solution)/shard_map/all_to_all | solution.py:1328
  124.6 3.1 collective-permute-start.7
  129.1 3.0 collective-permute-start.5
  134.9 4.4 project.3
  139.3 8.2 %collective-permute-done.7 = bf16[224,1024]{1,0:T(8,128)(2,1)S(1)} collective-permute-done((bf16[224,1024]{1,0:T(8,128)(2,1)S(1)}, bf16[224,1024]{1,0:T(8,128)(2,1)S(1)}, u32[]{:S(2)}, u32[]{:S(2)}) %collective-permute-start.7) | collective-permute-done | bytes 458784 | tf_op jit(solution)/shard_map/ppermute | solution.py:1226
  150.5 7.3 project.4
  158.8 4.4 project.5
  163.2 24.9 %self_forward.1 = (f32[3072,128]{1,0:T(8,128)}, bf16[8,384,128]{2,1,0:T(8,128)(2,1)}, f32[6,2,512]{2,1,0:T(2,128)}) custom-call(s32[8]{0:T(128)} %stack.105.lines_ref, s32[2]{0:T(128)} %bitcast.436, bf16[2,384,384]{2,1,0:T(8,128)(2,1)} %get-tuple-element.106.near_ref, bf16[4,384,384]{2,1,0:T(8,128)(2,1)} %get-tuple-element.107.next_ref, ...), custom_call_target="tpu_custom_call" | custom-call | flops 22499999744 | bytes 50000000 | tf_op jit(solution)/shard_map/self_forward/pallas_call | solution.py:941
  188.1 5.3 all-to-all-start.1
  197.8 7.4 all-to-all-done.1
  206.4 4.9 fusion.39
  212.8 2.7 convolution_convert_fusion.6.lookup_ref
  219.8 9.4 %cross_forward.1 = (f32[384,1024]{1,0:T(8,128)}, f32[8,2,384]{2,1,0:T(2,128)}) custom-call(bf16[384,1024]{1,0:T(8,128)(2,1)} %add_convert_fusion.4.probe_ref, bf16[512,1024]{1,0:T(8,128)(2,1)} %convolution_convert_fusion.6.lookup_ref, bf16[512,1024]{1,0:T(8,128)(2,1)} %add_convert_fusion.1.content_ref), custom_call_target="tpu_custom_call" | custom-call | flops 8999999488 | bytes 20000000 | tf_op jit(solution)/shard_map/cross_forward/pallas_call | solution.py:1136
  237.7 13.7 %collective-permute-done.16.refs_0_ = bf16[384,1024]{1,0:T(8,128)(2,1)S(1)} collective-permute-done((bf16[384,1024]{1,0:T(8,128)(2,1)S(1)}, bf16[384,1024]{1,0:T(8,128)(2,1)S(1)}, u32[]{:S(2)}, u32[]{:S(2)}) %collective-permute-start.16) | collective-permute-done | bytes 786464 | tf_op jit(solution)/shard_map/ppermute | solution.py:1226
  253.2 6.6 collective-permute-done.21
  261.8 3.2 collective-permute-start.25
  265.0 3.2 collective-permute-done.17
  274.6 12.7 %feed.4 = (bf16[2,768,1024]{2,1,0:T(8,128)(2,1)}, bf16[2,384,1024]{2,1,0:T(8,128)(2,1)}, bf16[2,384,1024]{2,1,0:T(8,128)(2,1)}, bf16[2,384,1024]{2,1,0:T(8,128)(2,1)}, bf16[2,384,1024]{2,1,0:T(8,128)(2,1)}) custom-call(bf16[384,1024]{1,0:T(8,128)(2,1)} %constant_dynamic-update-slice_fusion.2.refs_0_, bf16[384,1024]{1,0:T(8,128)(2,1)} %collective-permute-done.20.refs_1_, ...), custom_call_target="tpu_custom_call" | custom-call | flops 11699999744 | bytes 26000000 | tf_op jit(solution)/shard_map/feed/pallas_call | solution.py:1053
  287.3 2.7 slice_bitcast_fusion.2
  290.9 12.8 %feed.3 = (bf16[2,768,1024]{2,1,0:T(8,128)(2,1)}, bf16[2,384,1024]{2,1,0:T(8,128)(2,1)}, bf16[2,384,1024]{2,1,0:T(8,128)(2,1)}, bf16[2,384,1024]{2,1,0:T(8,128)(2,1)}, bf16[2,384,1024]{2,1,0:T(8,128)(2,1)}) custom-call(bf16[384,1024]{1,0:T(8,128)(2,1)} %copy-done.40, bf16[384,1024]{1,0:T(8,128)(2,1)} %collective-permute-done.10.refs_1_, ...), custom_call_target="tpu_custom_call" | custom-call | flops 11699999744 | bytes 26000000 | tf_op jit(solution)/shard_map/feed/pallas_call | solution.py:1053
  303.7 2.8 slice_bitcast_fusion.3
  312.1 22.0 %feed.5 = (bf16[4,768,1024]{2,1,0:T(8,128)(2,1)}, bf16[4,384,1024]{2,1,0:T(8,128)(2,1)}, bf16[4,384,1024]{2,1,0:T(8,128)(2,1)}, bf16[4,384,1024]{2,1,0:T(8,128)(2,1)}, bf16[4,384,1024]{2,1,0:T(8,128)(2,1)}) custom-call(bf16[384,1024]{1,0:T(8,128)(2,1)} %copy-done.50, bf16[384,1024]{1,0:T(8,128)(2,1)} %copy-done.51, bf16[384,1024]{1,0:T(8,128)(2,1)} %copy-done.65, ...), custom_call_target="tpu_custom_call" | custom-call | flops 23399999488 | bytes 52000000 | tf_op jit(solution)/shard_map/feed/pallas_call | solution.py:1053
  334.2 4.0 slice.599
  342.2 3.9 fusion.56
  346.2 3.6 fusion.57
  353.3 5.4 fusion.55
  358.7 3.5 fusion.38
  372.2 28.2 %collective-permute-done.33 = bf16[768,1024]{1,0:T(8,128)(2,1)S(1)} collective-permute-done((bf16[768,1024]{1,0:T(8,128)(2,1)S(1)}, bf16[768,1024]{1,0:T(8,128)(2,1)S(1)}, u32[]{:S(2)}, u32[]{:S(2)}) %collective-permute-start.33) | collective-permute-done | bytes 1572896 | tf_op jit(solution)/shard_map/ppermute | solution.py:1229
  400.4 2.8 fusion.4
  404.0 3.0 convert_reduce_fusion.6
  408.9 2.6 convolution_convert_fusion.3
  411.5 5.3 all-to-all-start.3
  418.9 4.6 collective-permute-start.34
  423.6 3.4 collective-permute-start.36
  429.1 13.1 %cross_backward.1 = (bf16[384,1024]{1,0:T(8,128)(2,1)}, bf16[8,128,1024]{2,1,0:T(8,128)(2,1)}, bf16[512,1024]{1,0:T(8,128)(2,1)}, bf16[512,1024]{1,0:T(8,128)(2,1)}) custom-call(bf16[384,1024]{1,0:T(8,128)(2,1)} %add_convert_fusion.4.probe_ref, bf16[512,1024]{1,0:T(8,128)(2,1)} %convolution_convert_fusion.6.lookup_ref, ...), custom_call_target="tpu_custom_call" | custom-call | flops 11699999744 | bytes 26000000 | tf_op jit(solution)/shard_map/cross_backward/pallas_call | solution.py:1155
  442.2 2.5 convolution_convert_fusion.2
  454.9 7.5 collective-permute-done.34
  462.4 11.5 %collective-permute-done.35 = bf16[272,1024]{1,0:T(8,128)(2,1)} collective-permute-done((bf16[272,1024]{1,0:T(8,128)(2,1)S(1)}, bf16[272,1024]{1,0:T(8,128)(2,1)}, u32[]{:S(2)}, u32[]{:S(2)}) %collective-permute-start.35) | collective-permute-done | bytes 557088 | tf_op jit(solution)/shard_map/ppermute | solution.py:1298
  473.9 3.3 collective-permute-done.37
  477.3 3.0 multiply_reduce_fusion.1
  489.9 2.6 convolution_convert_fusion.7
  494.1 3.7 all-to-all-start.4
  498.4 10.4 %all-to-all-done.4.grad_ref = bf16[8,384,128]{2,1,0:T(8,128)(2,1)S(1)} async-done(((bf16[8,384,128]{2,1,0:T(8,128)(2,1)}), bf16[8,384,128]{2,1,0:T(8,128)(2,1)S(1)}, u32[]{:S(2)}, u32[]{:S(2)}) %all-to-all-start.4) | async-done | bytes 786464 | tf_op jit(solution)/shard_map/all_to_all | solution.py:1328
  509.7 36.8 %self_backward.1 = (bf16[2,384,384]{2,1,0:T(8,128)(2,1)}, bf16[4,384,384]{2,1,0:T(8,128)(2,1)}, bf16[2,384,384]{2,1,0:T(8,128)(2,1)}) custom-call(s32[8]{0:T(128)} %stack.105.lines_ref, s32[2]{0:T(128)} %bitcast.437, bf16[2,384,384]{2,1,0:T(8,128)(2,1)} %get-tuple-element.106.near_ref, bf16[4,384,384]{2,1,0:T(8,128)(2,1)} %get-tuple-element.107.next_ref, ...), custom_call_target="tpu_custom_call" | custom-call | flops 33300000768 | bytes 74000000 | tf_op jit(solution)/shard_map/self_backward/pallas_call | solution.py:961
  546.4 4.1 collective-permute-start.38
  552.5 3.1 convolution_convert_fusion
  566.6 22.6 %collective-permute-done.41 = bf16[192,1024]{1,0:T(8,128)(2,1)S(1)} collective-permute-done((bf16[192,1024]{1,0:T(8,128)(2,1)S(1)}, bf16[192,1024]{1,0:T(8,128)(2,1)S(1)}, u32[]{:S(2)}, u32[]{:S(2)}) %collective-permute-start.41) | collective-permute-done | bytes 393248 | tf_op jit(solution)/shard_map/ppermute | solution.py:1226
  596.0 25.2 %collective-permute-done.45 = bf16[384,1024]{1,0:T(8,128)(2,1)S(1)} collective-permute-done((bf16[384,1024]{1,0:T(8,128)(2,1)S(1)}, bf16[384,1024]{1,0:T(8,128)(2,1)S(1)}, u32[]{:S(2)}, u32[]{:S(2)}) %collective-permute-start.45) | collective-permute-done | bytes 786464 | tf_op jit(solution)/shard_map/ppermute | solution.py:1229
  625.8 6.7 collective-permute-start.47
  644.5 36.3 %all-to-all-start.5 = ((bf16[8,128,640]{2,1,0:T(8,128)(2,1)}), bf16[8,128,640]{2,1,0:T(8,128)(2,1)}, u32[]{:S(2)}, u32[]{:S(2)}) async-start(bf16[8,128,640]{2,1,0:T(8,128)(2,1)} %bitcast.131), calls=%async_computation.6 | async-start | bytes 2621440 | tf_op jit(solution)/shard_map/all_to_all | solution.py:1328
  680.8 6.0 collective-permute-start.50
  698.8 3.9 settle_columns.1
  702.7 3.7 collective-permute-start.49
  707.1 3.3 all-to-all-start.6
  711.8 20.9 %all-to-all-done.6 = f32[8,2,128]{2,1,0:T(2,128)S(1)} async-done(((f32[8,2,128]{2,1,0:T(2,128)}), f32[8,2,128]{2,1,0:T(2,128)S(1)}, u32[]{:S(2)}, u32[]{:S(2)}) %all-to-all-start.6) | async-done | bytes 8224 | tf_op jit(solution)/shard_map/all_to_all | solution.py:1328
  732.7 5.6 collective-permute-start.48
  744.2 3.1 settle_heads.1
  (477 shorter events, 186.1 us)
Async XLA Ops:
  7.2 75.7 %copy-start = (bf16[1024,1024]{1,0:T(8,128)(2,1)S(1)}, bf16[1024,1024]{1,0:T(8,128)(2,1)}, u32[]{:S(2)}) copy-start(bf16[1024,1024]{1,0:T(8,128)(2,1)} %param.56) | copy-start | bytes 6291460
  26.5 47.7 %all-to-all-start = ((bf16[8,136,384]{2,1,0:T(8,128)(2,1)}), bf16[8,136,384]{2,1,0:T(8,128)(2,1)}, u32[]{:S(2)}, u32[]{:S(2)}) async-start(bf16[8,136,384]{2,1,0:T(8,128)(2,1)} %bitcast.9), calls=%async_computation | async-start | bytes 1671168 | tf_op jit(solution)/shard_map/all_to_all | solution.py:1328
  32.9 41.3 %copy-start.67 = (s32[2]{0:T(128)S(1)}, s32[2]{0:T(128)}, u32[]{:S(2)}) copy-start(s32[2]{0:T(128)} %param.33) | copy-start | bytes 28
  32.9 173.5 %all-gather.5.cloned.1.call-start = ((), (), s32[]{:S(2)}) async-start(), calls=%async_computation.9 | async-start | bytes 10813440 | tf_op jit(solution)/shard_map/all_gather | solution.py:1500
  33.9 40.2 %collective-permute-start = (bf16[448,1024]{1,0:T(8,128)(2,1)}, bf16[448,1024]{1,0:T(8,128)(2,1)S(1)}, u32[]{:S(2)}, u32[]{:S(2)}) collective-permute-start(bf16[448,1024]{1,0:T(8,128)(2,1)} %pad_maximum_fusion.11), channel_id=1, source_target_pairs={{0,0},{2,16},{4,8},{6,24},{8,4},{10,20},{12,12},{14,28},{16,2},{18... | collective-permute-start | bytes 2752520 | tf_op jit(solution)/shard_map/ppermute | solution.py:1272
  74.2 10.8 %collective-permute-start.1 = (s32[2]{0:T(128)S(1)}, s32[2]{0:T(128)S(1)}, u32[]{:S(2)}, u32[]{:S(2)}) collective-permute-start(s32[2]{0:T(128)S(1)} %copy-done.67), channel_id=1, source_target_pairs={{0,0},{2,8},{4,16},{6,24},{8,4},{10,12},{12,20},{14,28},{16,2},{18... | collective-permute-start | bytes 32 | tf_op jit(solution)/shard_map/ppermute | solution.py:1425
  85.7 46.4 %collective-permute-start.2 = (bf16[448,1024]{1,0:T(8,128)(2,1)S(1)}, bf16[448,1024]{1,0:T(8,128)(2,1)}, u32[]{:S(2)}, u32[]{:S(2)}) collective-permute-start(bf16[448,1024]{1,0:T(8,128)(2,1)S(1)} %collective-permute-done.refs_0_), channel_id=1, source_target_pairs={{0,8},{1,9},{8,0},{9,1},{16,24},{17,25},{24,16},{25,17},{2,10},{3,... | collective-permute-start | bytes 2752520 | tf_op jit(solution)/shard_map/ppermute | solution.py:1232
  85.7 37.9 %collective-permute-start.3 = (bf16[448,1024]{1,0:T(8,128)(2,1)S(1)}, bf16[448,1024]{1,0:T(8,128)(2,1)}, u32[]{:S(2)}, u32[]{:S(2)}) collective-permute-start(bf16[448,1024]{1,0:T(8,128)(2,1)S(1)} %collective-permute-done.refs_0_), channel_id=1, source_target_pairs={{0,16},{16,17},{17,1},{1,0},{8,24},{24,25},{25,9},{9,8},{2,18},{18... | collective-permute-start | bytes 2752520 | tf_op jit(solution)/shard_map/ppermute | solution.py:1226
  91.9 35.8 %collective-permute-start.4 = (bf16[448,1024]{1,0:T(8,128)(2,1)S(1)}, bf16[448,1024]{1,0:T(8,128)(2,1)}, u32[]{:S(2)}, u32[]{:S(2)}) collective-permute-start(bf16[448,1024]{1,0:T(8,128)(2,1)S(1)} %collective-permute-done.refs_0_), channel_id=1, source_target_pairs={{16,0},{17,16},{1,17},{0,1},{24,8},{25,24},{9,25},{8,9},{18,2},{19... | collective-permute-start | bytes 2752520 | tf_op jit(solution)/shard_map/ppermute | solution.py:1229
  93.6 28.5 %all-to-all-start.2 = ((bf16[2,128,1024]{1,2,0:T(8,128)(2,1)}), bf16[2,128,1024]{1,2,0:T(8,128)(2,1)S(1)}, u32[]{:S(2)}, u32[]{:S(2)}) async-start(bf16[2,128,1024]{1,2,0:T(8,128)(2,1)} %bitcast.47), calls=%async_computation.2 | async-start | bytes 1048576 | tf_op jit(solution)/shard_map/all_to_all | solution.py:1328
  97.1 176.7 %all-gather.7.cloned.1.call-start = ((), (), s32[]{:S(2)}) async-start(), calls=%async_computation.10 | async-start | bytes 5242880 | tf_op jit(solution)/shard_map/all_gather | solution.py:1526
  99.8 94.5 %collective-permute-start.11 = (bf16[384,1024]{1,0:T(8,128)(2,1)}, bf16[384,1024]{1,0:T(8,128)(2,1)}, u32[]{:S(2)}, u32[]{:S(2)}) collective-permute-start(bf16[384,1024]{1,0:T(8,128)(2,1)} %pad_maximum_fusion.12), channel_id=1, source_target_pairs={{0,0},{2,16},{4,8},{6,24},{8,4},{10,20},{12,12},{14,28},{16,2},{18... | collective-permute-start | bytes 2359304 | tf_op jit(solution)/shard_map/ppermute | solution.py:1272
  124.6 22.8 %collective-permute-start.7 = (bf16[224,1024]{1,0:T(8,128)(2,1)S(1)}, bf16[224,1024]{1,0:T(8,128)(2,1)S(1)}, u32[]{:S(2)}, u32[]{:S(2)}) collective-permute-start(bf16[224,1024]{1,0:T(8,128)(2,1)S(1)} %slice.725), channel_id=1, source_target_pairs={{0,16},{16,17},{17,1},{1,0},{8,24},{24,25},{25,9},{9,8},{2,18},{18... | collective-permute-start | bytes 1376264 | tf_op jit(solution)/shard_map/ppermute | solution.py:1226
  128.8 18.7 %collective-permute-start.8 = (bf16[224,1024]{1,0:T(8,128)(2,1)S(1)}, bf16[224,1024]{1,0:T(8,128)(2,1)S(1)}, u32[]{:S(2)}, u32[]{:S(2)}) collective-permute-start(bf16[224,1024]{1,0:T(8,128)(2,1)S(1)} %slice.726), channel_id=1, source_target_pairs={{16,0},{17,16},{1,17},{0,1},{24,8},{25,24},{9,25},{8,9},{18,2},{19... | collective-permute-start | bytes 1376264 | tf_op jit(solution)/shard_map/ppermute | solution.py:1229
  129.1 19.6 %collective-permute-start.5 = (bf16[448,1024]{1,0:T(8,128)(2,1)}, bf16[448,1024]{1,0:T(8,128)(2,1)S(1)}, u32[]{:S(2)}, u32[]{:S(2)}) collective-permute-start(bf16[448,1024]{1,0:T(8,128)(2,1)} %collective-permute-done.3.refs_0_), channel_id=1, source_target_pairs={{0,8},{1,9},{8,0},{9,1},{16,24},{17,25},{24,16},{25,17},{2,10},{3,... | collective-permute-start | bytes 2752520 | tf_op jit(solution)/shard_map/ppermute | solution.py:1232
  132.1 16.6 %collective-permute-start.6 = (bf16[448,1024]{1,0:T(8,128)(2,1)}, bf16[448,1024]{1,0:T(8,128)(2,1)S(1)}, u32[]{:S(2)}, u32[]{:S(2)}) collective-permute-start(bf16[448,1024]{1,0:T(8,128)(2,1)} %collective-permute-done.4.refs_1_), channel_id=1, source_target_pairs={{0,8},{1,9},{8,0},{9,1},{16,24},{17,25},{24,16},{25,17},{2,10},{3,... | collective-permute-start | bytes 2752520 | tf_op jit(solution)/shard_map/ppermute | solution.py:1232
  147.6 10.3 %collective-permute-start.9 = (bf16[448,1024]{1,0:T(8,128)(2,1)S(1)}, bf16[448,1024]{1,0:T(8,128)(2,1)S(1)}, u32[]{:S(2)}, u32[]{:S(2)}) collective-permute-start(bf16[448,1024]{1,0:T(8,128)(2,1)S(1)} %constant_dynamic-update-slice_fusion.refs_0_), channel_id=1, source_target_pairs={{0,8},{1,9},{8,0},{9,1},{16,24},{17,25},{24,16},{25,17},{2,10},{3,... | collective-permute-start | bytes 2752520 | tf_op jit(solution)/shard_map/ppermute | solution.py:1232
  188.1 17.1 %all-to-all-start.1 = ((bf16[8,384,128]{2,1,0:T(8,128)(2,1)}), bf16[8,384,128]{2,1,0:T(8,128)(2,1)S(1)}, u32[]{:S(2)}, u32[]{:S(2)}) async-start(bf16[8,384,128]{2,1,0:T(8,128)(2,1)} %get-tuple-element.109), calls=%async_computation.1 | async-start | bytes 1572864 | tf_op jit(solution)/shard_map/all_to_all | solution.py:1328
  194.3 39.6 %collective-permute-start.12 = (bf16[384,1024]{1,0:T(8,128)(2,1)}, bf16[384,1024]{1,0:T(8,128)(2,1)}, u32[]{:S(2)}, u32[]{:S(2)}) collective-permute-start(bf16[384,1024]{1,0:T(8,128)(2,1)} %collective-permute-done.11.refs_2_), channel_id=1, source_target_pairs={{0,16},{16,17},{17,1},{1,0},{8,24},{24,25},{25,9},{9,8},{2,18},{18... | collective-permute-start | bytes 2359304 | tf_op jit(solution)/shard_map/ppermute | solution.py:1226
  195.7 38.2 %collective-permute-start.13 = (bf16[384,1024]{1,0:T(8,128)(2,1)}, bf16[384,1024]{1,0:T(8,128)(2,1)}, u32[]{:S(2)}, u32[]{:S(2)}) collective-permute-start(bf16[384,1024]{1,0:T(8,128)(2,1)} %collective-permute-done.11.refs_2_), channel_id=1, source_target_pairs={{16,0},{17,16},{1,17},{0,1},{24,8},{25,24},{9,25},{8,9},{18,2},{19... | collective-permute-start | bytes 2359304 | tf_op jit(solution)/shard_map/ppermute | solution.py:1229
  196.2 37.7 %collective-permute-start.14 = (bf16[384,1024]{1,0:T(8,128)(2,1)}, bf16[384,1024]{1,0:T(8,128)(2,1)}, u32[]{:S(2)}, u32[]{:S(2)}) collective-permute-start(bf16[384,1024]{1,0:T(8,128)(2,1)} %collective-permute-done.11.refs_2_), channel_id=1, source_target_pairs={{0,8},{1,9},{8,0},{9,1},{16,24},{17,25},{24,16},{25,17},{2,10},{3,... | collective-permute-start | bytes 2359304 | tf_op jit(solution)/shard_map/ppermute | solution.py:1232
  232.4 18.9 %collective-permute-start.16 = (bf16[384,1024]{1,0:T(8,128)(2,1)S(1)}, bf16[384,1024]{1,0:T(8,128)(2,1)S(1)}, u32[]{:S(2)}, u32[]{:S(2)}) collective-permute-start(bf16[384,1024]{1,0:T(8,128)(2,1)S(1)} %add_convert_fusion.3.refs_0_), channel_id=1, source_target_pairs={{0,16},{16,17},{17,1},{1,0},{8,24},{24,25},{25,9},{9,8},{2,18},{18... | collective-permute-start | bytes 2359304 | tf_op jit(solution)/shard_map/ppermute | solution.py:1226
  233.2 19.0 %collective-permute-start.18 = (bf16[384,1024]{1,0:T(8,128)(2,1)S(1)}, bf16[384,1024]{1,0:T(8,128)(2,1)S(1)}, u32[]{:S(2)}, u32[]{:S(2)}) collective-permute-start(bf16[384,1024]{1,0:T(8,128)(2,1)S(1)} %add_convert_fusion.3.refs_0_), channel_id=1, source_target_pairs={{16,0},{17,16},{1,17},{0,1},{24,8},{25,24},{9,25},{8,9},{18,2},{19... | collective-permute-start | bytes 2359304 | tf_op jit(solution)/shard_map/ppermute | solution.py:1229
  233.9 26.3 %collective-permute-start.23 = (bf16[384,1024]{1,0:T(8,128)(2,1)}, bf16[384,1024]{1,0:T(8,128)(2,1)S(1)}, u32[]{:S(2)}, u32[]{:S(2)}) collective-permute-start(bf16[384,1024]{1,0:T(8,128)(2,1)} %collective-permute-done.12.refs_4_), channel_id=1, source_target_pairs={{0,8},{1,9},{8,0},{9,1},{16,24},{17,25},{24,16},{25,17},{2,10},{3,... | collective-permute-start | bytes 2359304 | tf_op jit(solution)/shard_map/ppermute | solution.py:1232
  234.9 25.3 %collective-permute-start.24 = (bf16[384,1024]{1,0:T(8,128)(2,1)}, bf16[384,1024]{1,0:T(8,128)(2,1)S(1)}, u32[]{:S(2)}, u32[]{:S(2)}) collective-permute-start(bf16[384,1024]{1,0:T(8,128)(2,1)} %collective-permute-done.13.refs_5_), channel_id=1, source_target_pairs={{0,8},{1,9},{8,0},{9,1},{16,24},{17,25},{24,16},{25,17},{2,10},{3,... | collective-permute-start | bytes 2359304 | tf_op jit(solution)/shard_map/ppermute | solution.py:1232
  236.0 23.7 %collective-permute-start.21 = (bf16[192,1024]{1,0:T(8,128)(2,1)S(1)}, bf16[192,1024]{1,0:T(8,128)(2,1)S(1)}, u32[]{:S(2)}, u32[]{:S(2)}) collective-permute-start(bf16[192,1024]{1,0:T(8,128)(2,1)S(1)} %slice.593), channel_id=1, source_target_pairs={{0,16},{16,17},{17,1},{1,0},{8,24},{24,25},{25,9},{9,8},{2,18},{18... | collective-permute-start | bytes 1179656 | tf_op jit(solution)/shard_map/ppermute | solution.py:1226
  251.3 8.8 %collective-permute-start.22 = (bf16[192,1024]{1,0:T(8,128)(2,1)S(1)}, bf16[192,1024]{1,0:T(8,128)(2,1)S(1)}, u32[]{:S(2)}, u32[]{:S(2)}) collective-permute-start(bf16[192,1024]{1,0:T(8,128)(2,1)S(1)} %slice.594), channel_id=1, source_target_pairs={{16,0},{17,16},{1,17},{0,1},{24,8},{25,24},{9,25},{8,9},{18,2},{19... | collective-permute-start | bytes 1179656 | tf_op jit(solution)/shard_map/ppermute | solution.py:1229
  252.2 16.0 %collective-permute-start.17 = (bf16[192,1024]{1,0:T(8,128)(2,1)S(1)}, bf16[192,1024]{1,0:T(8,128)(2,1)S(1)}, u32[]{:S(2)}, u32[]{:S(2)}) collective-permute-start(bf16[192,1024]{1,0:T(8,128)(2,1)S(1)} %slice.748), channel_id=1, source_target_pairs={{0,16},{16,17},{17,1},{1,0},{8,24},{24,25},{25,9},{9,8},{2,18},{18... | collective-permute-start | bytes 1179656 | tf_op jit(solution)/shard_map/ppermute | solution.py:1226
  259.8 9.2 %collective-permute-start.19 = (bf16[192,1024]{1,0:T(8,128)(2,1)S(1)}, bf16[192,1024]{1,0:T(8,128)(2,1)S(1)}, u32[]{:S(2)}, u32[]{:S(2)}) collective-permute-start(bf16[192,1024]{1,0:T(8,128)(2,1)S(1)} %slice.749), channel_id=1, source_target_pairs={{16,0},{17,16},{1,17},{0,1},{24,8},{25,24},{9,25},{8,9},{18,2},{19... | collective-permute-start | bytes 1179656 | tf_op jit(solution)/shard_map/ppermute | solution.py:1229
  261.8 11.9 %collective-permute-start.25 = (bf16[384,1024]{1,0:T(8,128)(2,1)}, bf16[384,1024]{1,0:T(8,128)(2,1)}, u32[]{:S(2)}, u32[]{:S(2)}) collective-permute-start(bf16[384,1024]{1,0:T(8,128)(2,1)} %constant_dynamic-update-slice_fusion.4.refs_2_), channel_id=1, source_target_pairs={{0,8},{1,9},{8,0},{9,1},{16,24},{17,25},{24,16},{25,17},{2,10},{3,... | collective-permute-start | bytes 2359304 | tf_op jit(solution)/shard_map/ppermute | solution.py:1232
  269.8 4.8 collective-permute-start.20
  273.7 17.1 %collective-permute-start.10 = (bf16[384,1024]{1,0:T(8,128)(2,1)}, bf16[384,1024]{1,0:T(8,128)(2,1)}, u32[]{:S(2)}, u32[]{:S(2)}) collective-permute-start(bf16[384,1024]{1,0:T(8,128)(2,1)} %copy-done.40), channel_id=1, source_target_pairs={{0,8},{1,9},{8,0},{9,1},{16,24},{17,25},{24,16},{25,17},{2,10},{3,... | collective-permute-start | bytes 2359304 | tf_op jit(solution)/shard_map/ppermute | solution.py:1232
  290.0 16.6 %collective-permute-start.26 = (bf16[768,1024]{1,0:T(8,128)(2,1)}, bf16[768,1024]{1,0:T(8,128)(2,1)}, u32[]{:S(2)}, u32[]{:S(2)}) collective-permute-start(bf16[768,1024]{1,0:T(8,128)(2,1)} %slice_bitcast_fusion.2), channel_id=1, source_target_pairs={{0,8},{1,9},{8,0},{9,1},{16,24},{17,25},{24,16},{25,17},{2,10},{3,... | collective-permute-start | bytes 4718600 | tf_op jit(solution)/shard_map/ppermute | solution.py:1232
  290.4 20.0 %collective-permute-start.28 = (bf16[384,1024]{1,0:T(8,128)(2,1)}, bf16[384,1024]{1,0:T(8,128)(2,1)S(1)}, u32[]{:S(2)}, u32[]{:S(2)}) collective-permute-start(bf16[384,1024]{1,0:T(8,128)(2,1)} %copy-done.50), channel_id=1, source_target_pairs={{0,8},{1,9},{8,0},{9,1},{16,24},{17,25},{24,16},{25,17},{2,10},{3,... | collective-permute-start | bytes 2359304 | tf_op jit(solution)/shard_map/ppermute | solution.py:1232
  290.5 19.9 %collective-permute-start.29 = (bf16[384,1024]{1,0:T(8,128)(2,1)}, bf16[384,1024]{1,0:T(8,128)(2,1)S(1)}, u32[]{:S(2)}, u32[]{:S(2)}) collective-permute-start(bf16[384,1024]{1,0:T(8,128)(2,1)} %copy-done.51), channel_id=1, source_target_pairs={{0,8},{1,9},{8,0},{9,1},{16,24},{17,25},{24,16},{25,17},{2,10},{3,... | collective-permute-start | bytes 2359304 | tf_op jit(solution)/shard_map/ppermute | solution.py:1232
  306.5 65.8 %collective-permute-start.15 = (bf16[768,1024]{1,0:T(8,128)(2,1)}, bf16[768,1024]{1,0:T(8,128)(2,1)}, u32[]{:S(2)}, u32[]{:S(2)}) collective-permute-start(bf16[768,1024]{1,0:T(8,128)(2,1)} %slice_bitcast_fusion.3), channel_id=1, source_target_pairs={{0,8},{1,9},{8,0},{9,1},{16,24},{17,25},{24,16},{25,17},{2,10},{3,... | collective-permute-start | bytes 4718600 | tf_op jit(solution)/shard_map/ppermute | solution.py:1232
  308.8 30.3 %collective-permute-start.27 = (bf16[384,1024]{1,0:T(8,128)(2,1)S(1)}, bf16[384,1024]{1,0:T(8,128)(2,1)S(1)}, u32[]{:S(2)}, u32[]{:S(2)}) collective-permute-start(bf16[384,1024]{1,0:T(8,128)(2,1)S(1)} %get-tuple-element.248), channel_id=1, source_target_pairs={{0,16},{16,17},{17,1},{1,0},{8,24},{24,25},{25,9},{9,8},{2,18},{18... | collective-permute-start | bytes 2359304 | tf_op jit(solution)/shard_map/ppermute | solution.py:1226
  309.8 29.3 %collective-permute-start.32 = (bf16[384,1024]{1,0:T(8,128)(2,1)S(1)}, bf16[384,1024]{1,0:T(8,128)(2,1)S(1)}, u32[]{:S(2)}, u32[]{:S(2)}) collective-permute-start(bf16[384,1024]{1,0:T(8,128)(2,1)S(1)} %get-tuple-element.249), channel_id=1, source_target_pairs={{16,0},{17,16},{1,17},{0,1},{24,8},{25,24},{9,25},{8,9},{18,2},{19... | collective-permute-start | bytes 2359304 | tf_op jit(solution)/shard_map/ppermute | solution.py:1229
  338.2 20.5 %collective-permute-start.30 = (bf16[2,768,1024]{2,1,0:T(8,128)(2,1)}, bf16[2,768,1024]{2,1,0:T(8,128)(2,1)}, u32[]{:S(2)}, u32[]{:S(2)}) collective-permute-start(bf16[2,768,1024]{2,1,0:T(8,128)(2,1)} %slice.599), channel_id=1, source_target_pairs={{0,8},{1,9},{8,0},{9,1},{16,24},{17,25},{24,16},{25,17},{2,10},{3,... | collective-permute-start | bytes 9437192 | tf_op jit(solution)/shard_map/ppermute | solution.py:1232
  364.4 36.1 %collective-permute-start.33 = (bf16[768,1024]{1,0:T(8,128)(2,1)S(1)}, bf16[768,1024]{1,0:T(8,128)(2,1)S(1)}, u32[]{:S(2)}, u32[]{:S(2)}) collective-permute-start(bf16[768,1024]{1,0:T(8,128)(2,1)S(1)} %pad_maximum_fusion.7), channel_id=1, source_target_pairs={{16,0},{17,16},{1,17},{0,1},{24,8},{25,24},{9,25},{8,9},{18,2},{19... | collective-permute-start | bytes 4718600 | tf_op jit(solution)/shard_map/ppermute | solution.py:1229
  364.6 35.8 %collective-permute-start.31 = (bf16[768,1024]{1,0:T(8,128)(2,1)S(1)}, bf16[768,1024]{1,0:T(8,128)(2,1)S(1)}, u32[]{:S(2)}, u32[]{:S(2)}) collective-permute-start(bf16[768,1024]{1,0:T(8,128)(2,1)S(1)} %pad_maximum_fusion.6), channel_id=1, source_target_pairs={{0,16},{16,17},{17,1},{1,0},{8,24},{24,25},{25,9},{9,8},{2,18},{18... | collective-permute-start | bytes 4718600 | tf_op jit(solution)/shard_map/ppermute | solution.py:1226
  411.5 65.7 %all-to-all-start.3 = ((bf16[8,128,1024]{2,1,0:T(8,128)(2,1)}), bf16[8,128,1024]{2,1,0:T(8,128)(2,1)}, u32[]{:S(2)}, u32[]{:S(2)}) async-start(bf16[8,128,1024]{2,1,0:T(8,128)(2,1)} %bitcast.328), calls=%async_computation.3 | async-start | bytes 4194304 | tf_op jit(solution)/shard_map/all_to_all | solution.py:1328
  416.8 206.4 %reduce-scatter.2.cloned.1.call-start = ((), (), s32[]{:S(2)}) async-start(), calls=%async_computation.8 | async-start | bytes 10911744 | tf_op jit(solution)/shard_map/reduce_scatter | solution.py:1634
  418.9 43.5 %collective-permute-start.34 = (bf16[272,1024]{1,0:T(8,128)(2,1)S(1)}, bf16[272,1024]{1,0:T(8,128)(2,1)S(1)}, u32[]{:S(2)}, u32[]{:S(2)}) collective-permute-start(bf16[272,1024]{1,0:T(8,128)(2,1)S(1)} %get-tuple-element.225), channel_id=1, source_target_pairs={{0,0},{2,16},{4,8},{6,24},{8,2},{10,18},{12,10},{14,26},{16,4},{18... | collective-permute-start | bytes 1671176 | tf_op jit(solution)/shard_map/ppermute | solution.py:1298
  423.5 50.4 %collective-permute-start.35 = (bf16[272,1024]{1,0:T(8,128)(2,1)S(1)}, bf16[272,1024]{1,0:T(8,128)(2,1)}, u32[]{:S(2)}, u32[]{:S(2)}) collective-permute-start(bf16[272,1024]{1,0:T(8,128)(2,1)S(1)} %get-tuple-element.224), channel_id=1, source_target_pairs={{0,2},{2,18},{4,10},{6,26},{8,0},{10,16},{12,8},{14,24},{16,6},{18... | collective-permute-start | bytes 1671176 | tf_op jit(solution)/shard_map/ppermute | solution.py:1298
  423.6 50.4 %collective-permute-start.36 = (bf16[272,1024]{1,0:T(8,128)(2,1)S(1)}, bf16[272,1024]{1,0:T(8,128)(2,1)}, u32[]{:S(2)}, u32[]{:S(2)}) collective-permute-start(bf16[272,1024]{1,0:T(8,128)(2,1)S(1)} %get-tuple-element.223), channel_id=1, source_target_pairs={{0,4},{2,20},{4,12},{6,28},{8,6},{10,22},{12,14},{14,30},{16,0},{1... | collective-permute-start | bytes 1671176 | tf_op jit(solution)/shard_map/ppermute | solution.py:1298
  427.0 50.3 %collective-permute-start.37 = (bf16[272,1024]{1,0:T(8,128)(2,1)S(1)}, bf16[272,1024]{1,0:T(8,128)(2,1)}, u32[]{:S(2)}, u32[]{:S(2)}) collective-permute-start(bf16[272,1024]{1,0:T(8,128)(2,1)S(1)} %get-tuple-element.222), channel_id=1, source_target_pairs={{0,6},{2,22},{4,14},{6,30},{8,4},{10,20},{12,12},{14,28},{16,2},{1... | collective-permute-start | bytes 1671176 | tf_op jit(solution)/shard_map/ppermute | solution.py:1298
  494.1 14.7 %all-to-all-start.4 = ((bf16[8,384,128]{2,1,0:T(8,128)(2,1)}), bf16[8,384,128]{2,1,0:T(8,128)(2,1)S(1)}, u32[]{:S(2)}, u32[]{:S(2)}) async-start(bf16[8,384,128]{2,1,0:T(8,128)(2,1)} %bitcast.79), calls=%async_computation.4 | async-start | bytes 1572864 | tf_op jit(solution)/shard_map/all_to_all | solution.py:1328
  509.7 42.8 %copy-start.37 = (bf16[8,128,384]{2,1,0:T(8,128)(2,1)S(1)}, bf16[8,128,384]{2,1,0:T(8,128)(2,1)}, u32[]{:S(2)}) copy-start(bf16[8,128,384]{2,1,0:T(8,128)(2,1)} %slice.562) | copy-start | bytes 2359300
  546.4 48.0 %collective-permute-start.38 = (bf16[384,1024]{1,0:T(8,128)(2,1)S(1)}, bf16[384,1024]{1,0:T(8,128)(2,1)S(1)}, u32[]{:S(2)}, u32[]{:S(2)}) collective-permute-start(bf16[384,1024]{1,0:T(8,128)(2,1)S(1)} %copy-done.32), channel_id=1, source_target_pairs={{0,0},{2,16},{4,8},{6,24},{8,4},{10,20},{12,12},{14,28},{16,2},{18... | collective-permute-start | bytes 2359304 | tf_op jit(solution)/shard_map/ppermute | solution.py:1280
  550.6 72.6 %collective-permute-start.46 = (bf16[8,128,1024]{2,1,0:T(8,128)(2,1)}, bf16[8,128,1024]{2,1,0:T(8,128)(2,1)}, u32[]{:S(2)}, u32[]{:S(2)}) collective-permute-start(bf16[8,128,1024]{2,1,0:T(8,128)(2,1)} %all-to-all-done.3), channel_id=1, source_target_pairs={{0,2},{2,18},{4,10},{6,26},{8,6},{10,22},{12,14},{14,30},{16,0},{1... | collective-permute-start | bytes 6291464 | tf_op jit(solution)/shard_map/ppermute | solution.py:1288
  555.9 9.4 %collective-permute-start.42 = (bf16[2,384,1024]{2,1,0:T(8,128)(2,1)S(1)}, bf16[2,384,1024]{2,1,0:T(8,128)(2,1)S(1)}, u32[]{:S(2)}, u32[]{:S(2)}) collective-permute-start(bf16[2,384,1024]{2,1,0:T(8,128)(2,1)S(1)} %bitcast.366), channel_id=1, source_target_pairs={{0,8},{1,9},{8,0},{9,1},{16,24},{17,25},{24,16},{25,17},{2,10},{3,... | collective-permute-start | bytes 4718600 | tf_op jit(solution)/shard_map/ppermute | solution.py:1232
  557.7 6.1 collective-permute-start.40
  560.2 35.7 %collective-permute-start.39 = (bf16[384,1024]{1,0:T(8,128)(2,1)S(1)}, bf16[384,1024]{1,0:T(8,128)(2,1)S(1)}, u32[]{:S(2)}, u32[]{:S(2)}) collective-permute-start(bf16[384,1024]{1,0:T(8,128)(2,1)S(1)} %slice.766), channel_id=1, source_target_pairs={{0,8},{1,9},{8,0},{9,1},{16,24},{17,25},{24,16},{25,17},{2,10},{3,... | collective-permute-start | bytes 2359304 | tf_op jit(solution)/shard_map/ppermute | solution.py:1232
  564.2 25.0 %collective-permute-start.41 = (bf16[192,1024]{1,0:T(8,128)(2,1)S(1)}, bf16[192,1024]{1,0:T(8,128)(2,1)S(1)}, u32[]{:S(2)}, u32[]{:S(2)}) collective-permute-start(bf16[192,1024]{1,0:T(8,128)(2,1)S(1)} %get-tuple-element.254), channel_id=1, source_target_pairs={{0,16},{16,17},{17,1},{1,0},{8,24},{24,25},{25,9},{9,8},{2,18},{18... | collective-permute-start | bytes 1179656 | tf_op jit(solution)/shard_map/ppermute | solution.py:1226
  565.3 24.0 %collective-permute-start.44 = (bf16[192,1024]{1,0:T(8,128)(2,1)S(1)}, bf16[192,1024]{1,0:T(8,128)(2,1)S(1)}, u32[]{:S(2)}, u32[]{:S(2)}) collective-permute-start(bf16[192,1024]{1,0:T(8,128)(2,1)S(1)} %get-tuple-element.255), channel_id=1, source_target_pairs={{16,0},{17,16},{1,17},{0,1},{24,8},{25,24},{9,25},{8,9},{18,2},{19... | collective-permute-start | bytes 1179656 | tf_op jit(solution)/shard_map/ppermute | solution.py:1229
  589.6 31.6 %collective-permute-start.45 = (bf16[384,1024]{1,0:T(8,128)(2,1)S(1)}, bf16[384,1024]{1,0:T(8,128)(2,1)S(1)}, u32[]{:S(2)}, u32[]{:S(2)}) collective-permute-start(bf16[384,1024]{1,0:T(8,128)(2,1)S(1)} %pad_maximum_fusion.14), channel_id=1, source_target_pairs={{16,0},{17,16},{1,17},{0,1},{24,8},{25,24},{9,25},{8,9},{18,2},{19... | collective-permute-start | bytes 2359304 | tf_op jit(solution)/shard_map/ppermute | solution.py:1229
  591.2 30.0 %collective-permute-start.43 = (bf16[384,1024]{1,0:T(8,128)(2,1)S(1)}, bf16[384,1024]{1,0:T(8,128)(2,1)S(1)}, u32[]{:S(2)}, u32[]{:S(2)}) collective-permute-start(bf16[384,1024]{1,0:T(8,128)(2,1)S(1)} %pad_maximum_fusion.13), channel_id=1, source_target_pairs={{0,16},{16,17},{17,1},{1,0},{8,24},{24,25},{25,9},{9,8},{2,18},{18... | collective-permute-start | bytes 2359304 | tf_op jit(solution)/shard_map/ppermute | solution.py:1226
  625.8 114.2 %collective-permute-start.47 = (bf16[848,1024]{1,0:T(8,128)(2,1)S(1)}, bf16[848,1024]{1,0:T(8,128)(2,1)S(1)}, u32[]{:S(2)}, u32[]{:S(2)}) collective-permute-start(bf16[848,1024]{1,0:T(8,128)(2,1)S(1)} %pad_maximum_fusion.5), channel_id=1, source_target_pairs={{0,0},{2,16},{4,8},{6,24},{8,4},{10,20},{12,12},{14,28},{16,2},{18... | collective-permute-start | bytes 5210120 | tf_op jit(solution)/shard_map/ppermute | solution.py:1280
  644.5 58.2 %all-to-all-start.5 = ((bf16[8,128,640]{2,1,0:T(8,128)(2,1)}), bf16[8,128,640]{2,1,0:T(8,128)(2,1)}, u32[]{:S(2)}, u32[]{:S(2)}) async-start(bf16[8,128,640]{2,1,0:T(8,128)(2,1)} %bitcast.131), calls=%async_computation.6 | async-start | bytes 2621440 | tf_op jit(solution)/shard_map/all_to_all | solution.py:1328
  680.8 57.5 %collective-permute-start.50 = (f32[3,128]{1,0:T(4,128)S(1)}, f32[3,128]{1,0:T(4,128)S(1)}, u32[]{:S(2)}, u32[]{:S(2)}) collective-permute-start(f32[3,128]{1,0:T(4,128)S(1)} %pad_maximum_fusion.20), channel_id=1, source_target_pairs={{0,0},{1,1},{2,16},{3,17},{4,8},{5,9},{6,24},{7,25},{8,2},{9,3},{1... | collective-permute-start | bytes 4616 | tf_op jit(solution)/shard_map/ppermute | solution.py:1314
  702.7 41.4 %collective-permute-start.49 = (bf16[8,128,640]{2,1,0:T(8,128)(2,1)}, bf16[8,128,640]{2,1,0:T(8,128)(2,1)}, u32[]{:S(2)}, u32[]{:S(2)}) collective-permute-start(bf16[8,128,640]{2,1,0:T(8,128)(2,1)} %all-to-all-done.5), channel_id=1, source_target_pairs={{0,2},{2,18},{4,10},{6,26},{8,6},{10,22},{12,14},{14,30},{16,0},{1... | collective-permute-start | bytes 3932168 | tf_op jit(solution)/shard_map/ppermute | solution.py:1288
  707.1 25.6 %all-to-all-start.6 = ((f32[8,2,128]{2,1,0:T(2,128)}), f32[8,2,128]{2,1,0:T(2,128)S(1)}, u32[]{:S(2)}, u32[]{:S(2)}) async-start(f32[8,2,128]{2,1,0:T(2,128)} %copy.183), calls=%async_computation.7 | async-start | bytes 16384 | tf_op jit(solution)/shard_map/all_to_all | solution.py:1328
  732.7 6.8 collective-permute-start.48
  (80 other events, 508.1 us)
Sparse Core Ops, SparseCore 0:
  74.3 113.5 all-gather.4
  190.1 78.9 all-gather.6
  490.0 96.1 reduce-scatter.1
